TPU v7x, 256 devices: a whole 4x4x8 slice. The times are simulated.
256 devices in a mesh: dom: 32 (over x, z), space: 8 (over y, core).
Axes of the slice: x: 4, y: 4, z: 8, core: 2. Of those that a mesh axis runs over, the one named last changes fastest.
Arguments:
- particles: float32 [512, 3, 128, 512], P('dom', None, 'space'), as said below
- counts: int32 [512], P('dom'), may hold values from 0 to 2, as said below
- bathymetry: float32 [128, 512], P('space'), may hold values from -0.5 to 0.5
Outputs:
- advanced: float32 [512, 3, 128, 512], P('dom', None, 'space')
Inputs may be any that keep to these rules, and one draw needn't show every extreme that they name: The counts sum to 512; counts[p] + counts[p + 256] = 2 for every p below 256; the particles of one group have at most 32 offspring together, and some group has exactly that many. `particles`: depths stay between 0.55 and 1.45, momenta within 0.6.
All inputs are finite; a program needn't handle non-finite values.
Results may differ from a plain program's by a relative error of at most 0.00002.
Values sent between devices are 32-bit elements; how exact they have to be, the bound alone decides.
No kernel may reach another device: no remote copies, remote signals or barrier semaphores. Data moves between devices by JAX's collectives and lax.ppermute only.
A program may use at most 64 MiB of HBM per device.

v0:
```python
import jax
import jax.numpy as jnp
from jax import lax
from jax.sharding import PartitionSpec as P

GRAVITY = 1.0
RATIO = 0.25


def with_halo(block, sides, width):
    for axis, dim in sides:
        count = lax.axis_size(axis)
        forward = [(i, i + 1) for i in range(count - 1)]
        forward.append((count - 1, 0))
        backward = [(target, source) for source, target in forward]
        low = lax.ppermute(
            lax.slice_in_dim(block, block.shape[dim] - width, None, axis=dim), axis, forward
        )
        high = lax.ppermute(lax.slice_in_dim(block, 0, width, axis=dim), axis, backward)
        block = jnp.concatenate([low, block, high], axis=dim)
    return block


def entering(part, axis, combine, identity):
    place = lax.axis_index(axis)
    gathered = lax.all_gather(part, axis)
    state = jnp.zeros_like(part) + jnp.asarray(identity, part.dtype)

    def one(lap, state):
        return combine(state, lax.dynamic_index_in_dim(gathered, lap, 0, False))

    return lax.fori_loop(0, place, one, state)


def advance(padded, bed):
    depth = padded[:, 0]
    east_flow = padded[:, 1]
    north_flow = padded[:, 2]
    flux_x = jnp.stack(
        [
            east_flow,
            east_flow * east_flow / depth + 0.5 * GRAVITY * depth * depth,
            east_flow * north_flow / depth,
        ],
        1,
    )
    flux_y = jnp.stack(
        [
            north_flow,
            east_flow * north_flow / depth,
            north_flow * north_flow / depth + 0.5 * GRAVITY * depth * depth,
        ],
        1,
    )
    centre = padded[:, :, 1:-1]
    inner_x = flux_x[:, :, 1:-1]
    mean = (
        jnp.roll(centre, -1, -1) + jnp.roll(centre, 1, -1) + padded[:, :, 2:] + padded[:, :, :-2]
    ) * 0.25
    drift = (
        mean
        - 0.5 * RATIO * (jnp.roll(inner_x, -1, -1) - jnp.roll(inner_x, 1, -1))
        - 0.5 * RATIO * (flux_y[:, :, 2:] - flux_y[:, :, :-2])
    )
    middle_depth = depth[:, 1:-1]
    bed_mid = bed[1:-1]
    slope_x = 0.5 * (jnp.roll(bed_mid, -1, -1) - jnp.roll(bed_mid, 1, -1))
    slope_y = 0.5 * (bed[2:] - bed[:-2])
    source = jnp.stack(
        [
            jnp.zeros_like(middle_depth),
            -RATIO * GRAVITY * middle_depth * slope_x,
            -RATIO * GRAVITY * middle_depth * slope_y,
        ],
        1,
    )
    return drift + source


def evolve(state, bed_wide):
    for turn in range(2):
        padded = with_halo(state, (("space", 2),), 1)
        state = advance(padded, bed_wide[1:-1])
    return state


def add_totals(earlier, later):
    return earlier + later


def group_base(counts):
    return entering(jnp.sum(counts), "dom", add_totals, jnp.int32(0))


def route(state, counts, base):
    per_group = counts.shape[0]
    groups_count = lax.axis_size("dom")
    capacity = (2 * per_group + groups_count - 1) // groups_count
    local_ends = jnp.cumsum(counts)
    total = local_ends[-1]
    groups = jnp.arange(groups_count, dtype=jnp.int32)[:, None]
    copies = jnp.arange(capacity, dtype=jnp.int32)[None, :]
    offset = (groups - base) % groups_count + copies * groups_count
    filled = offset < total
    source = jnp.sum((local_ends[None, None, :] <= offset[:, :, None]).astype(jnp.int32), axis=-1)
    source = jnp.minimum(source, per_group - 1)
    parcel = jnp.take(state, source.reshape(-1), axis=0).reshape(
        (groups_count, capacity) + state.shape[1:]
    )
    parcel = jnp.where(filled[:, :, None, None, None], parcel, 0.0)
    label = jnp.where(filled, base + offset, -1).astype(jnp.int32)
    parcel, label = (
        lax.all_to_all(parcel, "dom", split_axis=0, concat_axis=0, tiled=True),
        lax.all_to_all(label, "dom", split_axis=0, concat_axis=0, tiled=True),
    )
    flat = parcel.reshape((groups_count * capacity,) + state.shape[1:])
    labels = label.reshape(groups_count * capacity)
    members = jnp.arange(per_group, dtype=jnp.int32)
    wanted = members * groups_count + lax.axis_index("dom")
    hit = labels[None, :] == wanted[:, None]
    entry = jnp.sum(
        hit.astype(jnp.int32) * jnp.arange(groups_count * capacity, dtype=jnp.int32)[None, :],
        axis=1,
    )
    return jnp.take(flat, entry, axis=0)


def per_device(particles, counts, bathymetry):
    bed_wide = with_halo(bathymetry, (("space", 0),), 2)
    base = group_base(counts)
    state = route(particles, counts, base)
    state = evolve(state, bed_wide)
    return state


def solution(mesh):
    in_specs = (P("dom", None, "space", None), P("dom"), P("space", None))
    out_specs = P("dom", None, "space", None)
    return jax.shard_map(
        per_device, mesh=mesh, in_specs=in_specs, out_specs=out_specs, check_vma=False
    )
```

profile of v0, /device:TPU:16, one launch (start us, length us, event | category | flops | bytes accessed | tf_op | source)
XLA Modules:
  0.0 181.8 jit_solution(9708572456626858460)
XLA Ops:
  0.0 0.0 copy-start
  0.0 1.4 reduce_sum.29
  1.4 1.3 dynamic-slice
  2.8 1.4 dynamic-update-slice
  4.1 23.5 %all-reduce = s32[32]{0:T(128)S(1)} all-reduce(s32[32]{0:T(128)S(1)} %dynamic-update-slice), channel_id=1, replica_groups=mesh['dom'=32,'space'=8] {'dom'}, use_global_device_ids=true, to_apply=%add | all-reduce | flops 32 | bytes 256
  27.7 0.7 copy.176
  28.4 0.5 slice.224
  29.0 1.3 compare_select_fusion.2
  30.3 39.6 %all-to-all-start = ((s32[32,1,1]{2,1,0:T(1,128)}), s32[32,1,1]{2,1,0:T(1,128)S(1)}, u32[]{:S(2)}, u32[]{:S(2)}) async-start(s32[32,1,1]{2,1,0:T(1,128)} %compare_select_fusion.2), calls=%async_computation | async-start | bytes 32768 | tf_op jit(solution)/shard_map/all_to_all | solution.py:114
  69.9 0.1 reduce.2
  70.0 0.1 convert_reduce_fusion
  70.1 0.6 broadcast_compare_fusion
  70.8 0.0 copy-done
  70.8 2.4 %gather_fusion = f32[32,3,16,512]{3,2,1,0:T(8,128)} fusion(f32[16,3,16,512]{3,2,1,0:T(8,128)S(1)} %copy-done, s32[1024]{0:T(1024)S(1)} %pad_clamp_fusion.1), kind=kCustom, calls=%fused_computation | custom fusion | bytes 6291584 | tf_op jit(solution)/shard_map/jit(_take)/gather | solution.py:107
  73.2 4.4 %fusion = f32[32,1,3,16,512]{4,3,2,1,0:T(8,128)} fusion(f32[32,3,16,512]{3,2,1,0:T(8,128)} %gather_fusion, pred[32]{0:T(512)(128)(4,1)S(1)} %compare_and_fusion, pred[32]{0:T(512)(128)(4,1)S(1)} %broadcast_compare_fusion), kind=kLoop, calls=%fused_computation.3 | loop fusion | flops 1572864 | bytes 6291520 | tf_op jit(solution)/shard_map/jit(_where)/select_n | solution.py:110
  77.6 0.0 copy-start.1
  77.6 2.0 %all-to-all-done = s32[32,1,1]{2,1,0:T(1,128)S(1)} async-done(((s32[32,1,1]{2,1,0:T(1,128)}), s32[32,1,1]{2,1,0:T(1,128)S(1)}, u32[]{:S(2)}, u32[]{:S(2)}) %all-to-all-start) | async-done | bytes 160 | tf_op jit(solution)/shard_map/all_to_all | solution.py:114
  79.6 8.1 %all-to-all-start.1 = ((f32[32,1,3,16,512]{4,3,2,1,0:T(8,128)}), f32[32,1,3,16,512]{4,3,2,1,0:T(8,128)}, u32[]{:S(2)}, u32[]{:S(2)}) async-start(f32[32,1,3,16,512]{4,3,2,1,0:T(8,128)} %fusion), calls=%async_computation.1 | async-start | bytes 6291456 | tf_op jit(solution)/shard_map/all_to_all | solution.py:113
  87.6 0.0 copy-done.1
  87.7 0.0 collective-permute-start.2
  87.7 0.5 collective-permute-start.3
  88.2 0.1 fusion.38
  88.3 0.1 fusion.39
  88.3 0.1 fusion.25
  88.4 0.7 reduce.1
  89.1 0.2 select_reduce_fusion
  89.3 0.0 collective-permute-done.2
  89.3 1.4 collective-permute-done.3
  90.7 67.7 %all-to-all-done.1 = f32[32,1,3,16,512]{4,3,2,1,0:T(8,128)} async-done(((f32[32,1,3,16,512]{4,3,2,1,0:T(8,128)}), f32[32,1,3,16,512]{4,3,2,1,0:T(8,128)}, u32[]{:S(2)}, u32[]{:S(2)}) %all-to-all-start.1) | async-done | bytes 3145760 | tf_op jit(solution)/shard_map/all_to_all | solution.py:113
  158.5 2.5 %gather_fusion.1 = f32[16,3,16,512]{3,2,1,0:T(8,128)S(1)} fusion(f32[32,3,16,512]{3,2,1,0:T(8,128)} %bitcast.8, s32[1024]{0:T(1024)S(1)} %pad_clamp_fusion), kind=kCustom, calls=%fused_computation.1 | custom fusion | bytes 3145792 | tf_op jit(solution)/shard_map/jit(_take)/gather | solution.py:125
  161.0 1.0 copy_select_fusion
  162.0 0.6 fusion.36
  162.6 0.0 collective-permute-start
  162.7 0.5 collective-permute-start.1
  163.2 0.2 fusion.35
  163.4 1.5 collective-permute-done
  164.9 1.8 %collective-permute-done.1 = f32[16,3,1,512]{3,0,2,1:T(8,128)S(1)} collective-permute-done((f32[16,3,1,512]{3,0,2,1:T(8,128)S(1)}, f32[16,3,1,512]{3,0,2,1:T(8,128)S(1)}, u32[]{:S(2)}, u32[]{:S(2)}) %collective-permute-start.1) | collective-permute-done | bytes 98336 | tf_op jit(solution)/shard_map/ppermute | solution.py:16
  166.7 0.2 pad_maximum_fusion
  166.9 0.5 slice_bitcast_fusion.1
  167.4 0.4 pad_maximum_fusion.1
  167.8 0.6 fusion.31
  168.4 0.1 multiply_bitcast_fusion.3
  168.5 2.3 %fusion.14 = f32[16,3,16,512]{3,0,2,1:T(8,128)S(1)} fusion(f32[16,3,18,512]{3,0,2,1:T(8,128)S(1)} %get-tuple-element.72, f32[16,1,18,512]{3,0,2,1:T(8,128)S(1)} %get-tuple-element.47, f32[16,1,18,512]{3,0,2,1:T(8,128)S(1)} %get-tuple-element.49, f32[16,1,18,512]{3,0,2,1:T(8,128)S(1)} %get-tuple-element.50, f32[16,3,16,512]{3,0,2,1:T(8,128)S(1)} %copy_select_fusion, ...), kind=kLoop, calls=%fused_computation.31 | loop fusion | flops 9043968 | bytes 15591436 | tf_op jit(solution)/shard_map/add | solution.py:77
  170.9 0.6 fusion.33
  171.5 0.2 collective-permute-start.4
  171.7 0.3 collective-permute-start.5
  172.0 0.2 fusion.32
  172.2 1.7 collective-permute-done.4
  173.9 1.8 %collective-permute-done.5 = f32[16,3,1,512]{3,0,2,1:T(8,128)S(1)} collective-permute-done((f32[16,3,1,512]{3,0,2,1:T(8,128)S(1)}, f32[16,3,1,512]{3,0,2,1:T(8,128)S(1)}, u32[]{:S(2)}, u32[]{:S(2)}) %collective-permute-start.5) | collective-permute-done | bytes 98336 | tf_op jit(solution)/shard_map/ppermute | solution.py:16
  175.7 0.2 pad_maximum_fusion.3
  175.9 0.4 slice_bitcast_fusion
  176.3 0.3 pad_maximum_fusion.4
  176.7 0.6 fusion.30
  177.2 0.1 multiply_bitcast_fusion.1
  177.4 2.3 %fusion.3 = f32[16,3,16,512]{3,0,2,1:T(8,128)S(1)} fusion(f32[16,3,18,512]{3,0,2,1:T(8,128)S(1)} %get-tuple-element.68, f32[16,1,18,512]{3,0,2,1:T(8,128)S(1)} %get-tuple-element.39, f32[16,1,18,512]{3,0,2,1:T(8,128)S(1)} %get-tuple-element.41, f32[16,1,18,512]{3,0,2,1:T(8,128)S(1)} %get-tuple-element.42, f32[16,3,16,512]{3,0,2,1:T(8,128)S(1)} %fusion.14, ...), kind=kLoop, calls=%fused_computation.13 | loop fusion | flops 9043968 | bytes 15591436 | tf_op jit(solution)/shard_map/add | solution.py:77
  179.7 2.1 %copy.178 = f32[16,3,16,512]{3,2,1,0:T(8,128)} copy(f32[16,3,16,512]{3,0,2,1:T(8,128)S(1)} %fusion.3) | data formatting | bytes 3145728 | tf_op jit(solution)/shard_map/add | solution.py:77
  (16 shorter events, 0.1 us)
Async XLA Ops:
  0.0 70.8 %copy-start = (f32[16,3,16,512]{3,2,1,0:T(8,128)S(1)}, f32[16,3,16,512]{3,2,1,0:T(8,128)}, u32[]{:S(2)}) copy-start(f32[16,3,16,512]{3,2,1,0:T(8,128)} %param.5) | copy-start | bytes 4718596
  30.3 49.3 %all-to-all-start = ((s32[32,1,1]{2,1,0:T(1,128)}), s32[32,1,1]{2,1,0:T(1,128)S(1)}, u32[]{:S(2)}, u32[]{:S(2)}) async-start(s32[32,1,1]{2,1,0:T(1,128)} %compare_select_fusion.2), calls=%async_computation | async-start | bytes 32768 | tf_op jit(solution)/shard_map/all_to_all | solution.py:114
  77.6 10.1 %copy-start.1 = (f32[16,512]{1,0:T(8,128)S(1)}, f32[16,512]{1,0:T(8,128)}, u32[]{:S(2)}) copy-start(f32[16,512]{1,0:T(8,128)} %param.7) | copy-start | bytes 98308
  79.6 78.9 %all-to-all-start.1 = ((f32[32,1,3,16,512]{4,3,2,1,0:T(8,128)}), f32[32,1,3,16,512]{4,3,2,1,0:T(8,128)}, u32[]{:S(2)}, u32[]{:S(2)}) async-start(f32[32,1,3,16,512]{4,3,2,1,0:T(8,128)} %fusion), calls=%async_computation.1 | async-start | bytes 6291456 | tf_op jit(solution)/shard_map/all_to_all | solution.py:113
  87.7 1.7 collective-permute-start.2
  87.7 3.0 %collective-permute-start.3 = (f32[2,512]{1,0:T(2,128)S(1)}, f32[2,512]{1,0:T(2,128)S(1)}, u32[]{:S(2)}, u32[]{:S(2)}) collective-permute-start(f32[2,512]{1,0:T(2,128)S(1)} %get-tuple-element.78), channel_id=1, source_target_pairs={{0,1},{1,2},{2,3},{3,4},{4,5},{5,6},{6,7},{7,0},{8,9},{9,10},{10,1... | collective-permute-start | bytes 12296 | tf_op jit(solution)/shard_map/ppermute | solution.py:16
  162.6 2.2 %collective-permute-start = (f32[16,3,1,512]{3,0,2,1:T(8,128)S(1)}, f32[16,3,1,512]{3,0,2,1:T(8,128)S(1)}, u32[]{:S(2)}, u32[]{:S(2)}) collective-permute-start(f32[16,3,1,512]{3,0,2,1:T(8,128)S(1)} %get-tuple-element.64), channel_id=1, source_target_pairs={{1,0},{2,1},{3,2},{4,3},{5,4},{6,5},{7,6},{0,7},{9,8},{10,9},{11,1... | collective-permute-start | bytes 294920 | tf_op jit(solution)/shard_map/ppermute | solution.py:19
  162.7 4.1 %collective-permute-start.1 = (f32[16,3,1,512]{3,0,2,1:T(8,128)S(1)}, f32[16,3,1,512]{3,0,2,1:T(8,128)S(1)}, u32[]{:S(2)}, u32[]{:S(2)}) collective-permute-start(f32[16,3,1,512]{3,0,2,1:T(8,128)S(1)} %get-tuple-element.63), channel_id=1, source_target_pairs={{0,1},{1,2},{2,3},{3,4},{4,5},{5,6},{6,7},{7,0},{8,9},{9,10},{10,1... | collective-permute-start | bytes 294920 | tf_op jit(solution)/shard_map/ppermute | solution.py:16
  171.5 2.4 %collective-permute-start.4 = (f32[16,3,1,512]{3,0,2,1:T(8,128)S(1)}, f32[16,3,1,512]{3,0,2,1:T(8,128)S(1)}, u32[]{:S(2)}, u32[]{:S(2)}) collective-permute-start(f32[16,3,1,512]{3,0,2,1:T(8,128)S(1)} %get-tuple-element.58), channel_id=1, source_target_pairs={{1,0},{2,1},{3,2},{4,3},{5,4},{6,5},{7,6},{0,7},{9,8},{10,9},{11,1... | collective-permute-start | bytes 294920 | tf_op jit(solution)/shard_map/ppermute | solution.py:19
  171.7 4.0 %collective-permute-start.5 = (f32[16,3,1,512]{3,0,2,1:T(8,128)S(1)}, f32[16,3,1,512]{3,0,2,1:T(8,128)S(1)}, u32[]{:S(2)}, u32[]{:S(2)}) collective-permute-start(f32[16,3,1,512]{3,0,2,1:T(8,128)S(1)} %get-tuple-element.57), channel_id=1, source_target_pairs={{0,1},{1,2},{2,3},{3,4},{4,5},{5,6},{6,7},{7,0},{8,9},{9,10},{10,1... | collective-permute-start | bytes 294920 | tf_op jit(solution)/shard_map/ppermute | solution.py:16
where the time goes:
time: 183 us; the launch traced here: 182 us
  waiting for transfers between devices  78 us (43%)
  starting transfers between devices  49.2 us (27%)
  blocking collectives  23.5 us (13%)
  other arithmetic  16.9 us (9%)
  local copies, waits for them, and re-layouts  13.9 us (8%)
    all_to_all x1, waiting for transfers between devices, route(): lax.all_to_all(parcel, 'dom', split_axis=0, concat_axis=0, tiled=True)  67.7 us
    all_to_all x1, starting transfers between devices, route(): lax.all_to_all(label, 'dom', split_axis=0, concat_axis=0, tiled=True)  39.6 us
    unnamed x1, blocking collectives  23.5 us
    all_to_all x1, starting transfers between devices, route(): lax.all_to_all(parcel, 'dom', split_axis=0, concat_axis=0, tiled=True)  8.06 us
    ppermute x3, waiting for transfers between devices, with_halo(): lax.ppermute(lax.slice_in_dim(block, block.shape[dim] - width, None, axis...  5.08 us
    add x2, other arithmetic, advance(): return drift + source  4.64 us
    select_n x1, other arithmetic, route(): parcel = jnp.where(filled[:, :, None, None, None], parcel, 0.0)  4.38 us
  transfers between devices with their start and end apart: 8, of which 7 were waited for; matrix products, arithmetic and copies ran while one was open for 5% of the time, Pallas kernels for 0%

commit v1 on v0

v1 whole, which is shorter than its diff:
```python
import jax
import jax.numpy as jnp
from jax import lax
from jax.experimental import pallas as pl
from jax.experimental.pallas import tpu as pltpu
from jax.sharding import PartitionSpec as P


def halo_permutes(particles, bed):
    count = lax.axis_size("space")
    rows = particles.shape[2]
    up = [(i, (i + 1) % count) for i in range(count)]
    down = [(target, source) for source, target in up]
    flat = particles.reshape((-1,) + particles.shape[2:])

    def edge(lo):
        return jnp.concatenate([flat[:, lo : lo + 2], bed[None, lo : lo + 2]], axis=0)

    low = lax.ppermute(edge(rows - 2), "space", up)
    high = lax.ppermute(edge(0), "space", down)
    return low, high


def one_step(h, m, n, slope_x, slope_y):
    rows, cols = h.shape
    inv = 1.0 / h
    u = m * inv
    press = 0.0625 * (h * h)
    fx = 0.125 * (m * u) + press
    cross = 0.125 * (u * n)
    gy = 0.125 * (n * (n * inv)) + press

    def combine(q, f, g):
        q = 0.25 * q
        return (
            pltpu.roll(q - f, cols - 1, 1)
            + pltpu.roll(q + f, 1, 1)
            + pltpu.roll(q - g, rows - 1, 0)
            + pltpu.roll(q + g, 1, 0)
        )

    return (
        combine(h, 0.125 * m, 0.125 * n),
        combine(m, fx, cross) + h * slope_x,
        combine(n, cross, gy) + h * slope_y,
    )


def evolve_kernel(x_ref, low_ref, high_ref, bed_ref, bed_low_ref, bed_high_ref, o_ref, ext, sx, sy):
    rows = x_ref.shape[2]
    cols = x_ref.shape[3]

    @pl.when(pl.program_id(0) == 0)
    def _():
        ext[...] = jnp.ones_like(ext)
        ext[0, 0:rows] = bed_ref[...]
        ext[0, rows : rows + 2] = bed_high_ref[0]
        ext[0, rows + 6 : rows + 8] = bed_low_ref[0]
        b = ext[0]
        sx[...] = -0.125 * (pltpu.roll(b, cols - 1, 1) - pltpu.roll(b, 1, 1))
        sy[...] = -0.125 * (pltpu.roll(b, rows + 7, 0) - pltpu.roll(b, 1, 0))

    for f in range(3):
        ext[f, 0:rows] = x_ref[0, f]
        ext[f, rows : rows + 2] = high_ref[f]
        ext[f, rows + 6 : rows + 8] = low_ref[f]
    slope_x = sx[...]
    slope_y = sy[...]
    state = (ext[0], ext[1], ext[2])
    for _ in range(2):
        state = one_step(*state, slope_x, slope_y)
    for f in range(3):
        o_ref[0, f] = state[f][0:rows]


def evolve(particles, bed, low, high):
    count, fields, rows, cols = particles.shape
    return pl.pallas_call(
        evolve_kernel,
        grid=(count,),
        in_specs=[
            pl.BlockSpec((1, fields, rows, cols), lambda i: (i, 0, 0, 0)),
            pl.BlockSpec((fields, 2, cols), lambda i: (i, 0, 0)),
            pl.BlockSpec((fields, 2, cols), lambda i: (i, 0, 0)),
            pl.BlockSpec((rows, cols), lambda i: (0, 0)),
            pl.BlockSpec((1, 2, cols), lambda i: (count * fields, 0, 0)),
            pl.BlockSpec((1, 2, cols), lambda i: (count * fields, 0, 0)),
        ],
        out_specs=pl.BlockSpec((1, fields, rows, cols), lambda i: (i, 0, 0, 0)),
        out_shape=jax.ShapeDtypeStruct(particles.shape, jnp.float32),
        scratch_shapes=[
            pltpu.VMEM((fields, rows + 8, cols), jnp.float32),
            pltpu.VMEM((rows + 8, cols), jnp.float32),
            pltpu.VMEM((rows + 8, cols), jnp.float32),
        ],
    )(particles, low, high, bed, low, high)


def per_device(particles, counts, bed):
    groups = lax.axis_size("dom")
    per_group = counts.shape[0]
    me = lax.axis_index("dom")
    low, high = halo_permutes(particles, bed)
    total = jnp.sum(counts)
    totals = lax.all_to_all(
        jnp.broadcast_to(total[None], (groups,)), "dom", 0, 0, tiled=True
    )
    index = jnp.arange(groups, dtype=jnp.int32)
    ends = jnp.sum(jnp.where(index[None, :] <= index[:, None], totals[None, :], 0), axis=1)
    base = jnp.sum(jnp.where(index < me, totals, 0))
    done = evolve(particles, bed, low, high)
    local_ends = jnp.cumsum(counts)
    offset = (index - base) % groups
    source = jnp.sum((local_ends[None, :] <= offset[:, None]).astype(jnp.int32), axis=1)
    parcel = jnp.take(done, jnp.minimum(source, per_group - 1), axis=0, mode="clip")
    parcel = lax.all_to_all(parcel, "dom", 0, 0, tiled=True)
    wanted = jnp.arange(per_group, dtype=jnp.int32) * groups + me
    entry = jnp.sum((ends[None, :] <= wanted[:, None]).astype(jnp.int32), axis=1)
    return jnp.take(parcel, entry, axis=0, mode="clip")


def solution(mesh):
    in_specs = (P("dom", None, "space", None), P("dom"), P("space", None))
    out_specs = P("dom", None, "space", None)
    return jax.shard_map(
        per_device, mesh=mesh, in_specs=in_specs, out_specs=out_specs, check_vma=False
    )
```

time: 183 us -> 126 us (0.69)
  starting transfers between devices: 49.2 us -> 17.1 us
  blocking collectives: 23.5 us -> 0 us
  other arithmetic: 16.9 us -> 3.41 us
  Pallas kernels: 0 us -> 11.2 us
  waiting for transfers between devices: 78 us -> 82.4 us
  local copies, waits for them, and re-layouts: 13.9 us -> 10.6 us
    all_to_all x2, starting transfers between devices: 47.6 us -> 15.4 us  [the longest x1 11.3 us: per_device(): lax.all_to_all(jnp.broadcast_to(total[None], (groups,)), 'dom', 0, 0, til...]
    unnamed x1 -> x0, blocking collectives: 23.5 us -> none
    all_to_all x2, waiting for transfers between devices: 69.7 us -> 82.4 us  [the longest x1 72.9 us: per_device(): parcel = lax.all_to_all(parcel, 'dom', 0, 0, tiled=True)]
    pallas_call x0 -> x1, Pallas kernels: none -> 11.2 us  [evolve(): pl.pallas_call(evolve_kernel, grid=(count,), in_specs=[pl.BlockSpec((1, f...]
    ppermute x6 -> x2, waiting for transfers between devices: 8.29 us -> 0.01 us  [the longest x1 0.01 us: halo_permutes(): low = lax.ppermute(edge(rows - 2), 'space', up)]
    select_n x6 -> x1, other arithmetic: 6.68 us -> 0.65 us  [per_device(): offset = (index - base) % groups]
    add x3 -> x1, other arithmetic: 4.65 us -> 0.01 us  [per_device(): wanted = jnp.arange(per_group, dtype=jnp.int32) * groups + me]
    add x1 -> x0, local copies, waits for them, and re-layouts: 2.06 us -> none  [advance(): return drift + source]
  transfers between devices with their start and end apart: 8 -> 4, of which waited for: 7 -> 2; matrix products, arithmetic and copies ran while one was open for 5% -> 4% of each run, Pallas kernels for 0% -> 0%
where the time goes in v1:
time: 126 us; the launch traced here: 125 us
  waiting for transfers between devices  82.4 us (65%)
  starting transfers between devices  17.1 us (14%)
  Pallas kernels  11.2 us (9%)
  local copies, waits for them, and re-layouts  10.6 us (8%)
  other arithmetic  3.41 us (3%)
    all_to_all x1, waiting for transfers between devices, per_device(): parcel = lax.all_to_all(parcel, 'dom', 0, 0, tiled=True)  72.9 us
    all_to_all x1, starting transfers between devices, per_device(): lax.all_to_all(jnp.broadcast_to(total[None], (groups,)), 'dom', 0, 0, til...  11.3 us
    pallas_call x1, Pallas kernels, evolve(): pl.pallas_call(evolve_kernel, grid=(count,), in_specs=[pl.BlockSpec((1, f...  11.2 us
    all_to_all x1, waiting for transfers between devices, per_device(): lax.all_to_all(jnp.broadcast_to(total[None], (groups,)), 'dom', 0, 0, til...  9.47 us
    all_to_all x1, starting transfers between devices, per_device(): parcel = lax.all_to_all(parcel, 'dom', 0, 0, tiled=True)  4.07 us
    gather x1, local copies, waits for them, and re-layouts, per_device(): jnp.take(done, jnp.minimum(source, per_group - 1), axis=0, mode='clip')  3.82 us
  transfers between devices with their start and end apart: 4, of which 2 were waited for; matrix products, arithmetic and copies ran while one was open for 4% of the time, Pallas kernels for 0%

profile of v1, /device:TPU:16, one launch (start us, length us, event | category | flops | bytes accessed | tf_op | source)
XLA Modules:
  0.0 124.9 jit_solution(13397233389393327956)
XLA Ops:
  0.0 0.0 copy-start.2
  0.0 1.6 %fusion.2 = (f32[48,2,512]{2,1,0:T(2,128)S(1)}, f32[48,2,512]{2,1,0:T(2,128)S(1)}) fusion(f32[48,16,512]{2,1,0:T(8,128)} %bitcast.6), kind=kLoop, calls=%fused_computation.20 | loop fusion | bytes 786432 | tf_op jit(solution)/shard_map/slice | solution.py:17
  1.6 0.7 slice_bitcast_fusion
  2.3 0.1 pad_maximum_fusion
  2.4 0.0 collective-permute-start
  2.4 0.1 pad_maximum_fusion.1
  2.5 1.7 %collective-permute-start.1 = (f32[49,2,512]{2,1,0:T(2,128)S(1)}, f32[49,2,512]{2,1,0:T(2,128)S(1)}, u32[]{:S(2)}, u32[]{:S(2)}) collective-permute-start(f32[49,2,512]{2,1,0:T(2,128)S(1)} %pad_maximum_fusion.1), channel_id=1, source_target_pairs={{1,0},{2,1},{3,2},{4,3},{5,4},{6,5},{7,6},{0,7},{9,8},{10,9},{11,1... | collective-permute-start | bytes 602120 | tf_op jit(solution)/shard_map/ppermute | solution.py:20
  4.3 0.0 copy-done.2
  4.3 0.7 reduce_sum.45
  5.0 1.3 %broadcast_in_dim.43 = s32[32,1,1]{2,1,0:T(1,128)} broadcast(s32[]{:T(128)} %reduce_sum.45), dimensions={} | broadcast | bytes 132 | tf_op jit(solution)/shard_map/broadcast_in_dim | solution.py:106
  6.3 11.3 %all-to-all-start = ((s32[32,1,1]{2,1,0:T(1,128)}), s32[32,1,1]{2,1,0:T(1,128)S(1)}, u32[]{:S(2)}, u32[]{:S(2)}) async-start(s32[32,1,1]{2,1,0:T(1,128)} %broadcast_in_dim.43), calls=%async_computation | async-start | bytes 32768 | tf_op jit(solution)/shard_map/all_to_all | solution.py:105
  17.6 0.1 copy.8
  17.7 0.1 reduce
  17.9 9.5 %all-to-all-done = s32[32,1,1]{2,1,0:T(1,128)S(1)} async-done(((s32[32,1,1]{2,1,0:T(1,128)}), s32[32,1,1]{2,1,0:T(1,128)S(1)}, u32[]{:S(2)}, u32[]{:S(2)}) %all-to-all-start) | async-done | bytes 160 | tf_op jit(solution)/shard_map/all_to_all | solution.py:105
  27.3 0.7 reduce.1
  28.0 0.6 fusion
  28.6 0.7 and_select_fusion
  29.3 0.1 convert_reduce_fusion.1
  29.4 0.0 collective-permute-done.low_ref.bed_low_ref
  29.4 0.0 copy-start
  29.4 0.0 collective-permute-done.1.high_ref.bed_high_ref
  29.4 0.7 copy-done
  30.1 0.0 copy-start.1
  30.1 0.7 copy-done.1
  30.7 11.2 %shard_map.37 = f32[16,3,16,512]{3,2,1,0:T(8,128)} custom-call(f32[16,3,16,512]{3,2,1,0:T(8,128)} %x_ref.1, f32[49,2,512]{2,1,0:T(2,128)} %copy-done, f32[49,2,512]{2,1,0:T(2,128)} %copy-done.1, f32[16,512]{1,0:T(8,128)} %bed_ref.1, f32[49,2,512]{2,1,0:T(2,128)} %copy-done, f32[49,2,512]{2,1,0:T(2,128)} %copy-done.1), custom_call_target="tpu_custom_call" | custom-call | tf_op jit(solution)/shard_map/pallas_call | solution.py:78
  42.0 3.8 %gather_fusion = f32[32,3,16,512]{3,2,1,0:T(8,128)} fusion(f32[16,3,16,512]{3,2,1,0:T(8,128)} %shard_map.37, s32[1024]{0:T(1024)S(1)} %pad_clamp_fusion.1), kind=kCustom, calls=%fused_computation | custom fusion | bytes 6291584 | tf_op jit(solution)/shard_map/jit(_take)/gather | solution.py:115
  45.8 4.1 %all-to-all-start.1 = ((f32[32,3,16,512]{3,2,1,0:T(8,128)}), f32[32,3,16,512]{3,2,1,0:T(8,128)S(1)}, u32[]{:S(2)}, u32[]{:S(2)}) async-start(f32[32,3,16,512]{3,2,1,0:T(8,128)} %gather_fusion), calls=%async_computation.1 | async-start | bytes 6291456 | tf_op jit(solution)/shard_map/all_to_all | solution.py:116
  49.9 0.1 select_reduce_fusion
  50.0 0.2 convert_reduce_fusion
  50.2 72.9 %all-to-all-done.1 = f32[32,3,16,512]{3,2,1,0:T(8,128)S(1)} async-done(((f32[32,3,16,512]{3,2,1,0:T(8,128)}), f32[32,3,16,512]{3,2,1,0:T(8,128)S(1)}, u32[]{:S(2)}, u32[]{:S(2)}) %all-to-all-start.1) | async-done | bytes 3145760 | tf_op jit(solution)/shard_map/all_to_all | solution.py:116
  123.1 1.8 %gather_fusion.1 = f32[16,3,16,512]{3,2,1,0:T(8,128)} fusion(f32[32,3,16,512]{3,2,1,0:T(8,128)S(1)} %all-to-all-done.1, s32[1024]{0:T(1024)S(1)} %pad_clamp_fusion), kind=kCustom, calls=%fused_computation.1 | custom fusion | bytes 3145792 | tf_op jit(solution)/shard_map/jit(_take)/gather | solution.py:119
  (5 shorter events, 0.1 us)
Async XLA Ops:
  0.0 4.3 %copy-start.2 = (s32[16]{0:T(128)S(1)}, s32[16]{0:T(128)}, u32[]{:S(2)}) copy-start(s32[16]{0:T(128)} %param.4) | copy-start | bytes 196
  2.4 27.0 %collective-permute-start = (f32[49,2,512]{2,1,0:T(2,128)S(1)}, f32[49,2,512]{2,1,0:T(2,128)S(1)}, u32[]{:S(2)}, u32[]{:S(2)}) collective-permute-start(f32[49,2,512]{2,1,0:T(2,128)S(1)} %pad_maximum_fusion), channel_id=1, source_target_pairs={{0,1},{1,2},{2,3},{3,4},{4,5},{5,6},{6,7},{7,0},{8,9},{9,10},{10,1... | collective-permute-start | bytes 602120 | tf_op jit(solution)/shard_map/ppermute | solution.py:19
  2.5 26.9 %collective-permute-start.1 = (f32[49,2,512]{2,1,0:T(2,128)S(1)}, f32[49,2,512]{2,1,0:T(2,128)S(1)}, u32[]{:S(2)}, u32[]{:S(2)}) collective-permute-start(f32[49,2,512]{2,1,0:T(2,128)S(1)} %pad_maximum_fusion.1), channel_id=1, source_target_pairs={{1,0},{2,1},{3,2},{4,3},{5,4},{6,5},{7,6},{0,7},{9,8},{10,9},{11,1... | collective-permute-start | bytes 602120 | tf_op jit(solution)/shard_map/ppermute | solution.py:20
  6.3 21.0 %all-to-all-start = ((s32[32,1,1]{2,1,0:T(1,128)}), s32[32,1,1]{2,1,0:T(1,128)S(1)}, u32[]{:S(2)}, u32[]{:S(2)}) async-start(s32[32,1,1]{2,1,0:T(1,128)} %broadcast_in_dim.43), calls=%async_computation | async-start | bytes 32768 | tf_op jit(solution)/shard_map/all_to_all | solution.py:105
  29.4 0.7 copy-start
  30.1 0.7 copy-start.1
  45.8 77.3 %all-to-all-start.1 = ((f32[32,3,16,512]{3,2,1,0:T(8,128)}), f32[32,3,16,512]{3,2,1,0:T(8,128)S(1)}, u32[]{:S(2)}, u32[]{:S(2)}) async-start(f32[32,3,16,512]{3,2,1,0:T(8,128)} %gather_fusion), calls=%async_computation.1 | async-start | bytes 6291456 | tf_op jit(solution)/shard_map/all_to_all | solution.py:116

commit v2 on v1

v2 whole, which is shorter than its diff:
```python
import functools

import jax
import jax.numpy as jnp
from jax import lax
from jax.experimental import pallas as pl
from jax.experimental.pallas import tpu as pltpu
from jax.sharding import Mesh, PartitionSpec as P

F32 = jnp.float32
XS, ZS = 4, 8
LANES = 128
BOXES = 10
VMEM = pl.BlockSpec(memory_space=pltpu.VMEM)
SMEM = pl.BlockSpec(memory_space=pltpu.SMEM)


def one_step(h, m, n, slope_x, slope_y):
    rows, cols = h.shape
    inv = 1.0 / h
    u = m * inv
    press = 0.0625 * (h * h)
    fx = 0.125 * (m * u) + press
    cross = 0.125 * (u * n)
    gy = 0.125 * (n * (n * inv)) + press

    def combine(q, f, g):
        q = 0.25 * q
        return (
            pltpu.roll(q - f, cols - 1, 1)
            + pltpu.roll(q + f, 1, 1)
            + pltpu.roll(q - g, rows - 1, 0)
            + pltpu.roll(q + g, 1, 0)
        )

    return (
        combine(h, 0.125 * m, 0.125 * n),
        combine(m, fx, cross) + h * slope_x,
        combine(n, cross, gy) + h * slope_y,
    )


def edge_kernel(place_ref, x_ref, bed_ref, counts_ref, low_ref, high_ref, row_ref):
    count, fields, rows, _ = x_ref.shape
    for p in range(count):
        for f in range(fields):
            low_ref[p * fields + f] = x_ref[p, f, rows - 2 : rows]
            high_ref[p * fields + f] = x_ref[p, f, 0:2]
    low_ref[count * fields] = bed_ref[rows - 2 : rows]
    high_ref[count * fields] = bed_ref[0:2]
    sub = lax.broadcasted_iota(jnp.int32, (8, LANES), 0)
    lane = lax.broadcasted_iota(jnp.int32, (8, LANES), 1)
    total = jnp.int32(0)
    tile = jnp.zeros((8, LANES), jnp.int32)
    for j in range(count):
        c = counts_ref[j]
        total = total + c
        tile = jnp.where(lane == j, c, tile)
    tile = jnp.where(lane == count, total, tile)
    tile = jnp.where(sub == place_ref[1], tile, 0).astype(F32)
    for z in range(ZS):
        row_ref[z] = tile


def evolve_kernel(place_ref, x_ref, low_ref, high_ref, bed_ref, row_ref, *refs):
    upper, lower = refs[0:XS], refs[XS : 2 * XS]
    ext, sx, sy, res = refs[2 * XS :]
    count, fields, rows, cols = x_ref.shape
    ext[...] = jnp.ones_like(ext)
    ext[0, 0:rows] = bed_ref[...]
    ext[0, rows : rows + 2] = high_ref[count * fields]
    ext[0, rows + 6 : rows + 8] = low_ref[count * fields]
    b = ext[0]
    sx[...] = -0.125 * (pltpu.roll(b, cols - 1, 1) - pltpu.roll(b, 1, 1))
    sy[...] = -0.125 * (pltpu.roll(b, rows + 7, 0) - pltpu.roll(b, 1, 0))
    x = place_ref[0]

    def body(p, carry):
        for f in range(fields):
            ext[f, 0:rows] = x_ref[p, f]
            ext[f, rows : rows + 2] = high_ref[p * fields + f]
            ext[f, rows + 6 : rows + 8] = low_ref[p * fields + f]
        slope_x = sx[...]
        slope_y = sy[...]
        state = (ext[0], ext[1], ext[2])
        for _ in range(2):
            state = one_step(*state, slope_x, slope_y)
        for f in range(fields):
            res[f] = state[f][0:rows]
        for k in range(XS):
            at = pl.multiple_of(((x + k) % XS) * LANES, LANES)
            for f in range(fields):
                upper[k][p, f] = res[f, 0:8, pl.ds(at, LANES)]
                lower[k][p, f] = res[f, 8:16, pl.ds(at, LANES)]
        return carry

    lax.fori_loop(0, count, body, 0)
    tile = row_ref[0]
    for z in range(1, ZS):
        tile = tile + row_ref[z]
    for k in range(XS):
        upper[k][count, 0] = tile
        upper[k][count, 1] = tile
        upper[k][count, 2] = tile


def load_counts(x, tiles, cnt, sem):
    copies = []
    for k in range(XS):
        copies.append(
            pltpu.make_async_copy(tiles[k], cnt.at[(x + XS - k) % XS], sem.at[k])
        )
    for copy in copies:
        copy.start()
    for copy in copies:
        copy.wait()


def pack_kernel(with_table, half, place_ref, *refs):
    tiles, data = refs[0:XS], refs[XS : 2 * XS]
    out_ref = refs[2 * XS]
    table_ref = refs[2 * XS + 1] if with_table else None
    cnt, base, ctr, sem = refs[-4:]
    x, z = place_ref[0], place_ref[1]
    load_counts(x, [t.at[16, 0] for t in tiles], cnt, sem)
    total = jnp.int32(0)
    for g in range(XS * ZS):
        base[g] = total
        total = total + cnt[g // ZS, g % ZS, 16].astype(jnp.int32)
    base[XS * ZS] = total
    for i in range(ZS):
        ctr[i] = 0

    def put(src, j, slot):
        to = slot & (ZS - 1)
        t = ctr[to]
        ctr[to] = t + 1
        out_ref[to, t] = src[j]

    for k in range(XS):
        at = (x + XS - k) % XS
        src = data[k]

        def body(j, e):
            c = cnt[at, z, j].astype(jnp.int32)

            @pl.when(c > 0)
            def _():
                put(src, j, e)

            @pl.when(c > 1)
            def _():
                put(src, j, e + 1)

            return e + c

        lax.fori_loop(0, 16, body, base[at * ZS + z])

    if with_table:
        for i in range(ZS):
            ctr[i] = 0
        for i in range(16 * XS):
            table_ref[i] = 0
        for k in range(XS):
            at = (x + XS - k) % XS

            def groups(zs, carry):
                lo = base[at * ZS + zs]
                hi = base[at * ZS + zs + 1]
                first = lo + ((z - lo) & (ZS - 1))
                for i in range(4):
                    s = first + i * ZS

                    @pl.when(s < hi)
                    def _():
                        t = ctr[zs]
                        ctr[zs] = t + 1
                        table_ref[s >> 3] = zs * 16 + t

                return carry

            lax.fori_loop(0, ZS, groups, 0)


def pack(place, tiles, data, with_table):
    out_shape = [jax.ShapeDtypeStruct((ZS, BOXES, 3, 8, LANES), F32)]
    out_specs = [VMEM]
    if with_table:
        out_shape.append(jax.ShapeDtypeStruct((16 * XS,), jnp.int32))
        out_specs.append(SMEM)
    return pl.pallas_call(
        functools.partial(pack_kernel, with_table, 0),
        in_specs=[SMEM] + [VMEM] * (2 * XS),
        out_specs=out_specs,
        out_shape=out_shape,
        scratch_shapes=[
            pltpu.SMEM((XS, 8, LANES), F32),
            pltpu.SMEM((XS * ZS + 1,), jnp.int32),
            pltpu.SMEM((ZS,), jnp.int32),
            pltpu.SemaphoreType.DMA((XS,)),
        ],
        cost_estimate=pl.CostEstimate(flops=0, bytes_accessed=4_000_000, transcendentals=0),
    )(place, *tiles, *data)


def spread_kernel(place_ref, table_ref, in_ref, *outs):
    x = place_ref[0]
    for k in range(XS):
        to = (x + k) % XS
        out = outs[k]

        def body(i, carry):
            code = table_ref[i * XS + to]
            out[i] = in_ref[code >> 4, code & 15]
            return carry

        lax.fori_loop(0, 16, body, 0, unroll=4)


def spread(place, table, boxes):
    return pl.pallas_call(
        spread_kernel,
        in_specs=[SMEM, SMEM, VMEM],
        out_specs=[VMEM] * XS,
        out_shape=[jax.ShapeDtypeStruct((16, 3, 8, LANES), F32)] * XS,
        cost_estimate=pl.CostEstimate(flops=0, bytes_accessed=4_000_000, transcendentals=0),
    )(place, table, boxes)


def join_kernel(place_ref, *refs):
    parts, out_ref = refs[: 2 * XS], refs[2 * XS]
    x = place_ref[0]
    for k in range(XS):
        at = pl.multiple_of(((x + XS - k) % XS) * LANES, LANES)

        def body(i, carry):
            for f in range(3):
                out_ref[i, f, 0:8, pl.ds(at, LANES)] = parts[k][i, f]
                out_ref[i, f, 8:16, pl.ds(at, LANES)] = parts[XS + k][i, f]
            return carry

        lax.fori_loop(0, 16, body, 0, unroll=4)


def along_x(parts):
    return [parts[0]] + [
        lax.ppermute(parts[k], "x", [(i, (i + k) % XS) for i in range(XS)]) for k in range(1, XS)
    ]


def per_device(particles, counts, bed):
    count, fields, rows, cols = particles.shape
    place = jnp.stack([lax.axis_index("x"), lax.axis_index("z")]).astype(jnp.int32)
    edges = jax.ShapeDtypeStruct((count * fields + 1, 2, cols), F32)
    low, high, row = pl.pallas_call(
        edge_kernel,
        in_specs=[SMEM, VMEM, VMEM, SMEM],
        out_specs=[VMEM] * 3,
        out_shape=[edges, edges, jax.ShapeDtypeStruct((ZS, 8, LANES), F32)],
    )(place, particles, bed, counts)
    strips = lax.axis_size("space")
    low = lax.ppermute(low, "space", [(i, (i + 1) % strips) for i in range(strips)])
    high = lax.ppermute(high, "space", [((i + 1) % strips, i) for i in range(strips)])
    row = lax.all_to_all(row, "z", 0, 0, tiled=True)
    first = jax.ShapeDtypeStruct((count + 1, fields, 8, LANES), F32)
    second = jax.ShapeDtypeStruct((count, fields, 8, LANES), F32)
    parts = pl.pallas_call(
        evolve_kernel,
        in_specs=[SMEM] + [VMEM] * 5,
        out_specs=[VMEM] * (2 * XS),
        out_shape=[first] * XS + [second] * XS,
        scratch_shapes=[
            pltpu.VMEM((fields, rows + 8, cols), F32),
            pltpu.VMEM((rows + 8, cols), F32),
            pltpu.VMEM((rows + 8, cols), F32),
            pltpu.VMEM((fields, rows, cols), F32),
        ],
        cost_estimate=pl.CostEstimate(flops=0, bytes_accessed=20_000_000, transcendentals=0),
    )(place, particles, low, high, bed, row)
    upper = along_x(parts[:XS])
    lower = along_x(parts[XS:])
    boxes_a, table = pack(place, upper, upper, True)
    boxes_a = lax.all_to_all(boxes_a, "z", 0, 0, tiled=True)
    boxes_b = pack(place, upper, lower, False)[0]
    boxes_b = lax.all_to_all(boxes_b, "z", 0, 0, tiled=True)
    out_a = along_x(spread(place, table, boxes_a))
    out_b = along_x(spread(place, table, boxes_b))
    return pl.pallas_call(
        join_kernel,
        in_specs=[SMEM] + [VMEM] * (2 * XS),
        out_specs=VMEM,
        out_shape=jax.ShapeDtypeStruct(particles.shape, F32),
    )(place, *out_a, *out_b)


def solution(mesh):
    wide = Mesh(mesh.devices.reshape(XS, ZS, -1), ("x", "z", "space"))
    in_specs = (P(("x", "z"), None, "space", None), P(("x", "z")), P("space", None))
    out_specs = P(("x", "z"), None, "space", None)
    return jax.shard_map(
        per_device, mesh=wide, in_specs=in_specs, out_specs=out_specs, check_vma=False
    )
```

time: 126 us -> 129 us (1.024)
  waiting for transfers between devices: 82.4 us -> 41.9 us
  Pallas kernels: 11.2 us -> 28.6 us
  starting transfers between devices: 17.1 us -> 34.5 us
  blocking collectives: 0 us -> 16.6 us
  local copies, waits for them, and re-layouts: 10.6 us -> 4.56 us
  other arithmetic: 3.41 us -> 0.64 us
    all_to_all x2, waiting for transfers between devices: 82.4 us -> 24.3 us  [the longest x1 16.4 us: per_device(): boxes_b = lax.all_to_all(boxes_b, 'z', 0, 0, tiled=True)]
    ppermute x2 -> x14, starting transfers between devices: 1.76 us -> 27.4 us  [the longest x12 25.6 us: along_x(): lax.ppermute(parts[k], 'x', [(i, (i + k) % XS) for i in range(XS)])]
    ppermute x2 -> x14, waiting for transfers between devices: 0.01 us -> 17.5 us  [the longest x12 17.5 us: along_x(): lax.ppermute(parts[k], 'x', [(i, (i + k) % XS) for i in range(XS)])]
    pallas_call x1 -> x7, Pallas kernels: 11.2 us -> 28.6 us  [the longest x2 11.2 us: pack(): pl.pallas_call(functools.partial(pack_kernel, with_table, 0), in_specs=[S...]
    all_to_all x0 -> x1, blocking collectives: none -> 16.6 us  [per_device(): row = lax.all_to_all(row, 'z', 0, 0, tiled=True)]
    all_to_all x2, starting transfers between devices: 15.4 us -> 7.12 us  [the longest x1 3.57 us: per_device(): boxes_a = lax.all_to_all(boxes_a, 'z', 0, 0, tiled=True)]
    gather x2 -> x0, local copies, waits for them, and re-layouts: 5.61 us -> none  [the longest x1 3.82 us: per_device(): jnp.take(done, jnp.minimum(source, per_group - 1), axis=0, mode='clip')]
    unnamed x6 -> x38, local copies, waits for them, and re-layouts: 1.33 us -> 4.56 us
  transfers between devices with their start and end apart: 4 -> 16, of which waited for: 2 -> 8; matrix products, arithmetic and copies ran while one was open for 4% -> 0% of each run, Pallas kernels for 0% -> 8%
where the time goes in v2:
time: 129 us; the launch traced here: 127 us
  waiting for transfers between devices  41.9 us (32%)
  starting transfers between devices  34.5 us (27%)
  Pallas kernels  28.6 us (22%)
  blocking collectives  16.6 us (13%)
  local copies, waits for them, and re-layouts  4.56 us (4%)
    ppermute x12, starting transfers between devices, along_x(): lax.ppermute(parts[k], 'x', [(i, (i + k) % XS) for i in range(XS)])  25.6 us
    ppermute x12, waiting for transfers between devices, along_x(): lax.ppermute(parts[k], 'x', [(i, (i + k) % XS) for i in range(XS)])  17.5 us
    all_to_all x1, blocking collectives, per_device(): row = lax.all_to_all(row, 'z', 0, 0, tiled=True)  16.6 us
    all_to_all x1, waiting for transfers between devices, per_device(): boxes_b = lax.all_to_all(boxes_b, 'z', 0, 0, tiled=True)  16.4 us
    pallas_call x2, Pallas kernels, pack(): pl.pallas_call(functools.partial(pack_kernel, with_table, 0), in_specs=[S...  11.2 us
    all_to_all x1, waiting for transfers between devices, per_device(): boxes_a = lax.all_to_all(boxes_a, 'z', 0, 0, tiled=True)  7.94 us
    pallas_call x1, Pallas kernels, per_device(): pl.pallas_call(evolve_kernel, in_specs=[SMEM] + [VMEM] * 5, out_specs=[VM...  7.61 us
    pallas_call x2, Pallas kernels, spread(): pl.pallas_call(spread_kernel, in_specs=[SMEM, SMEM, VMEM], out_specs=[VME...  4.72 us
  transfers between devices with their start and end apart: 16, of which 8 were waited for; matrix products, arithmetic and copies ran while one was open for 0% of the time, Pallas kernels for 8%

profile of v2, /device:TPU:16, one launch (start us, length us, event | category | flops | bytes accessed | tf_op | source)
XLA Modules:
  0.0 126.9 jit_solution(12612708350505129558)
XLA Ops:
  0.0 0.6 pad_add_fusion.place_ref
  0.6 2.2 %shard_map.37 = (f32[49,2,512]{2,1,0:T(2,128)}, f32[49,2,512]{2,1,0:T(2,128)}, f32[8,8,128]{2,1,0:T(8,128)}) custom-call(s32[2]{0:T(128)} %pad_add_fusion.place_ref, f32[16,3,16,512]{3,2,1,0:T(8,128)} %x_ref.3, f32[16,512]{1,0:T(8,128)} %bed_ref.3, s32[16]{0:T(128)} %counts_ref.1), custom_call_target="tpu_custom_call" | custom-call | tf_op jit(solution)/shard_map/pallas_call | solution.py:255
  2.9 0.0 collective-permute-start
  2.9 1.7 %collective-permute-start.1 = (f32[49,2,512]{2,1,0:T(2,128)}, f32[49,2,512]{2,1,0:T(2,128)S(1)}, u32[]{:S(2)}, u32[]{:S(2)}) collective-permute-start(f32[49,2,512]{2,1,0:T(2,128)} %get-tuple-element.27), channel_id=1, source_target_pairs={{1,0},{2,1},{3,2},{4,3},{5,4},{6,5},{7,6},{0,7},{9,8},{10,9},{11,1... | collective-permute-start | bytes 602120 | tf_op jit(solution)/shard_map/ppermute | solution.py:263
  4.6 16.6 %all_to_all.15.row_ref = f32[8,8,128]{2,1,0:T(8,128)} all-to-all(f32[8,8,128]{2,1,0:T(8,128)} %get-tuple-element.28), channel_id=1, replica_groups=mesh['x'=4,'z'=8,'space'=8] {'z'}, dimensions={0} | all-to-all | bytes 65536 | tf_op jit(solution)/shard_map/all_to_all | solution.py:264
  21.2 0.0 collective-permute-done.low_ref
  21.2 0.0 copy-start.5
  21.2 0.0 collective-permute-done.1.high_ref
  21.2 0.7 copy-done.5
  21.9 0.0 copy-start.6
  21.9 0.7 copy-done.6
  22.6 7.6 %shard_map.38 = (f32[17,3,8,128]{3,2,1,0:T(8,128)}, f32[17,3,8,128]{3,2,1,0:T(8,128)}, f32[17,3,8,128]{3,2,1,0:T(8,128)}, f32[17,3,8,128]{3,2,1,0:T(8,128)}, f32...) custom-call(s32[2]{0:T(128)} %pad_add_fusion.place_ref, ...), custom_call_target="tpu_custom_call" | custom-call | bytes 20000000 | tf_op jit(solution)/shard_map/pallas_call | solution.py:267
  30.2 1.4 %collective-permute-start.2 = (f32[17,3,8,128]{3,2,1,0:T(8,128)}, f32[17,3,8,128]{3,2,1,0:T(8,128)S(1)}, u32[]{:S(2)}, u32[]{:S(2)}) collective-permute-start(f32[17,3,8,128]{3,2,1,0:T(8,128)} %get-tuple-element.30), channel_id=1, source_target_pairs={{0,64},{64,128},{128,192},{192,0},{1,65},{65,129},{129,193},{193,1... | collective-permute-start | bytes 626696 | tf_op jit(solution)/shard_map/ppermute | solution.py:247
  31.6 2.8 %collective-permute-start.3 = (f32[17,3,8,128]{3,2,1,0:T(8,128)}, f32[17,3,8,128]{3,2,1,0:T(8,128)S(1)}, u32[]{:S(2)}, u32[]{:S(2)}) collective-permute-start(f32[17,3,8,128]{3,2,1,0:T(8,128)} %get-tuple-element.31), channel_id=1, source_target_pairs={{0,128},{64,192},{128,0},{192,64},{1,129},{65,193},{129,1},{193,65... | collective-permute-start | bytes 626696 | tf_op jit(solution)/shard_map/ppermute | solution.py:247
  34.4 1.4 %collective-permute-start.4 = (f32[17,3,8,128]{3,2,1,0:T(8,128)}, f32[17,3,8,128]{3,2,1,0:T(8,128)S(1)}, u32[]{:S(2)}, u32[]{:S(2)}) collective-permute-start(f32[17,3,8,128]{3,2,1,0:T(8,128)} %get-tuple-element.32), channel_id=1, source_target_pairs={{0,192},{64,0},{128,64},{192,128},{1,193},{65,1},{129,65},{193,129... | collective-permute-start | bytes 626696 | tf_op jit(solution)/shard_map/ppermute | solution.py:247
  35.8 3.9 %collective-permute-done.2.refs_1_.refs_5_ = f32[17,3,8,128]{3,2,1,0:T(8,128)S(1)} collective-permute-done((f32[17,3,8,128]{3,2,1,0:T(8,128)}, f32[17,3,8,128]{3,2,1,0:T(8,128)S(1)}, u32[]{:S(2)}, u32[]{:S(2)}) %collective-permute-start.2) | collective-permute-done | bytes 208928 | tf_op jit(solution)/shard_map/ppermute | solution.py:247
  39.7 2.7 %collective-permute-done.3.refs_2_.refs_6_ = f32[17,3,8,128]{3,2,1,0:T(8,128)S(1)} collective-permute-done((f32[17,3,8,128]{3,2,1,0:T(8,128)}, f32[17,3,8,128]{3,2,1,0:T(8,128)S(1)}, u32[]{:S(2)}, u32[]{:S(2)}) %collective-permute-start.3) | collective-permute-done | bytes 208928 | tf_op jit(solution)/shard_map/ppermute | solution.py:247
  42.4 0.0 copy-start.3
  42.4 0.0 collective-permute-done.4.refs_3_.refs_7_
  42.4 0.0 copy-done.2
  42.4 0.7 copy-done.3
  43.1 0.1 copy-done.4
  43.2 6.1 %shard_map.39 = (f32[8,10,3,8,128]{4,3,2,1,0:T(8,128)}, s32[64]{0:T(128)}) custom-call(s32[2]{0:T(128)} %pad_add_fusion.place_ref, f32[17,3,8,128]{3,2,1,0:T(8,128)} %get-tuple-element.29.refs_0_.refs_4_, f32[17,3,8,128]{3,2,1,0:T(8,128)} %copy-done.2, f32[17,3,8,128]{3,2,1,0:T(8,128)} %copy-done.3, f32[17,3,8,128]{3,2,1,0:T(8,128)} %copy-done.4, ...), custom_call_target="tpu_custom_call" | custom-call | bytes 4000000 | tf_op jit(solution)/shard_map/pallas_call | solution.py:191
  49.2 3.6 %all-to-all-start.1 = ((f32[8,10,3,8,128]{4,3,2,1,0:T(8,128)}), f32[8,10,3,8,128]{4,3,2,1,0:T(8,128)S(1)}, u32[]{:S(2)}, u32[]{:S(2)}) async-start(f32[8,10,3,8,128]{4,3,2,1,0:T(8,128)} %get-tuple-element.34), calls=%async_computation.1 | async-start | bytes 1966080 | tf_op jit(solution)/shard_map/all_to_all | solution.py:283
  52.8 0.0 copy-done.18
  52.8 1.3 %collective-permute-start.8 = (f32[16,3,8,128]{3,2,1,0:T(8,128)S(1)}, f32[16,3,8,128]{3,2,1,0:T(8,128)S(1)}, u32[]{:S(2)}, u32[]{:S(2)}) collective-permute-start(f32[16,3,8,128]{3,2,1,0:T(8,128)S(1)} %copy-done.18), channel_id=1, source_target_pairs={{0,64},{64,128},{128,192},{192,0},{1,65},{65,129},{129,193},{193,1... | collective-permute-start | bytes 589832 | tf_op jit(solution)/shard_map/ppermute | solution.py:247
  54.2 0.0 copy-done.17
  54.2 2.4 %collective-permute-start.9 = (f32[16,3,8,128]{3,2,1,0:T(8,128)S(1)}, f32[16,3,8,128]{3,2,1,0:T(8,128)S(1)}, u32[]{:S(2)}, u32[]{:S(2)}) collective-permute-start(f32[16,3,8,128]{3,2,1,0:T(8,128)S(1)} %copy-done.17), channel_id=1, source_target_pairs={{0,128},{64,192},{128,0},{192,64},{1,129},{65,193},{129,1},{193,65... | collective-permute-start | bytes 589832 | tf_op jit(solution)/shard_map/ppermute | solution.py:247
  56.5 0.0 copy-done.16
  56.5 1.5 %collective-permute-start.10 = (f32[16,3,8,128]{3,2,1,0:T(8,128)S(1)}, f32[16,3,8,128]{3,2,1,0:T(8,128)S(1)}, u32[]{:S(2)}, u32[]{:S(2)}) collective-permute-start(f32[16,3,8,128]{3,2,1,0:T(8,128)S(1)} %copy-done.16), channel_id=1, source_target_pairs={{0,192},{64,0},{128,64},{192,128},{1,193},{65,1},{129,65},{193,129... | collective-permute-start | bytes 589832 | tf_op jit(solution)/shard_map/ppermute | solution.py:247
  58.1 3.6 %collective-permute-done.8.refs_5_ = f32[16,3,8,128]{3,2,1,0:T(8,128)S(1)} collective-permute-done((f32[16,3,8,128]{3,2,1,0:T(8,128)S(1)}, f32[16,3,8,128]{3,2,1,0:T(8,128)S(1)}, u32[]{:S(2)}, u32[]{:S(2)}) %collective-permute-start.8) | collective-permute-done | bytes 196640 | tf_op jit(solution)/shard_map/ppermute | solution.py:247
  61.6 2.1 %collective-permute-done.9.refs_6_ = f32[16,3,8,128]{3,2,1,0:T(8,128)S(1)} collective-permute-done((f32[16,3,8,128]{3,2,1,0:T(8,128)S(1)}, f32[16,3,8,128]{3,2,1,0:T(8,128)S(1)}, u32[]{:S(2)}, u32[]{:S(2)}) %collective-permute-start.9) | collective-permute-done | bytes 196640 | tf_op jit(solution)/shard_map/ppermute | solution.py:247
  63.7 0.0 collective-permute-done.10.refs_7_
  63.7 0.0 copy-done.7
  63.7 0.7 copy-done.8
  64.4 0.1 copy-done.9
  64.5 5.1 %shard_map.41 = f32[8,10,3,8,128]{4,3,2,1,0:T(8,128)} custom-call(s32[2]{0:T(128)} %pad_add_fusion.place_ref, f32[17,3,8,128]{3,2,1,0:T(8,128)} %get-tuple-element.29.refs_0_.refs_4_, f32[17,3,8,128]{3,2,1,0:T(8,128)} %copy-done.2, f32[17,3,8,128]{3,2,1,0:T(8,128)} %copy-done.3, f32[17,3,8,128]{3,2,1,0:T(8,128)} %copy-done.4, ...), custom_call_target="tpu_custom_call" | custom-call | bytes 4000000 | tf_op jit(solution)/shard_map/pallas_call | solution.py:191
  69.6 7.9 %all-to-all-done.1.in_ref = f32[8,10,3,8,128]{4,3,2,1,0:T(8,128)S(1)} async-done(((f32[8,10,3,8,128]{4,3,2,1,0:T(8,128)}), f32[8,10,3,8,128]{4,3,2,1,0:T(8,128)S(1)}, u32[]{:S(2)}, u32[]{:S(2)}) %all-to-all-start.1) | async-done | bytes 983072 | tf_op jit(solution)/shard_map/all_to_all | solution.py:283
  77.5 3.6 %all-to-all-start.2 = ((f32[8,10,3,8,128]{4,3,2,1,0:T(8,128)}), f32[8,10,3,8,128]{4,3,2,1,0:T(8,128)S(1)}, u32[]{:S(2)}, u32[]{:S(2)}) async-start(f32[8,10,3,8,128]{4,3,2,1,0:T(8,128)} %shard_map.41), calls=%async_computation.2 | async-start | bytes 1966080 | tf_op jit(solution)/shard_map/all_to_all | solution.py:285
  81.1 0.0 copy-done
  81.1 2.4 %shard_map.40 = (f32[16,3,8,128]{3,2,1,0:T(8,128)}, f32[16,3,8,128]{3,2,1,0:T(8,128)}, f32[16,3,8,128]{3,2,1,0:T(8,128)}, f32[16,3,8,128]{3,2,1,0:T(8,128)}) custom-call(s32[2]{0:T(128)} %pad_add_fusion.place_ref, s32[64]{0:T(128)} %get-tuple-element.33.table_ref, f32[8,10,3,8,128]{4,3,2,1,0:T(8,128)} %copy-done), custom_call_target="tpu_custom_call" | custom-call | bytes 4000000 | tf_op jit(solution)/shard_map/pallas_call | solution.py:221
  83.5 3.2 %collective-permute-start.5 = (f32[16,3,8,128]{3,2,1,0:T(8,128)}, f32[16,3,8,128]{3,2,1,0:T(8,128)S(1)}, u32[]{:S(2)}, u32[]{:S(2)}) collective-permute-start(f32[16,3,8,128]{3,2,1,0:T(8,128)} %get-tuple-element.36), channel_id=1, source_target_pairs={{0,64},{64,128},{128,192},{192,0},{1,65},{65,129},{129,193},{193,1... | collective-permute-start | bytes 589832 | tf_op jit(solution)/shard_map/ppermute | solution.py:247
  86.7 1.6 %collective-permute-start.6 = (f32[16,3,8,128]{3,2,1,0:T(8,128)}, f32[16,3,8,128]{3,2,1,0:T(8,128)S(1)}, u32[]{:S(2)}, u32[]{:S(2)}) collective-permute-start(f32[16,3,8,128]{3,2,1,0:T(8,128)} %get-tuple-element.37), channel_id=1, source_target_pairs={{0,128},{64,192},{128,0},{192,64},{1,129},{65,193},{129,1},{193,65... | collective-permute-start | bytes 589832 | tf_op jit(solution)/shard_map/ppermute | solution.py:247
  88.3 1.1 collective-permute-start.7
  89.3 16.4 %all-to-all-done.2.in_ref = f32[8,10,3,8,128]{4,3,2,1,0:T(8,128)S(1)} async-done(((f32[8,10,3,8,128]{4,3,2,1,0:T(8,128)}), f32[8,10,3,8,128]{4,3,2,1,0:T(8,128)S(1)}, u32[]{:S(2)}, u32[]{:S(2)}) %all-to-all-start.2) | async-done | bytes 983072 | tf_op jit(solution)/shard_map/all_to_all | solution.py:285
  105.8 0.9 copy-done.1
  106.7 2.4 %shard_map.42 = (f32[16,3,8,128]{3,2,1,0:T(8,128)}, f32[16,3,8,128]{3,2,1,0:T(8,128)}, f32[16,3,8,128]{3,2,1,0:T(8,128)}, f32[16,3,8,128]{3,2,1,0:T(8,128)}) custom-call(s32[2]{0:T(128)} %pad_add_fusion.place_ref, s32[64]{0:T(128)} %get-tuple-element.33.table_ref, f32[8,10,3,8,128]{4,3,2,1,0:T(8,128)} %copy-done.1), custom_call_target="tpu_custom_call" | custom-call | bytes 4000000 | tf_op jit(solution)/shard_map/pallas_call | solution.py:221
  109.0 6.2 %collective-permute-start.11 = (f32[16,3,8,128]{3,2,1,0:T(8,128)}, f32[16,3,8,128]{3,2,1,0:T(8,128)S(1)}, u32[]{:S(2)}, u32[]{:S(2)}) collective-permute-start(f32[16,3,8,128]{3,2,1,0:T(8,128)} %get-tuple-element.44), channel_id=1, source_target_pairs={{0,64},{64,128},{128,192},{192,0},{1,65},{65,129},{129,193},{193,1... | collective-permute-start | bytes 589832 | tf_op jit(solution)/shard_map/ppermute | solution.py:247
  115.3 0.0 collective-permute-start.12
  115.3 0.0 collective-permute-done.5.refs_1_
  115.3 2.7 %collective-permute-start.13 = (f32[16,3,8,128]{3,2,1,0:T(8,128)}, f32[16,3,8,128]{3,2,1,0:T(8,128)S(1)}, u32[]{:S(2)}, u32[]{:S(2)}) collective-permute-start(f32[16,3,8,128]{3,2,1,0:T(8,128)} %get-tuple-element.46), channel_id=1, source_target_pairs={{0,192},{64,0},{128,64},{192,128},{1,193},{65,1},{129,65},{193,129... | collective-permute-start | bytes 589832 | tf_op jit(solution)/shard_map/ppermute | solution.py:247
  118.0 0.0 collective-permute-done.6.refs_2_
  118.0 0.0 collective-permute-done.7.refs_3_
  118.0 0.0 copy-start.12
  118.0 2.0 %collective-permute-done.11.refs_5_ = f32[16,3,8,128]{3,2,1,0:T(8,128)S(1)} collective-permute-done((f32[16,3,8,128]{3,2,1,0:T(8,128)}, f32[16,3,8,128]{3,2,1,0:T(8,128)S(1)}, u32[]{:S(2)}, u32[]{:S(2)}) %collective-permute-start.11) | collective-permute-done | bytes 196640 | tf_op jit(solution)/shard_map/ppermute | solution.py:247
  120.0 3.3 %collective-permute-done.12.refs_6_ = f32[16,3,8,128]{3,2,1,0:T(8,128)S(1)} collective-permute-done((f32[16,3,8,128]{3,2,1,0:T(8,128)}, f32[16,3,8,128]{3,2,1,0:T(8,128)S(1)}, u32[]{:S(2)}, u32[]{:S(2)}) %collective-permute-start.12) | collective-permute-done | bytes 196640 | tf_op jit(solution)/shard_map/ppermute | solution.py:247
  123.3 0.0 collective-permute-done.13.refs_7_
  123.3 0.0 copy-done.10
  123.3 0.0 copy-done.11
  123.3 0.0 copy-done.12
  123.3 0.0 copy-done.13
  123.3 0.6 copy-done.14
  124.0 0.1 copy-done.15
  124.0 2.8 %shard_map.43 = f32[16,3,16,512]{3,2,1,0:T(8,128)} custom-call(s32[2]{0:T(128)} %pad_add_fusion.place_ref, f32[16,3,8,128]{3,2,1,0:T(8,128)} %get-tuple-element.35.refs_0_, f32[16,3,8,128]{3,2,1,0:T(8,128)} %copy-done.10, f32[16,3,8,128]{3,2,1,0:T(8,128)} %copy-done.11, f32[16,3,8,128]{3,2,1,0:T(8,128)} %copy-done.12, ...), custom_call_target="tpu_custom_call" | custom-call | tf_op jit(solution)/shard_map/pallas_call | solution.py:288
  (15 shorter events, 0.0 us)
Async XLA Ops:
  2.9 18.3 %collective-permute-start = (f32[49,2,512]{2,1,0:T(2,128)}, f32[49,2,512]{2,1,0:T(2,128)S(1)}, u32[]{:S(2)}, u32[]{:S(2)}) collective-permute-start(f32[49,2,512]{2,1,0:T(2,128)} %get-tuple-element.26), channel_id=1, source_target_pairs={{0,1},{1,2},{2,3},{3,4},{4,5},{5,6},{6,7},{7,0},{8,9},{9,10},{10,1... | collective-permute-start | bytes 602120 | tf_op jit(solution)/shard_map/ppermute | solution.py:262
  2.9 18.3 %collective-permute-start.1 = (f32[49,2,512]{2,1,0:T(2,128)}, f32[49,2,512]{2,1,0:T(2,128)S(1)}, u32[]{:S(2)}, u32[]{:S(2)}) collective-permute-start(f32[49,2,512]{2,1,0:T(2,128)} %get-tuple-element.27), channel_id=1, source_target_pairs={{1,0},{2,1},{3,2},{4,3},{5,4},{6,5},{7,6},{0,7},{9,8},{10,9},{11,1... | collective-permute-start | bytes 602120 | tf_op jit(solution)/shard_map/ppermute | solution.py:263
  21.2 0.7 copy-start.5
  21.9 0.7 copy-start.6
  30.2 9.5 %collective-permute-start.2 = (f32[17,3,8,128]{3,2,1,0:T(8,128)}, f32[17,3,8,128]{3,2,1,0:T(8,128)S(1)}, u32[]{:S(2)}, u32[]{:S(2)}) collective-permute-start(f32[17,3,8,128]{3,2,1,0:T(8,128)} %get-tuple-element.30), channel_id=1, source_target_pairs={{0,64},{64,128},{128,192},{192,0},{1,65},{65,129},{129,193},{193,1... | collective-permute-start | bytes 626696 | tf_op jit(solution)/shard_map/ppermute | solution.py:247
  31.6 10.8 %collective-permute-start.3 = (f32[17,3,8,128]{3,2,1,0:T(8,128)}, f32[17,3,8,128]{3,2,1,0:T(8,128)S(1)}, u32[]{:S(2)}, u32[]{:S(2)}) collective-permute-start(f32[17,3,8,128]{3,2,1,0:T(8,128)} %get-tuple-element.31), channel_id=1, source_target_pairs={{0,128},{64,192},{128,0},{192,64},{1,129},{65,193},{129,1},{193,65... | collective-permute-start | bytes 626696 | tf_op jit(solution)/shard_map/ppermute | solution.py:247
  34.4 8.0 %collective-permute-start.4 = (f32[17,3,8,128]{3,2,1,0:T(8,128)}, f32[17,3,8,128]{3,2,1,0:T(8,128)S(1)}, u32[]{:S(2)}, u32[]{:S(2)}) collective-permute-start(f32[17,3,8,128]{3,2,1,0:T(8,128)} %get-tuple-element.32), channel_id=1, source_target_pairs={{0,192},{64,0},{128,64},{192,128},{1,193},{65,1},{129,65},{193,129... | collective-permute-start | bytes 626696 | tf_op jit(solution)/shard_map/ppermute | solution.py:247
  39.7 2.7 %copy-start.2 = (f32[17,3,8,128]{3,2,1,0:T(8,128)}, f32[17,3,8,128]{3,2,1,0:T(8,128)S(1)}, u32[]{:S(2)}) copy-start(f32[17,3,8,128]{3,2,1,0:T(8,128)S(1)} %collective-permute-done.2.refs_1_.refs_5_) | copy-start | bytes 626692
  42.4 0.7 copy-start.3
  42.4 0.7 copy-start.4
  43.1 9.7 %copy-start.18 = (f32[16,3,8,128]{3,2,1,0:T(8,128)S(1)}, f32[16,3,8,128]{3,2,1,0:T(8,128)}, u32[]{:S(2)}) copy-start(f32[16,3,8,128]{3,2,1,0:T(8,128)} %get-tuple-element.40) | copy-start | bytes 589828
  43.1 11.0 %copy-start.17 = (f32[16,3,8,128]{3,2,1,0:T(8,128)S(1)}, f32[16,3,8,128]{3,2,1,0:T(8,128)}, u32[]{:S(2)}) copy-start(f32[16,3,8,128]{3,2,1,0:T(8,128)} %get-tuple-element.41) | copy-start | bytes 589828
  43.2 13.4 %copy-start.16 = (f32[16,3,8,128]{3,2,1,0:T(8,128)S(1)}, f32[16,3,8,128]{3,2,1,0:T(8,128)}, u32[]{:S(2)}) copy-start(f32[16,3,8,128]{3,2,1,0:T(8,128)} %get-tuple-element.42) | copy-start | bytes 589828
  49.2 28.3 %all-to-all-start.1 = ((f32[8,10,3,8,128]{4,3,2,1,0:T(8,128)}), f32[8,10,3,8,128]{4,3,2,1,0:T(8,128)S(1)}, u32[]{:S(2)}, u32[]{:S(2)}) async-start(f32[8,10,3,8,128]{4,3,2,1,0:T(8,128)} %get-tuple-element.34), calls=%async_computation.1 | async-start | bytes 1966080 | tf_op jit(solution)/shard_map/all_to_all | solution.py:283
  52.8 8.8 %collective-permute-start.8 = (f32[16,3,8,128]{3,2,1,0:T(8,128)S(1)}, f32[16,3,8,128]{3,2,1,0:T(8,128)S(1)}, u32[]{:S(2)}, u32[]{:S(2)}) collective-permute-start(f32[16,3,8,128]{3,2,1,0:T(8,128)S(1)} %copy-done.18), channel_id=1, source_target_pairs={{0,64},{64,128},{128,192},{192,0},{1,65},{65,129},{129,193},{193,1... | collective-permute-start | bytes 589832 | tf_op jit(solution)/shard_map/ppermute | solution.py:247
  54.2 9.6 %collective-permute-start.9 = (f32[16,3,8,128]{3,2,1,0:T(8,128)S(1)}, f32[16,3,8,128]{3,2,1,0:T(8,128)S(1)}, u32[]{:S(2)}, u32[]{:S(2)}) collective-permute-start(f32[16,3,8,128]{3,2,1,0:T(8,128)S(1)} %copy-done.17), channel_id=1, source_target_pairs={{0,128},{64,192},{128,0},{192,64},{1,129},{65,193},{129,1},{193,65... | collective-permute-start | bytes 589832 | tf_op jit(solution)/shard_map/ppermute | solution.py:247
  56.5 7.2 %collective-permute-start.10 = (f32[16,3,8,128]{3,2,1,0:T(8,128)S(1)}, f32[16,3,8,128]{3,2,1,0:T(8,128)S(1)}, u32[]{:S(2)}, u32[]{:S(2)}) collective-permute-start(f32[16,3,8,128]{3,2,1,0:T(8,128)S(1)} %copy-done.16), channel_id=1, source_target_pairs={{0,192},{64,0},{128,64},{192,128},{1,193},{65,1},{129,65},{193,129... | collective-permute-start | bytes 589832 | tf_op jit(solution)/shard_map/ppermute | solution.py:247
  61.6 2.1 %copy-start.7 = (f32[16,3,8,128]{3,2,1,0:T(8,128)}, f32[16,3,8,128]{3,2,1,0:T(8,128)S(1)}, u32[]{:S(2)}) copy-start(f32[16,3,8,128]{3,2,1,0:T(8,128)S(1)} %collective-permute-done.8.refs_5_) | copy-start | bytes 589828
  63.7 0.7 copy-start.8
  63.7 0.8 copy-start.9
  77.5 3.6 %copy-start = (f32[8,10,3,8,128]{4,3,2,1,0:T(8,128)}, f32[8,10,3,8,128]{4,3,2,1,0:T(8,128)S(1)}, u32[]{:S(2)}) copy-start(f32[8,10,3,8,128]{4,3,2,1,0:T(8,128)S(1)} %all-to-all-done.1.in_ref) | copy-start | bytes 2949124
  77.5 28.2 %all-to-all-start.2 = ((f32[8,10,3,8,128]{4,3,2,1,0:T(8,128)}), f32[8,10,3,8,128]{4,3,2,1,0:T(8,128)S(1)}, u32[]{:S(2)}, u32[]{:S(2)}) async-start(f32[8,10,3,8,128]{4,3,2,1,0:T(8,128)} %shard_map.41), calls=%async_computation.2 | async-start | bytes 1966080 | tf_op jit(solution)/shard_map/all_to_all | solution.py:285
  83.5 31.8 %collective-permute-start.5 = (f32[16,3,8,128]{3,2,1,0:T(8,128)}, f32[16,3,8,128]{3,2,1,0:T(8,128)S(1)}, u32[]{:S(2)}, u32[]{:S(2)}) collective-permute-start(f32[16,3,8,128]{3,2,1,0:T(8,128)} %get-tuple-element.36), channel_id=1, source_target_pairs={{0,64},{64,128},{128,192},{192,0},{1,65},{65,129},{129,193},{193,1... | collective-permute-start | bytes 589832 | tf_op jit(solution)/shard_map/ppermute | solution.py:247
  86.7 31.3 %collective-permute-start.6 = (f32[16,3,8,128]{3,2,1,0:T(8,128)}, f32[16,3,8,128]{3,2,1,0:T(8,128)S(1)}, u32[]{:S(2)}, u32[]{:S(2)}) collective-permute-start(f32[16,3,8,128]{3,2,1,0:T(8,128)} %get-tuple-element.37), channel_id=1, source_target_pairs={{0,128},{64,192},{128,0},{192,64},{1,129},{65,193},{129,1},{193,65... | collective-permute-start | bytes 589832 | tf_op jit(solution)/shard_map/ppermute | solution.py:247
  88.3 29.7 %collective-permute-start.7 = (f32[16,3,8,128]{3,2,1,0:T(8,128)}, f32[16,3,8,128]{3,2,1,0:T(8,128)S(1)}, u32[]{:S(2)}, u32[]{:S(2)}) collective-permute-start(f32[16,3,8,128]{3,2,1,0:T(8,128)} %get-tuple-element.38), channel_id=1, source_target_pairs={{0,192},{64,0},{128,64},{192,128},{1,193},{65,1},{129,65},{193,129... | collective-permute-start | bytes 589832 | tf_op jit(solution)/shard_map/ppermute | solution.py:247
  105.7 0.9 copy-start.1
  109.0 10.9 %collective-permute-start.11 = (f32[16,3,8,128]{3,2,1,0:T(8,128)}, f32[16,3,8,128]{3,2,1,0:T(8,128)S(1)}, u32[]{:S(2)}, u32[]{:S(2)}) collective-permute-start(f32[16,3,8,128]{3,2,1,0:T(8,128)} %get-tuple-element.44), channel_id=1, source_target_pairs={{0,64},{64,128},{128,192},{192,0},{1,65},{65,129},{129,193},{193,1... | collective-permute-start | bytes 589832 | tf_op jit(solution)/shard_map/ppermute | solution.py:247
  115.3 8.0 %collective-permute-start.12 = (f32[16,3,8,128]{3,2,1,0:T(8,128)}, f32[16,3,8,128]{3,2,1,0:T(8,128)S(1)}, u32[]{:S(2)}, u32[]{:S(2)}) collective-permute-start(f32[16,3,8,128]{3,2,1,0:T(8,128)} %get-tuple-element.45), channel_id=1, source_target_pairs={{0,128},{64,192},{128,0},{192,64},{1,129},{65,193},{129,1},{193,65... | collective-permute-start | bytes 589832 | tf_op jit(solution)/shard_map/ppermute | solution.py:247
  115.3 8.0 %copy-start.10 = (f32[16,3,8,128]{3,2,1,0:T(8,128)}, f32[16,3,8,128]{3,2,1,0:T(8,128)S(1)}, u32[]{:S(2)}) copy-start(f32[16,3,8,128]{3,2,1,0:T(8,128)S(1)} %collective-permute-done.5.refs_1_) | copy-start | bytes 589828
  115.3 8.0 %collective-permute-start.13 = (f32[16,3,8,128]{3,2,1,0:T(8,128)}, f32[16,3,8,128]{3,2,1,0:T(8,128)S(1)}, u32[]{:S(2)}, u32[]{:S(2)}) collective-permute-start(f32[16,3,8,128]{3,2,1,0:T(8,128)} %get-tuple-element.46), channel_id=1, source_target_pairs={{0,192},{64,0},{128,64},{192,128},{1,193},{65,1},{129,65},{193,129... | collective-permute-start | bytes 589832 | tf_op jit(solution)/shard_map/ppermute | solution.py:247
  118.0 5.3 %copy-start.11 = (f32[16,3,8,128]{3,2,1,0:T(8,128)}, f32[16,3,8,128]{3,2,1,0:T(8,128)S(1)}, u32[]{:S(2)}) copy-start(f32[16,3,8,128]{3,2,1,0:T(8,128)S(1)} %collective-permute-done.6.refs_2_) | copy-start | bytes 589828
  118.0 5.3 %copy-start.12 = (f32[16,3,8,128]{3,2,1,0:T(8,128)}, f32[16,3,8,128]{3,2,1,0:T(8,128)S(1)}, u32[]{:S(2)}) copy-start(f32[16,3,8,128]{3,2,1,0:T(8,128)S(1)} %collective-permute-done.7.refs_3_) | copy-start | bytes 589828
  120.0 3.4 %copy-start.13 = (f32[16,3,8,128]{3,2,1,0:T(8,128)}, f32[16,3,8,128]{3,2,1,0:T(8,128)S(1)}, u32[]{:S(2)}) copy-start(f32[16,3,8,128]{3,2,1,0:T(8,128)S(1)} %collective-permute-done.11.refs_5_) | copy-start | bytes 589828
  123.3 0.7 copy-start.14
  123.3 0.8 copy-start.15

commit v3 on v2

v3 whole, which is shorter than its diff:
```python
import functools

import jax
import jax.numpy as jnp
from jax import lax
from jax.experimental import pallas as pl
from jax.experimental.pallas import tpu as pltpu
from jax.sharding import Mesh, PartitionSpec as P

F32 = jnp.float32
XS, ZS = 4, 8
LANES = 128
BOXES = 10
VMEM = pl.BlockSpec(memory_space=pltpu.VMEM)
SMEM = pl.BlockSpec(memory_space=pltpu.SMEM)
PARAMS = pltpu.CompilerParams(vmem_limit_bytes=12 * 1024 * 1024)


def one_step(h, m, n, slope_x, slope_y):
    rows, cols = h.shape
    inv = 1.0 / h
    u = m * inv
    press = 0.0625 * (h * h)
    fx = 0.125 * (m * u) + press
    cross = 0.125 * (u * n)
    gy = 0.125 * (n * (n * inv)) + press

    def combine(q, f, g):
        q = 0.25 * q
        return (
            pltpu.roll(q - f, cols - 1, 1)
            + pltpu.roll(q + f, 1, 1)
            + pltpu.roll(q - g, rows - 1, 0)
            + pltpu.roll(q + g, 1, 0)
        )

    return (
        combine(h, 0.125 * m, 0.125 * n),
        combine(m, fx, cross) + h * slope_x,
        combine(n, cross, gy) + h * slope_y,
    )


def edge_kernel(x_ref, bed_ref, low_ref, high_ref):
    count, fields, rows, _ = x_ref.shape
    for p in range(count):
        for f in range(fields):
            low_ref[p * fields + f] = x_ref[p, f, rows - 2 : rows]
            high_ref[p * fields + f] = x_ref[p, f, 0:2]
    low_ref[count * fields] = bed_ref[rows - 2 : rows]
    high_ref[count * fields] = bed_ref[0:2]


def evolve_kernel(place_ref, counts_ref, x_ref, low_ref, high_ref, bed_ref, *refs):
    upper, lower = refs[0:XS], refs[XS : 2 * XS]
    row_ref, ext, sx, sy, res = refs[2 * XS :]
    count, fields, rows, cols = x_ref.shape
    ext[...] = jnp.ones_like(ext)
    ext[0, 0:rows] = bed_ref[...]
    ext[0, rows : rows + 2] = high_ref[count * fields]
    ext[0, rows + 6 : rows + 8] = low_ref[count * fields]
    b = ext[0]
    sx[...] = -0.125 * (pltpu.roll(b, cols - 1, 1) - pltpu.roll(b, 1, 1))
    sy[...] = -0.125 * (pltpu.roll(b, rows + 7, 0) - pltpu.roll(b, 1, 0))
    x = place_ref[0]

    def body(p, carry):
        for f in range(fields):
            ext[f, 0:rows] = x_ref[p, f]
            ext[f, rows : rows + 2] = high_ref[p * fields + f]
            ext[f, rows + 6 : rows + 8] = low_ref[p * fields + f]
        slope_x = sx[...]
        slope_y = sy[...]
        state = (ext[0], ext[1], ext[2])
        for _ in range(2):
            state = one_step(*state, slope_x, slope_y)
        for f in range(fields):
            res[f] = state[f][0:rows]
        for k in range(XS):
            at = pl.multiple_of(((x + k) % XS) * LANES, LANES)
            for f in range(fields):
                upper[k][p, f] = res[f, 0:8, pl.ds(at, LANES)]
                lower[k][p, f] = res[f, 8:16, pl.ds(at, LANES)]
        return carry

    lax.fori_loop(0, count, body, 0)
    lane = lax.broadcasted_iota(jnp.int32, (1, LANES), 1)
    total = jnp.int32(0)
    tile = jnp.zeros((1, LANES), jnp.int32)
    for j in range(count):
        c = counts_ref[j]
        total = total + c
        tile = jnp.where(lane == j, c, tile)
    tile = jnp.where(lane == count, total, tile)
    for g in range(XS * ZS):
        row_ref[g] = tile


def plan_kernel(place_ref, row_ref, put_ref, take_ref, base, ctr):
    x, z = place_ref[0], place_ref[1]
    total = jnp.int32(0)
    for g in range(XS * ZS):
        base[g] = total
        total = total + row_ref[g, 0, 16]
    base[XS * ZS] = total
    for i in range(ZS):
        ctr[i] = 0

    def reserve(slot):
        to = slot & (ZS - 1)
        t = ctr[to]
        ctr[to] = t + 1
        return to * 16 + t

    for k in range(XS):
        group = ((x + XS - k) % XS) * ZS + z
        e = base[group]
        for j in range(16):
            c = row_ref[group, 0, j]
            at = 2 * (k * 16 + j)
            put_ref[at] = -1
            put_ref[at + 1] = -1

            @pl.when(c > 0)
            def _():
                put_ref[at] = reserve(e)

            @pl.when(c > 1)
            def _():
                put_ref[at + 1] = reserve(e + 1)

            e = e + c
    spare = jnp.int32(0)
    for i in range(ZS):
        spare = jnp.where(ctr[i] < BOXES, i * 16 + BOXES - 1, spare)
    for i in range(32 * XS):
        code = put_ref[i]
        put_ref[i] = jnp.where(code < 0, spare, code)

    for i in range(ZS):
        ctr[i] = 0
    for i in range(16 * XS):
        take_ref[i] = 0
    for k in range(XS):
        for zs in range(ZS):
            group = ((x + XS - k) % XS) * ZS + zs
            lo = base[group]
            hi = base[group + 1]
            first = lo + ((z - lo) & (ZS - 1))
            t0 = ctr[zs]
            for i in range(4):
                s = first + i * ZS

                @pl.when(s < hi)
                def _():
                    take_ref[s >> 3] = zs * 16 + t0 + i
                    ctr[zs] = t0 + i + 1


def plan(place, row):
    return pl.pallas_call(
        plan_kernel,
        in_specs=[SMEM, SMEM],
        out_specs=[SMEM, SMEM],
        out_shape=[
            jax.ShapeDtypeStruct((32 * XS,), jnp.int32),
            jax.ShapeDtypeStruct((16 * XS,), jnp.int32),
        ],
        scratch_shapes=[
            pltpu.SMEM((XS * ZS + 1,), jnp.int32),
            pltpu.SMEM((ZS,), jnp.int32),
        ],
        compiler_params=PARAMS,
    )(place, row)


def pack_kernel(put_ref, *refs):
    data, out_ref = refs[0:XS], refs[XS]
    for k in range(XS):
        for j in range(16):
            item = data[k][j]
            for i in range(2):
                code = put_ref[2 * (k * 16 + j) + i]
                out_ref[code >> 4, code & 15] = item


def pack(put, data):
    return pl.pallas_call(
        pack_kernel,
        in_specs=[SMEM] + [VMEM] * XS,
        out_specs=VMEM,
        out_shape=jax.ShapeDtypeStruct((ZS, BOXES, 3, 8, LANES), F32),
        compiler_params=PARAMS,
        cost_estimate=pl.CostEstimate(flops=0, bytes_accessed=3_000_000, transcendentals=0),
    )(put, *data)


def spread_kernel(place_ref, table_ref, in_ref, *outs):
    x = place_ref[0]
    for k in range(XS):
        to = (x + k) % XS
        out = outs[k]

        def body(i, carry):
            code = table_ref[i * XS + to]
            out[i] = in_ref[code >> 4, code & 15]
            return carry

        lax.fori_loop(0, 16, body, 0, unroll=4)


def spread(place, table, boxes):
    return pl.pallas_call(
        spread_kernel,
        in_specs=[SMEM, SMEM, VMEM],
        out_specs=[VMEM] * XS,
        out_shape=[jax.ShapeDtypeStruct((16, 3, 8, LANES), F32)] * XS,
        compiler_params=PARAMS,
        cost_estimate=pl.CostEstimate(flops=0, bytes_accessed=4_000_000, transcendentals=0),
    )(place, table, boxes)


def join_kernel(place_ref, *refs):
    parts, out_ref = refs[: 2 * XS], refs[2 * XS]
    x = place_ref[0]
    for k in range(XS):
        at = pl.multiple_of(((x + XS - k) % XS) * LANES, LANES)

        def body(i, carry):
            for f in range(3):
                out_ref[i, f, 0:8, pl.ds(at, LANES)] = parts[k][i, f]
                out_ref[i, f, 8:16, pl.ds(at, LANES)] = parts[XS + k][i, f]
            return carry

        lax.fori_loop(0, 16, body, 0, unroll=4)


def along_x(parts):
    return [parts[0]] + [
        lax.ppermute(parts[k], "x", [(i, (i + k) % XS) for i in range(XS)]) for k in range(1, XS)
    ]


def per_device(particles, counts, bed):
    count, fields, rows, cols = particles.shape
    place = jnp.stack([lax.axis_index("x"), lax.axis_index("z")]).astype(jnp.int32)
    edges = jax.ShapeDtypeStruct((count * fields + 1, 2, cols), F32)
    low, high = pl.pallas_call(
        edge_kernel,
        in_specs=[VMEM, VMEM],
        out_specs=[VMEM] * 2,
        out_shape=[edges, edges],
        compiler_params=PARAMS,
    )(particles, bed)
    strips = lax.axis_size("space")
    low = lax.ppermute(low, "space", [(i, (i + 1) % strips) for i in range(strips)])
    high = lax.ppermute(high, "space", [((i + 1) % strips, i) for i in range(strips)])
    half = jax.ShapeDtypeStruct((count, fields, 8, LANES), F32)
    *parts, row = pl.pallas_call(
        evolve_kernel,
        in_specs=[SMEM, SMEM] + [VMEM] * 4,
        out_specs=[VMEM] * (2 * XS + 1),
        out_shape=[half] * (2 * XS) + [jax.ShapeDtypeStruct((XS * ZS, 1, LANES), jnp.int32)],
        scratch_shapes=[
            pltpu.VMEM((fields, rows + 8, cols), F32),
            pltpu.VMEM((rows + 8, cols), F32),
            pltpu.VMEM((rows + 8, cols), F32),
            pltpu.VMEM((fields, rows, cols), F32),
        ],
        compiler_params=PARAMS,
        cost_estimate=pl.CostEstimate(flops=0, bytes_accessed=20_000_000, transcendentals=0),
    )(place, counts, particles, low, high, bed)
    upper = along_x(parts[:XS])
    row = lax.all_to_all(row, ("x", "z"), 0, 0, tiled=True)
    lower = along_x(parts[XS:])
    put, take = plan(place, row)
    boxes_a = lax.all_to_all(pack(put, upper), "z", 0, 0, tiled=True)
    boxes_b = lax.all_to_all(pack(put, lower), "z", 0, 0, tiled=True)
    out_a = along_x(spread(place, take, boxes_a))
    out_b = along_x(spread(place, take, boxes_b))
    return pl.pallas_call(
        join_kernel,
        in_specs=[SMEM] + [VMEM] * (2 * XS),
        out_specs=VMEM,
        out_shape=jax.ShapeDtypeStruct(particles.shape, F32),
        compiler_params=PARAMS,
    )(place, *out_a, *out_b)


def solution(mesh):
    wide = Mesh(mesh.devices.reshape(XS, ZS, -1), ("x", "z", "space"))
    in_specs = (P(("x", "z"), None, "space", None), P(("x", "z")), P("space", None))
    out_specs = P(("x", "z"), None, "space", None)
    return jax.shard_map(
        per_device, mesh=wide, in_specs=in_specs, out_specs=out_specs, check_vma=False
    )
```

time: 129 us -> 117 us (0.907); the launches traced: 127 us -> 117 us
  Pallas kernels: 28.6 us -> 15.2 us
  waiting for transfers between devices: 41.9 us -> 54.3 us
  starting transfers between devices: 34.5 us -> 26.4 us
  local copies, waits for them, and re-layouts: 4.56 us -> 2.18 us
  blocking collectives: 16.6 us -> 18.5 us
    all_to_all x2, waiting for transfers between devices: 24.3 us -> 35.9 us  [the longest x1 22.9 us: per_device(): boxes_b = lax.all_to_all(pack(put, lower), 'z', 0, 0, tiled=True)]
    pallas_call x4 -> x5, Pallas kernels: 21 us -> 11.7 us  [the longest x1 5.46 us: per_device(): pl.pallas_call(evolve_kernel, in_specs=[SMEM, SMEM] + [VMEM] * 4, out_spe...]
    ppermute x12, starting transfers between devices: 25.6 us -> 17.5 us  [along_x(): lax.ppermute(parts[k], 'x', [(i, (i + k) % XS) for i in range(XS)])]
    ppermute x1, waiting for transfers between devices: 0.01 us -> 3.32 us  [per_device(): lax.ppermute(low, 'space', [(i, (i + 1) % strips) for i in range(strips)])]
    pallas_call x2, Pallas kernels: 4.72 us -> 1.6 us  [spread(): pl.pallas_call(spread_kernel, in_specs=[SMEM, SMEM, VMEM], out_specs=[VME...]
    ppermute x12, waiting for transfers between devices: 17.5 us -> 15 us  [along_x(): lax.ppermute(parts[k], 'x', [(i, (i + k) % XS) for i in range(XS)])]
    unnamed x38 -> x10, local copies, waits for them, and re-layouts: 4.56 us -> 2.18 us
    all_to_all x1, blocking collectives: 16.6 us -> 18.5 us  [per_device(): row = lax.all_to_all(row, ('x', 'z'), 0, 0, tiled=True)]
  transfers between devices with their start and end apart: 16 -> 16, of which waited for: 8 -> 7; matrix products, arithmetic and copies ran while one was open for 0% -> 0% of each run, Pallas kernels for 8% -> 5%
where the time goes in v3:
time: 117 us
  waiting for transfers between devices  54.3 us (46%)
  starting transfers between devices  26.4 us (23%)
  blocking collectives  18.5 us (16%)
  Pallas kernels  15.2 us (13%)
  local copies, waits for them, and re-layouts  2.18 us (2%)
    all_to_all x1, waiting for transfers between devices, per_device(): boxes_b = lax.all_to_all(pack(put, lower), 'z', 0, 0, tiled=True)  22.9 us
    all_to_all x1, blocking collectives, per_device(): row = lax.all_to_all(row, ('x', 'z'), 0, 0, tiled=True)  18.5 us
    ppermute x12, starting transfers between devices, along_x(): lax.ppermute(parts[k], 'x', [(i, (i + k) % XS) for i in range(XS)])  17.5 us
    ppermute x12, waiting for transfers between devices, along_x(): lax.ppermute(parts[k], 'x', [(i, (i + k) % XS) for i in range(XS)])  15 us
    all_to_all x1, waiting for transfers between devices, per_device(): boxes_a = lax.all_to_all(pack(put, upper), 'z', 0, 0, tiled=True)  13 us
    pallas_call x1, Pallas kernels, per_device(): pl.pallas_call(evolve_kernel, in_specs=[SMEM, SMEM] + [VMEM] * 4, out_spe...  5.46 us
    all_to_all x1, starting transfers between devices, per_device(): boxes_a = lax.all_to_all(pack(put, upper), 'z', 0, 0, tiled=True)  3.56 us
    all_to_all x1, starting transfers between devices, per_device(): boxes_b = lax.all_to_all(pack(put, lower), 'z', 0, 0, tiled=True)  3.56 us
  transfers between devices with their start and end apart: 16, of which 7 were waited for; matrix products, arithmetic and copies ran while one was open for 0% of the time, Pallas kernels for 5%

profile of v3, /device:TPU:16, one launch (start us, length us, event | category | flops | bytes accessed | tf_op | source)
XLA Modules:
  0.0 116.7 jit_solution(2631339323738058534)
XLA Ops:
  0.0 0.0 copy-start
  0.0 1.4 %copy-done = f32[16,3,16,512]{3,2,1,0:T(8,128)S(1)} copy-done((f32[16,3,16,512]{3,2,1,0:T(8,128)S(1)}, f32[16,3,16,512]{3,2,1,0:T(8,128)}, u32[]{:S(2)}) %copy-start) | copy-done | bytes 1572888
  1.4 0.0 copy-start.2
  1.4 0.8 copy-done.2
  2.2 0.0 copy-start.1
  2.2 0.0 copy-start.3
  2.2 0.0 copy-start.4
  2.2 0.1 shard_map.37
  2.3 0.0 collective-permute-start
  2.3 1.7 %collective-permute-start.1 = (f32[49,2,512]{2,1,0:T(2,128)S(1)}, f32[49,2,512]{2,1,0:T(2,128)S(1)}, u32[]{:S(2)}, u32[]{:S(2)}) collective-permute-start(f32[49,2,512]{2,1,0:T(2,128)S(1)} %get-tuple-element.27), channel_id=1, source_target_pairs={{1,0},{2,1},{3,2},{4,3},{5,4},{6,5},{7,6},{0,7},{9,8},{10,9},{11,1... | collective-permute-start | bytes 602120 | tf_op jit(solution)/shard_map/ppermute | solution.py:257
  4.0 0.1 pad_add_fusion.place_ref
  4.1 3.3 %collective-permute-done.low_ref = f32[49,2,512]{2,1,0:T(2,128)S(1)} collective-permute-done((f32[49,2,512]{2,1,0:T(2,128)S(1)}, f32[49,2,512]{2,1,0:T(2,128)S(1)}, u32[]{:S(2)}, u32[]{:S(2)}) %collective-permute-start) | collective-permute-done | bytes 200736 | tf_op jit(solution)/shard_map/ppermute | solution.py:256
  7.4 0.0 collective-permute-done.1.high_ref
  7.4 0.0 copy-done.1
  7.4 0.0 copy-done.3
  7.4 0.0 copy-done.4
  7.4 5.5 %shard_map.38 = (f32[16,3,8,128]{3,2,1,0:T(8,128)S(1)}, f32[16,3,8,128]{3,2,1,0:T(8,128)S(1)}, f32[16,3,8,128]{3,2,1,0:T(8,128)S(1)}, f32[16,3,8,128]{3,2,1,0:T(...) custom-call(s32[2]{0:T(128)S(1)} %pad_add_fusion.place_ref, ...), custom_call_target="tpu_custom_call" | custom-call | bytes 20000000 | tf_op jit(solution)/shard_map/pallas_call | solution.py:259
  12.9 1.5 %collective-permute-start.2 = (f32[16,3,8,128]{3,2,1,0:T(8,128)S(1)}, f32[16,3,8,128]{3,2,1,0:T(8,128)S(1)}, u32[]{:S(2)}, u32[]{:S(2)}) collective-permute-start(f32[16,3,8,128]{3,2,1,0:T(8,128)S(1)} %get-tuple-element.32), channel_id=1, source_target_pairs={{0,64},{64,128},{128,192},{192,0},{1,65},{65,129},{129,193},{193,1... | collective-permute-start | bytes 589832 | tf_op jit(solution)/shard_map/ppermute | solution.py:240
  14.4 2.8 %collective-permute-start.3 = (f32[16,3,8,128]{3,2,1,0:T(8,128)S(1)}, f32[16,3,8,128]{3,2,1,0:T(8,128)S(1)}, u32[]{:S(2)}, u32[]{:S(2)}) collective-permute-start(f32[16,3,8,128]{3,2,1,0:T(8,128)S(1)} %get-tuple-element.33), channel_id=1, source_target_pairs={{0,128},{64,192},{128,0},{192,64},{1,129},{65,193},{129,1},{193,65... | collective-permute-start | bytes 589832 | tf_op jit(solution)/shard_map/ppermute | solution.py:240
  17.2 1.4 %collective-permute-start.4 = (f32[16,3,8,128]{3,2,1,0:T(8,128)S(1)}, f32[16,3,8,128]{3,2,1,0:T(8,128)S(1)}, u32[]{:S(2)}, u32[]{:S(2)}) collective-permute-start(f32[16,3,8,128]{3,2,1,0:T(8,128)S(1)} %get-tuple-element.34), channel_id=1, source_target_pairs={{0,192},{64,0},{128,64},{192,128},{1,193},{65,1},{129,65},{193,129... | collective-permute-start | bytes 589832 | tf_op jit(solution)/shard_map/ppermute | solution.py:240
  18.6 18.5 %all_to_all.15.row_ref = s32[32,1,128]{2,1,0:T(1,128)S(1)} all-to-all(s32[32,1,128]{2,1,0:T(1,128)S(1)} %get-tuple-element.28), channel_id=1, replica_groups=mesh['x'=4,'z'=8,'space'=8] {'x','z'}, dimensions={0} | all-to-all | bytes 32768 | tf_op jit(solution)/shard_map/all_to_all | solution.py:274
  37.1 2.6 %shard_map.39 = (s32[128]{0:T(128)S(1)}, s32[64]{0:T(128)S(1)}) custom-call(s32[2]{0:T(128)S(1)} %pad_add_fusion.place_ref, s32[32,1,128]{2,1,0:T(1,128)S(1)} %all_to_all.15.row_ref), custom_call_target="tpu_custom_call" | custom-call | tf_op jit(solution)/shard_map/pallas_call | solution.py:161
  39.7 0.0 collective-permute-done.2.refs_1_
  39.8 0.0 collective-permute-done.3.refs_2_
  39.8 0.0 collective-permute-done.4.refs_3_
  39.8 1.7 %shard_map.40 = f32[8,10,3,8,128]{4,3,2,1,0:T(8,128)} custom-call(s32[128]{0:T(128)S(1)} %get-tuple-element.30.put_ref, f32[16,3,8,128]{3,2,1,0:T(8,128)S(1)} %get-tuple-element.31.refs_0_, f32[16,3,8,128]{3,2,1,0:T(8,128)S(1)} %collective-permute-done.2.refs_1_, f32[16,3,8,128]{3,2,1,0:T(8,128)S(1)} %collective-permute-done.3.refs_2_, ...), custom_call_target="tpu_custom_call" | custom-call | bytes 3000000 | tf_op jit(solution)/shard_map/pallas_call | solution.py:188
  41.5 3.6 %all-to-all-start.1 = ((f32[8,10,3,8,128]{4,3,2,1,0:T(8,128)}), f32[8,10,3,8,128]{4,3,2,1,0:T(8,128)S(1)}, u32[]{:S(2)}, u32[]{:S(2)}) async-start(f32[8,10,3,8,128]{4,3,2,1,0:T(8,128)} %shard_map.40), calls=%async_computation.1 | async-start | bytes 1966080 | tf_op jit(solution)/shard_map/all_to_all | solution.py:277
  45.1 0.7 collective-permute-start.8
  45.8 2.0 %collective-permute-start.9 = (f32[16,3,8,128]{3,2,1,0:T(8,128)S(1)}, f32[16,3,8,128]{3,2,1,0:T(8,128)S(1)}, u32[]{:S(2)}, u32[]{:S(2)}) collective-permute-start(f32[16,3,8,128]{3,2,1,0:T(8,128)S(1)} %get-tuple-element.41), channel_id=1, source_target_pairs={{0,128},{64,192},{128,0},{192,64},{1,129},{65,193},{129,1},{193,65... | collective-permute-start | bytes 589832 | tf_op jit(solution)/shard_map/ppermute | solution.py:240
  47.8 1.2 %collective-permute-start.10 = (f32[16,3,8,128]{3,2,1,0:T(8,128)S(1)}, f32[16,3,8,128]{3,2,1,0:T(8,128)S(1)}, u32[]{:S(2)}, u32[]{:S(2)}) collective-permute-start(f32[16,3,8,128]{3,2,1,0:T(8,128)S(1)} %get-tuple-element.42), channel_id=1, source_target_pairs={{0,192},{64,0},{128,64},{192,128},{1,193},{65,1},{129,65},{193,129... | collective-permute-start | bytes 589832 | tf_op jit(solution)/shard_map/ppermute | solution.py:240
  49.0 7.5 %collective-permute-done.8.refs_1_ = f32[16,3,8,128]{3,2,1,0:T(8,128)S(1)} collective-permute-done((f32[16,3,8,128]{3,2,1,0:T(8,128)S(1)}, f32[16,3,8,128]{3,2,1,0:T(8,128)S(1)}, u32[]{:S(2)}, u32[]{:S(2)}) %collective-permute-start.8) | collective-permute-done | bytes 196640 | tf_op jit(solution)/shard_map/ppermute | solution.py:240
  56.5 0.0 collective-permute-done.9.refs_2_
  56.5 0.6 collective-permute-done.10.refs_3_
  57.1 1.8 %shard_map.42 = f32[8,10,3,8,128]{4,3,2,1,0:T(8,128)} custom-call(s32[128]{0:T(128)S(1)} %get-tuple-element.30.put_ref, f32[16,3,8,128]{3,2,1,0:T(8,128)S(1)} %get-tuple-element.39.refs_0_, f32[16,3,8,128]{3,2,1,0:T(8,128)S(1)} %collective-permute-done.8.refs_1_, f32[16,3,8,128]{3,2,1,0:T(8,128)S(1)} %collective-permute-done.9.refs_2_, ...), custom_call_target="tpu_custom_call" | custom-call | bytes 3000000 | tf_op jit(solution)/shard_map/pallas_call | solution.py:188
  58.9 13.0 %all-to-all-done.1.in_ref = f32[8,10,3,8,128]{4,3,2,1,0:T(8,128)S(1)} async-done(((f32[8,10,3,8,128]{4,3,2,1,0:T(8,128)}), f32[8,10,3,8,128]{4,3,2,1,0:T(8,128)S(1)}, u32[]{:S(2)}, u32[]{:S(2)}) %all-to-all-start.1) | async-done | bytes 983072 | tf_op jit(solution)/shard_map/all_to_all | solution.py:277
  71.9 3.6 %all-to-all-start.2 = ((f32[8,10,3,8,128]{4,3,2,1,0:T(8,128)}), f32[8,10,3,8,128]{4,3,2,1,0:T(8,128)S(1)}, u32[]{:S(2)}, u32[]{:S(2)}) async-start(f32[8,10,3,8,128]{4,3,2,1,0:T(8,128)} %shard_map.42), calls=%async_computation.2 | async-start | bytes 1966080 | tf_op jit(solution)/shard_map/all_to_all | solution.py:278
  75.4 0.8 shard_map.41
  76.2 0.7 collective-permute-start.5
  76.9 2.0 %collective-permute-start.6 = (f32[16,3,8,128]{3,2,1,0:T(8,128)S(1)}, f32[16,3,8,128]{3,2,1,0:T(8,128)S(1)}, u32[]{:S(2)}, u32[]{:S(2)}) collective-permute-start(f32[16,3,8,128]{3,2,1,0:T(8,128)S(1)} %get-tuple-element.37), channel_id=1, source_target_pairs={{0,128},{64,192},{128,0},{192,64},{1,129},{65,193},{129,1},{193,65... | collective-permute-start | bytes 589832 | tf_op jit(solution)/shard_map/ppermute | solution.py:240
  78.9 1.2 %collective-permute-start.7 = (f32[16,3,8,128]{3,2,1,0:T(8,128)S(1)}, f32[16,3,8,128]{3,2,1,0:T(8,128)S(1)}, u32[]{:S(2)}, u32[]{:S(2)}) collective-permute-start(f32[16,3,8,128]{3,2,1,0:T(8,128)S(1)} %get-tuple-element.38), channel_id=1, source_target_pairs={{0,192},{64,0},{128,64},{192,128},{1,193},{65,1},{129,65},{193,129... | collective-permute-start | bytes 589832 | tf_op jit(solution)/shard_map/ppermute | solution.py:240
  80.2 22.9 %all-to-all-done.2.in_ref = f32[8,10,3,8,128]{4,3,2,1,0:T(8,128)S(1)} async-done(((f32[8,10,3,8,128]{4,3,2,1,0:T(8,128)}), f32[8,10,3,8,128]{4,3,2,1,0:T(8,128)S(1)}, u32[]{:S(2)}, u32[]{:S(2)}) %all-to-all-start.2) | async-done | bytes 983072 | tf_op jit(solution)/shard_map/all_to_all | solution.py:278
  103.1 0.8 shard_map.43
  103.9 0.7 collective-permute-start.11
  104.6 2.0 %collective-permute-start.12 = (f32[16,3,8,128]{3,2,1,0:T(8,128)S(1)}, f32[16,3,8,128]{3,2,1,0:T(8,128)S(1)}, u32[]{:S(2)}, u32[]{:S(2)}) collective-permute-start(f32[16,3,8,128]{3,2,1,0:T(8,128)S(1)} %get-tuple-element.45), channel_id=1, source_target_pairs={{0,128},{64,192},{128,0},{192,64},{1,129},{65,193},{129,1},{193,65... | collective-permute-start | bytes 589832 | tf_op jit(solution)/shard_map/ppermute | solution.py:240
  106.6 0.0 collective-permute-done.5.refs_1_
  106.6 1.2 %collective-permute-start.13 = (f32[16,3,8,128]{3,2,1,0:T(8,128)S(1)}, f32[16,3,8,128]{3,2,1,0:T(8,128)S(1)}, u32[]{:S(2)}, u32[]{:S(2)}) collective-permute-start(f32[16,3,8,128]{3,2,1,0:T(8,128)S(1)} %get-tuple-element.46), channel_id=1, source_target_pairs={{0,192},{64,0},{128,64},{192,128},{1,193},{65,1},{129,65},{193,129... | collective-permute-start | bytes 589832 | tf_op jit(solution)/shard_map/ppermute | solution.py:240
  107.9 0.0 collective-permute-done.6.refs_2_
  107.9 0.0 collective-permute-done.7.refs_3_
  107.9 6.2 %collective-permute-done.11.refs_5_ = f32[16,3,8,128]{3,2,1,0:T(8,128)S(1)} collective-permute-done((f32[16,3,8,128]{3,2,1,0:T(8,128)S(1)}, f32[16,3,8,128]{3,2,1,0:T(8,128)S(1)}, u32[]{:S(2)}, u32[]{:S(2)}) %collective-permute-start.11) | collective-permute-done | bytes 196640 | tf_op jit(solution)/shard_map/ppermute | solution.py:240
  114.1 0.0 collective-permute-done.12.refs_6_
  114.1 0.7 collective-permute-done.13.refs_7_
  114.8 1.9 %shard_map.44 = f32[16,3,16,512]{3,2,1,0:T(8,128)} custom-call(s32[2]{0:T(128)S(1)} %pad_add_fusion.place_ref, f32[16,3,8,128]{3,2,1,0:T(8,128)S(1)} %get-tuple-element.35.refs_0_, f32[16,3,8,128]{3,2,1,0:T(8,128)S(1)} %collective-permute-done.5.refs_1_, f32[16,3,8,128]{3,2,1,0:T(8,128)S(1)} %collective-permute-done.6.refs_2_, ...), custom_call_target="tpu_custom_call" | custom-call | tf_op jit(solution)/shard_map/pallas_call | solution.py:281
Async XLA Ops:
  0.0 1.4 %copy-start = (f32[16,3,16,512]{3,2,1,0:T(8,128)S(1)}, f32[16,3,16,512]{3,2,1,0:T(8,128)}, u32[]{:S(2)}) copy-start(f32[16,3,16,512]{3,2,1,0:T(8,128)} %x_ref.3) | copy-start | bytes 4718596
  1.4 0.8 copy-start.2
  2.2 5.2 %copy-start.1 = (f32[16,3,16,512]{3,2,1,0:T(8,128)S(1)}, f32[16,3,16,512]{3,2,1,0:T(8,128)}, u32[]{:S(2)}) copy-start(f32[16,3,16,512]{3,2,1,0:T(8,128)} %x_ref.3) | copy-start | bytes 4718596
  2.2 5.2 %copy-start.3 = (f32[16,512]{1,0:T(8,128)S(1)}, f32[16,512]{1,0:T(8,128)}, u32[]{:S(2)}) copy-start(f32[16,512]{1,0:T(8,128)} %bed_ref.3) | copy-start | bytes 98308
  2.2 5.2 %copy-start.4 = (s32[16]{0:T(128)S(1)}, s32[16]{0:T(128)}, u32[]{:S(2)}) copy-start(s32[16]{0:T(128)} %counts_ref.1) | copy-start | bytes 196
  2.3 5.2 %collective-permute-start = (f32[49,2,512]{2,1,0:T(2,128)S(1)}, f32[49,2,512]{2,1,0:T(2,128)S(1)}, u32[]{:S(2)}, u32[]{:S(2)}) collective-permute-start(f32[49,2,512]{2,1,0:T(2,128)S(1)} %get-tuple-element.26), channel_id=1, source_target_pairs={{0,1},{1,2},{2,3},{3,4},{4,5},{5,6},{6,7},{7,0},{8,9},{9,10},{10,1... | collective-permute-start | bytes 602120 | tf_op jit(solution)/shard_map/ppermute | solution.py:256
  2.3 5.1 %collective-permute-start.1 = (f32[49,2,512]{2,1,0:T(2,128)S(1)}, f32[49,2,512]{2,1,0:T(2,128)S(1)}, u32[]{:S(2)}, u32[]{:S(2)}) collective-permute-start(f32[49,2,512]{2,1,0:T(2,128)S(1)} %get-tuple-element.27), channel_id=1, source_target_pairs={{1,0},{2,1},{3,2},{4,3},{5,4},{6,5},{7,6},{0,7},{9,8},{10,9},{11,1... | collective-permute-start | bytes 602120 | tf_op jit(solution)/shard_map/ppermute | solution.py:257
  12.9 26.9 %collective-permute-start.2 = (f32[16,3,8,128]{3,2,1,0:T(8,128)S(1)}, f32[16,3,8,128]{3,2,1,0:T(8,128)S(1)}, u32[]{:S(2)}, u32[]{:S(2)}) collective-permute-start(f32[16,3,8,128]{3,2,1,0:T(8,128)S(1)} %get-tuple-element.32), channel_id=1, source_target_pairs={{0,64},{64,128},{128,192},{192,0},{1,65},{65,129},{129,193},{193,1... | collective-permute-start | bytes 589832 | tf_op jit(solution)/shard_map/ppermute | solution.py:240
  14.4 25.4 %collective-permute-start.3 = (f32[16,3,8,128]{3,2,1,0:T(8,128)S(1)}, f32[16,3,8,128]{3,2,1,0:T(8,128)S(1)}, u32[]{:S(2)}, u32[]{:S(2)}) collective-permute-start(f32[16,3,8,128]{3,2,1,0:T(8,128)S(1)} %get-tuple-element.33), channel_id=1, source_target_pairs={{0,128},{64,192},{128,0},{192,64},{1,129},{65,193},{129,1},{193,65... | collective-permute-start | bytes 589832 | tf_op jit(solution)/shard_map/ppermute | solution.py:240
  17.2 22.6 %collective-permute-start.4 = (f32[16,3,8,128]{3,2,1,0:T(8,128)S(1)}, f32[16,3,8,128]{3,2,1,0:T(8,128)S(1)}, u32[]{:S(2)}, u32[]{:S(2)}) collective-permute-start(f32[16,3,8,128]{3,2,1,0:T(8,128)S(1)} %get-tuple-element.34), channel_id=1, source_target_pairs={{0,192},{64,0},{128,64},{192,128},{1,193},{65,1},{129,65},{193,129... | collective-permute-start | bytes 589832 | tf_op jit(solution)/shard_map/ppermute | solution.py:240
  41.5 30.4 %all-to-all-start.1 = ((f32[8,10,3,8,128]{4,3,2,1,0:T(8,128)}), f32[8,10,3,8,128]{4,3,2,1,0:T(8,128)S(1)}, u32[]{:S(2)}, u32[]{:S(2)}) async-start(f32[8,10,3,8,128]{4,3,2,1,0:T(8,128)} %shard_map.40), calls=%async_computation.1 | async-start | bytes 1966080 | tf_op jit(solution)/shard_map/all_to_all | solution.py:277
  45.1 11.4 %collective-permute-start.8 = (f32[16,3,8,128]{3,2,1,0:T(8,128)S(1)}, f32[16,3,8,128]{3,2,1,0:T(8,128)S(1)}, u32[]{:S(2)}, u32[]{:S(2)}) collective-permute-start(f32[16,3,8,128]{3,2,1,0:T(8,128)S(1)} %get-tuple-element.40), channel_id=1, source_target_pairs={{0,64},{64,128},{128,192},{192,0},{1,65},{65,129},{129,193},{193,1... | collective-permute-start | bytes 589832 | tf_op jit(solution)/shard_map/ppermute | solution.py:240
  45.8 10.7 %collective-permute-start.9 = (f32[16,3,8,128]{3,2,1,0:T(8,128)S(1)}, f32[16,3,8,128]{3,2,1,0:T(8,128)S(1)}, u32[]{:S(2)}, u32[]{:S(2)}) collective-permute-start(f32[16,3,8,128]{3,2,1,0:T(8,128)S(1)} %get-tuple-element.41), channel_id=1, source_target_pairs={{0,128},{64,192},{128,0},{192,64},{1,129},{65,193},{129,1},{193,65... | collective-permute-start | bytes 589832 | tf_op jit(solution)/shard_map/ppermute | solution.py:240
  47.8 9.3 %collective-permute-start.10 = (f32[16,3,8,128]{3,2,1,0:T(8,128)S(1)}, f32[16,3,8,128]{3,2,1,0:T(8,128)S(1)}, u32[]{:S(2)}, u32[]{:S(2)}) collective-permute-start(f32[16,3,8,128]{3,2,1,0:T(8,128)S(1)} %get-tuple-element.42), channel_id=1, source_target_pairs={{0,192},{64,0},{128,64},{192,128},{1,193},{65,1},{129,65},{193,129... | collective-permute-start | bytes 589832 | tf_op jit(solution)/shard_map/ppermute | solution.py:240
  71.9 31.3 %all-to-all-start.2 = ((f32[8,10,3,8,128]{4,3,2,1,0:T(8,128)}), f32[8,10,3,8,128]{4,3,2,1,0:T(8,128)S(1)}, u32[]{:S(2)}, u32[]{:S(2)}) async-start(f32[8,10,3,8,128]{4,3,2,1,0:T(8,128)} %shard_map.42), calls=%async_computation.2 | async-start | bytes 1966080 | tf_op jit(solution)/shard_map/all_to_all | solution.py:278
  76.2 30.4 %collective-permute-start.5 = (f32[16,3,8,128]{3,2,1,0:T(8,128)S(1)}, f32[16,3,8,128]{3,2,1,0:T(8,128)S(1)}, u32[]{:S(2)}, u32[]{:S(2)}) collective-permute-start(f32[16,3,8,128]{3,2,1,0:T(8,128)S(1)} %get-tuple-element.36), channel_id=1, source_target_pairs={{0,64},{64,128},{128,192},{192,0},{1,65},{65,129},{129,193},{193,1... | collective-permute-start | bytes 589832 | tf_op jit(solution)/shard_map/ppermute | solution.py:240
  76.9 31.0 %collective-permute-start.6 = (f32[16,3,8,128]{3,2,1,0:T(8,128)S(1)}, f32[16,3,8,128]{3,2,1,0:T(8,128)S(1)}, u32[]{:S(2)}, u32[]{:S(2)}) collective-permute-start(f32[16,3,8,128]{3,2,1,0:T(8,128)S(1)} %get-tuple-element.37), channel_id=1, source_target_pairs={{0,128},{64,192},{128,0},{192,64},{1,129},{65,193},{129,1},{193,65... | collective-permute-start | bytes 589832 | tf_op jit(solution)/shard_map/ppermute | solution.py:240
  78.9 28.9 %collective-permute-start.7 = (f32[16,3,8,128]{3,2,1,0:T(8,128)S(1)}, f32[16,3,8,128]{3,2,1,0:T(8,128)S(1)}, u32[]{:S(2)}, u32[]{:S(2)}) collective-permute-start(f32[16,3,8,128]{3,2,1,0:T(8,128)S(1)} %get-tuple-element.38), channel_id=1, source_target_pairs={{0,192},{64,0},{128,64},{192,128},{1,193},{65,1},{129,65},{193,129... | collective-permute-start | bytes 589832 | tf_op jit(solution)/shard_map/ppermute | solution.py:240
  103.9 10.2 %collective-permute-start.11 = (f32[16,3,8,128]{3,2,1,0:T(8,128)S(1)}, f32[16,3,8,128]{3,2,1,0:T(8,128)S(1)}, u32[]{:S(2)}, u32[]{:S(2)}) collective-permute-start(f32[16,3,8,128]{3,2,1,0:T(8,128)S(1)} %get-tuple-element.44), channel_id=1, source_target_pairs={{0,64},{64,128},{128,192},{192,0},{1,65},{65,129},{129,193},{193,1... | collective-permute-start | bytes 589832 | tf_op jit(solution)/shard_map/ppermute | solution.py:240
  104.6 9.5 %collective-permute-start.12 = (f32[16,3,8,128]{3,2,1,0:T(8,128)S(1)}, f32[16,3,8,128]{3,2,1,0:T(8,128)S(1)}, u32[]{:S(2)}, u32[]{:S(2)}) collective-permute-start(f32[16,3,8,128]{3,2,1,0:T(8,128)S(1)} %get-tuple-element.45), channel_id=1, source_target_pairs={{0,128},{64,192},{128,0},{192,64},{1,129},{65,193},{129,1},{193,65... | collective-permute-start | bytes 589832 | tf_op jit(solution)/shard_map/ppermute | solution.py:240
  106.6 8.1 %collective-permute-start.13 = (f32[16,3,8,128]{3,2,1,0:T(8,128)S(1)}, f32[16,3,8,128]{3,2,1,0:T(8,128)S(1)}, u32[]{:S(2)}, u32[]{:S(2)}) collective-permute-start(f32[16,3,8,128]{3,2,1,0:T(8,128)S(1)} %get-tuple-element.46), channel_id=1, source_target_pairs={{0,192},{64,0},{128,64},{192,128},{1,193},{65,1},{129,65},{193,129... | collective-permute-start | bytes 589832 | tf_op jit(solution)/shard_map/ppermute | solution.py:240

commit v4 on v3

v4 whole, which is shorter than its diff:
```python
import functools

import jax
import jax.numpy as jnp
from jax import lax
from jax.experimental import pallas as pl
from jax.experimental.pallas import tpu as pltpu
from jax.sharding import Mesh, PartitionSpec as P

F32 = jnp.float32
XS, ZS = 4, 8
LANES = 128
BOXES = 10
VMEM = pl.BlockSpec(memory_space=pltpu.VMEM)
SMEM = pl.BlockSpec(memory_space=pltpu.SMEM)
PARAMS = pltpu.CompilerParams(vmem_limit_bytes=12 * 1024 * 1024)


def one_step(h, m, n, slope_x, slope_y):
    rows, cols = h.shape
    inv = 1.0 / h
    u = m * inv
    press = 0.0625 * (h * h)
    fx = 0.125 * (m * u) + press
    cross = 0.125 * (u * n)
    gy = 0.125 * (n * (n * inv)) + press

    def combine(q, f, g):
        q = 0.25 * q
        return (
            pltpu.roll(q - f, cols - 1, 1)
            + pltpu.roll(q + f, 1, 1)
            + pltpu.roll(q - g, rows - 1, 0)
            + pltpu.roll(q + g, 1, 0)
        )

    return (
        combine(h, 0.125 * m, 0.125 * n),
        combine(m, fx, cross) + h * slope_x,
        combine(n, cross, gy) + h * slope_y,
    )


def edge_kernel(counts_ref, x_ref, bed_ref, low_ref, high_ref, row_ref):
    count, fields, rows, _ = x_ref.shape
    for p in range(count):
        for f in range(fields):
            low_ref[p * fields + f] = x_ref[p, f, rows - 2 : rows]
            high_ref[p * fields + f] = x_ref[p, f, 0:2]
    low_ref[count * fields] = bed_ref[rows - 2 : rows]
    high_ref[count * fields] = bed_ref[0:2]
    lane = lax.broadcasted_iota(jnp.int32, (1, LANES), 1)
    total = jnp.int32(0)
    tile = jnp.zeros((1, LANES), jnp.int32)
    for j in range(count):
        c = counts_ref[j]
        total = total + c
        tile = jnp.where(lane == j, c, tile)
    tile = jnp.where(lane == count, total, tile)
    row_ref[...] = tile


def evolve_kernel(place_ref, x_ref, low_ref, high_ref, bed_ref, *refs):
    rows_ref, refs = refs[0:XS], refs[XS:]
    upper, lower = refs[0:XS], refs[XS : 2 * XS]
    row_ref, ext, sx, sy, res = refs[2 * XS :]
    count, fields, rows, cols = x_ref.shape
    ext[...] = jnp.ones_like(ext)
    ext[0, 0:rows] = bed_ref[...]
    ext[0, rows : rows + 2] = high_ref[count * fields]
    ext[0, rows + 6 : rows + 8] = low_ref[count * fields]
    b = ext[0]
    sx[...] = -0.125 * (pltpu.roll(b, cols - 1, 1) - pltpu.roll(b, 1, 1))
    sy[...] = -0.125 * (pltpu.roll(b, rows + 7, 0) - pltpu.roll(b, 1, 0))
    x = place_ref[0]

    def body(p, carry):
        for f in range(fields):
            ext[f, 0:rows] = x_ref[p, f]
            ext[f, rows : rows + 2] = high_ref[p * fields + f]
            ext[f, rows + 6 : rows + 8] = low_ref[p * fields + f]
        slope_x = sx[...]
        slope_y = sy[...]
        state = (ext[0], ext[1], ext[2])
        for _ in range(2):
            state = one_step(*state, slope_x, slope_y)
        for f in range(fields):
            res[f] = state[f][0:rows]
        for k in range(XS):
            at = pl.multiple_of(((x + k) % XS) * LANES, LANES)
            for f in range(fields):
                upper[k][p, f] = res[f, 0:8, pl.ds(at, LANES)]
                lower[k][p, f] = res[f, 8:16, pl.ds(at, LANES)]
        return carry

    lax.fori_loop(0, count, body, 0)
    for z in range(ZS):
        for k in range(XS):
            row_ref[z, k : k + 1] = rows_ref[k][...]


def plan_kernel(place_ref, row_ref, put_ref, take_ref, base, ctr):
    x, z = place_ref[0], place_ref[1]
    back = [(x + XS - k) % XS for k in range(XS)]
    total = jnp.int32(0)
    for at in range(XS):
        k = (x + XS - at) % XS
        for zs in range(ZS):
            base[at * ZS + zs] = total
            total = total + row_ref[zs, k, 16]
    base[XS * ZS] = total
    for i in range(ZS):
        ctr[i] = 0
    for i in range(16 * ZS):
        put_ref[i] = 0
    dump = 16 * ZS

    for k in range(XS):
        e = base[back[k] * ZS + z]
        for j in range(16):
            c = row_ref[z, k, j]
            for i in range(2):
                to = (e + i - z) & (ZS - 1)
                t = ctr[to]
                live = c > i
                ctr[to] = t + live.astype(jnp.int32)
                put_ref[jnp.where(live, to * 16 + t, dump)] = k * 16 + j
            e = e + c

    for i in range(ZS):
        ctr[i] = 0
    dump = 16 * XS
    for k in range(XS):
        for zs in range(ZS):
            lo = base[back[k] * ZS + zs]
            hi = base[back[k] * ZS + zs + 1]
            first = lo + ((z - lo) & (ZS - 1))
            t0 = ctr[zs]
            box = ((z - zs) & (ZS - 1)) * 16 + t0
            for i in range(4):
                s = first + i * ZS
                take_ref[jnp.where(s < hi, s >> 3, dump)] = box + i
            ctr[zs] = t0 + jnp.maximum((hi - first + ZS - 1) >> 3, 0)


def plan(place, row):
    return pl.pallas_call(
        plan_kernel,
        in_specs=[SMEM, SMEM],
        out_specs=[SMEM, SMEM],
        out_shape=[
            jax.ShapeDtypeStruct((16 * ZS + 8,), jnp.int32),
            jax.ShapeDtypeStruct((16 * XS + 8,), jnp.int32),
        ],
        scratch_shapes=[
            pltpu.SMEM((XS * ZS + 1,), jnp.int32),
            pltpu.SMEM((ZS,), jnp.int32),
        ],
        compiler_params=PARAMS,
        cost_estimate=pl.CostEstimate(flops=0, bytes_accessed=4_000_000, transcendentals=0),
    )(place, row)


def pick(parts, code):
    which, item = code >> 4, code & 15
    value = parts[0][item]
    for k in range(1, len(parts)):
        value = jnp.where(which == k, parts[k][item], value)
    return value


def pack_kernel(put_ref, *refs):
    data, outs = refs[0:XS], refs[XS:]
    for zs in range(ZS):

        def body(t, carry):
            outs[zs][t] = pick(data, put_ref[zs * 16 + t])
            return carry

        lax.fori_loop(0, BOXES, body, 0, unroll=5)


def pack(put, data):
    return pl.pallas_call(
        pack_kernel,
        in_specs=[SMEM] + [VMEM] * XS,
        out_specs=[VMEM] * ZS,
        out_shape=[jax.ShapeDtypeStruct((BOXES, 3, 8, LANES), F32)] * ZS,
        compiler_params=PARAMS,
        cost_estimate=pl.CostEstimate(flops=0, bytes_accessed=3_000_000, transcendentals=0),
    )(put, *data)


def spread_kernel(place_ref, take_ref, *refs):
    boxes, outs = refs[0:ZS], refs[ZS:]
    x = place_ref[0]
    for k in range(XS):
        to = (x + k) % XS

        def body(i, carry):
            code = take_ref[i * XS + to]
            outs[k][i] = pick(boxes, code)
            return carry

        lax.fori_loop(0, 16, body, 0, unroll=4)


def spread(place, take, boxes):
    return pl.pallas_call(
        spread_kernel,
        in_specs=[SMEM, SMEM] + [VMEM] * ZS,
        out_specs=[VMEM] * XS,
        out_shape=[jax.ShapeDtypeStruct((16, 3, 8, LANES), F32)] * XS,
        compiler_params=PARAMS,
        cost_estimate=pl.CostEstimate(flops=0, bytes_accessed=3_000_000, transcendentals=0),
    )(place, take, *boxes)


def join_kernel(place_ref, *refs):
    parts, out_ref = refs[: 2 * XS], refs[2 * XS]
    x = place_ref[0]
    for k in range(XS):
        at = pl.multiple_of(((x + XS - k) % XS) * LANES, LANES)

        def body(i, carry):
            for f in range(3):
                out_ref[i, f, 0:8, pl.ds(at, LANES)] = parts[k][i, f]
                out_ref[i, f, 8:16, pl.ds(at, LANES)] = parts[XS + k][i, f]
            return carry

        lax.fori_loop(0, 16, body, 0, unroll=4)


def along(axis, parts):
    n = len(parts)
    return [parts[0]] + [
        lax.ppermute(parts[k], axis, [(i, (i + k) % n) for i in range(n)]) for k in range(1, n)
    ]


def per_device(particles, counts, bed):
    count, fields, rows, cols = particles.shape
    place = jnp.stack([lax.axis_index("x"), lax.axis_index("z")]).astype(jnp.int32)
    edges = jax.ShapeDtypeStruct((count * fields + 1, 2, cols), F32)
    low, high, row = pl.pallas_call(
        edge_kernel,
        in_specs=[SMEM, VMEM, VMEM],
        out_specs=[VMEM] * 3,
        out_shape=[edges, edges, jax.ShapeDtypeStruct((1, LANES), jnp.int32)],
        compiler_params=PARAMS,
    )(counts, particles, bed)
    strips = lax.axis_size("space")
    low = lax.ppermute(low, "space", [(i, (i + 1) % strips) for i in range(strips)])
    high = lax.ppermute(high, "space", [((i + 1) % strips, i) for i in range(strips)])
    known = along("x", [row] * XS)
    half = jax.ShapeDtypeStruct((count, fields, 8, LANES), F32)
    *parts, row = pl.pallas_call(
        evolve_kernel,
        in_specs=[SMEM] + [VMEM] * (4 + XS),
        out_specs=[VMEM] * (2 * XS + 1),
        out_shape=[half] * (2 * XS) + [jax.ShapeDtypeStruct((ZS, XS, LANES), jnp.int32)],
        scratch_shapes=[
            pltpu.VMEM((fields, rows + 8, cols), F32),
            pltpu.VMEM((rows + 8, cols), F32),
            pltpu.VMEM((rows + 8, cols), F32),
            pltpu.VMEM((fields, rows, cols), F32),
        ],
        compiler_params=PARAMS,
        cost_estimate=pl.CostEstimate(flops=0, bytes_accessed=20_000_000, transcendentals=0),
    )(place, particles, low, high, bed, *known)
    upper = along("x", parts[:XS])
    row = lax.all_to_all(row, "z", 0, 0, tiled=True)
    lower = along("x", parts[XS:])
    put, take = plan(place, row)
    boxes_a = along("z", pack(put, upper))
    boxes_b = along("z", pack(put, lower))
    out_a = along("x", spread(place, take, boxes_a))
    out_b = along("x", spread(place, take, boxes_b))
    return pl.pallas_call(
        join_kernel,
        in_specs=[SMEM] + [VMEM] * (2 * XS),
        out_specs=VMEM,
        out_shape=jax.ShapeDtypeStruct(particles.shape, F32),
        compiler_params=PARAMS,
    )(place, *out_a, *out_b)


def solution(mesh):
    wide = Mesh(mesh.devices.reshape(XS, ZS, -1), ("x", "z", "space"))
    in_specs = (P(("x", "z"), None, "space", None), P(("x", "z")), P("space", None))
    out_specs = P(("x", "z"), None, "space", None)
    return jax.shard_map(
        per_device, mesh=wide, in_specs=in_specs, out_specs=out_specs, check_vma=False
    )
```

time: 117 us -> 116 us (level)
  starting transfers between devices: 26.4 us -> 46.1 us
  waiting for transfers between devices: 54.3 us -> 35.4 us
  blocking collectives: 18.5 us -> 16.2 us
    all_to_all x2 -> x0, waiting for transfers between devices: 35.9 us -> none  [the longest x1 22.9 us: per_device(): boxes_b = lax.all_to_all(pack(put, lower), 'z', 0, 0, tiled=True)]
    ppermute x12 -> x29, starting transfers between devices: 17.5 us -> 44.3 us  [along(): lax.ppermute(parts[k], axis, [(i, (i + k) % n) for i in range(n)])]
    ppermute x12 -> x29, waiting for transfers between devices: 15 us -> 35.4 us  [along(): lax.ppermute(parts[k], axis, [(i, (i + k) % n) for i in range(n)])]
    all_to_all x2 -> x0, starting transfers between devices: 7.11 us -> none  [the longest x1 3.56 us: per_device(): boxes_a = lax.all_to_all(pack(put, upper), 'z', 0, 0, tiled=True)]
    ppermute x1, waiting for transfers between devices: 3.32 us -> 0.01 us  [per_device(): lax.ppermute(low, 'space', [(i, (i + 1) % strips) for i in range(strips)])]
    all_to_all x1, blocking collectives: 18.5 us -> 16.2 us  [per_device(): row = lax.all_to_all(row, 'z', 0, 0, tiled=True)]
  transfers between devices with their start and end apart: 16 -> 31, of which waited for: 7 -> 11; matrix products, arithmetic and copies ran while one was open for 0% -> 0% of each run, Pallas kernels for 5% -> 6%
where the time goes in v4:
time: 116 us
  starting transfers between devices  46.1 us (40%)
  waiting for transfers between devices  35.4 us (31%)
  blocking collectives  16.2 us (14%)
  Pallas kernels  15.1 us (13%)
  local copies, waits for them, and re-layouts  2.83 us (2%)
    ppermute x29, starting transfers between devices, along(): lax.ppermute(parts[k], axis, [(i, (i + k) % n) for i in range(n)])  44.3 us
    ppermute x29, waiting for transfers between devices, along(): lax.ppermute(parts[k], axis, [(i, (i + k) % n) for i in range(n)])  35.4 us
    all_to_all x1, blocking collectives, per_device(): row = lax.all_to_all(row, 'z', 0, 0, tiled=True)  16.2 us
    pallas_call x1, Pallas kernels, per_device(): pl.pallas_call(evolve_kernel, in_specs=[SMEM] + [VMEM] * (4 + XS), out_sp...  5.45 us
    unnamed x10, local copies, waits for them, and re-layouts  2.83 us
    pallas_call x1, Pallas kernels, plan(): pl.pallas_call(plan_kernel, in_specs=[SMEM, SMEM], out_specs=[SMEM, SMEM]...  2.52 us
    pallas_call x2, Pallas kernels, spread(): pl.pallas_call(spread_kernel, in_specs=[SMEM, SMEM] + [VMEM] * ZS, out_sp...  2.48 us
  transfers between devices with their start and end apart: 31, of which 11 were waited for; matrix products, arithmetic and copies ran while one was open for 0% of the time, Pallas kernels for 6%

profile of v4, /device:TPU:16, one launch (start us, length us, event | category | flops | bytes accessed | tf_op | source)
XLA Modules:
  0.0 115.9 jit_solution(15402154284309025558)
XLA Ops:
  0.0 1.4 %copy-done = f32[16,3,16,512]{3,2,1,0:T(8,128)S(1)} copy-done((f32[16,3,16,512]{3,2,1,0:T(8,128)S(1)}, f32[16,3,16,512]{3,2,1,0:T(8,128)}, u32[]{:S(2)}) %copy-start) | copy-done | bytes 1572888
  1.4 0.8 copy-done.2
  2.2 0.7 copy-done.4
  2.8 0.6 shard_map.37
  3.5 0.0 collective-permute-start
  3.5 1.7 %collective-permute-start.1 = (f32[49,2,512]{2,1,0:T(2,128)S(1)}, f32[49,2,512]{2,1,0:T(2,128)S(1)}, u32[]{:S(2)}, u32[]{:S(2)}) collective-permute-start(f32[49,2,512]{2,1,0:T(2,128)S(1)} %get-tuple-element.44), channel_id=1, source_target_pairs={{1,0},{2,1},{3,2},{4,3},{5,4},{6,5},{7,6},{0,7},{9,8},{10,9},{11,1... | collective-permute-start | bytes 602120 | tf_op jit(solution)/shard_map/ppermute | solution.py:254
  5.2 2.8 %collective-permute-start.4 = (s32[1,128]{1,0:T(1,128)S(1)}, s32[1,128]{1,0:T(1,128)S(1)}, u32[]{:S(2)}, u32[]{:S(2)}) collective-permute-start(s32[1,128]{1,0:T(1,128)S(1)} %get-tuple-element.45.refs_0_), channel_id=1, source_target_pairs={{0,192},{64,0},{128,64},{192,128},{1,193},{65,1},{129,65},{193,129... | collective-permute-start | bytes 1544 | tf_op jit(solution)/shard_map/ppermute | solution.py:237
  8.0 0.8 collective-permute-start.3
  8.8 0.9 collective-permute-start.2
  9.7 0.1 pad_add_fusion.place_ref
  9.7 0.0 collective-permute-done.4.refs_3_
  9.7 3.3 %collective-permute-done.3.refs_2_ = s32[1,128]{1,0:T(1,128)S(1)} collective-permute-done((s32[1,128]{1,0:T(1,128)S(1)}, s32[1,128]{1,0:T(1,128)S(1)}, u32[]{:S(2)}, u32[]{:S(2)}) %collective-permute-start.3) | collective-permute-done | bytes 544 | tf_op jit(solution)/shard_map/ppermute | solution.py:237
  13.0 0.5 collective-permute-done.2.refs_1_
  13.5 0.0 collective-permute-done.low_ref
  13.5 0.0 collective-permute-done.1.high_ref
  13.6 5.5 %shard_map.38 = (f32[16,3,8,128]{3,2,1,0:T(8,128)S(1)}, f32[16,3,8,128]{3,2,1,0:T(8,128)S(1)}, f32[16,3,8,128]{3,2,1,0:T(8,128)S(1)}, f32[16,3,8,128]{3,2,1,0:T(...) custom-call(s32[2]{0:T(128)S(1)} %pad_add_fusion.place_ref, ...), custom_call_target="tpu_custom_call" | custom-call | bytes 20000000 | tf_op jit(solution)/shard_map/pallas_call | solution.py:257
  19.0 0.1 collective-permute-start.5
  19.1 1.8 %collective-permute-start.6 = (f32[16,3,8,128]{3,2,1,0:T(8,128)S(1)}, f32[16,3,8,128]{3,2,1,0:T(8,128)S(1)}, u32[]{:S(2)}, u32[]{:S(2)}) collective-permute-start(f32[16,3,8,128]{3,2,1,0:T(8,128)S(1)} %get-tuple-element.51), channel_id=1, source_target_pairs={{0,128},{64,192},{128,0},{192,64},{1,129},{65,193},{129,1},{193,65... | collective-permute-start | bytes 589832 | tf_op jit(solution)/shard_map/ppermute | solution.py:237
  20.9 2.3 %collective-permute-start.7 = (f32[16,3,8,128]{3,2,1,0:T(8,128)S(1)}, f32[16,3,8,128]{3,2,1,0:T(8,128)S(1)}, u32[]{:S(2)}, u32[]{:S(2)}) collective-permute-start(f32[16,3,8,128]{3,2,1,0:T(8,128)S(1)} %get-tuple-element.52), channel_id=1, source_target_pairs={{0,192},{64,0},{128,64},{192,128},{1,193},{65,1},{129,65},{193,129... | collective-permute-start | bytes 589832 | tf_op jit(solution)/shard_map/ppermute | solution.py:237
  23.2 2.1 %collective-permute-start.19 = (f32[16,3,8,128]{3,2,1,0:T(8,128)S(1)}, f32[16,3,8,128]{3,2,1,0:T(8,128)S(1)}, u32[]{:S(2)}, u32[]{:S(2)}) collective-permute-start(f32[16,3,8,128]{3,2,1,0:T(8,128)S(1)} %get-tuple-element.67), channel_id=1, source_target_pairs={{0,128},{64,192},{128,0},{192,64},{1,129},{65,193},{129,1},{193,65... | collective-permute-start | bytes 589832 | tf_op jit(solution)/shard_map/ppermute | solution.py:237
  25.3 6.8 %collective-permute-done.5.refs_1_ = f32[16,3,8,128]{3,2,1,0:T(8,128)S(1)} collective-permute-done((f32[16,3,8,128]{3,2,1,0:T(8,128)S(1)}, f32[16,3,8,128]{3,2,1,0:T(8,128)S(1)}, u32[]{:S(2)}, u32[]{:S(2)}) %collective-permute-start.5) | collective-permute-done | bytes 196640 | tf_op jit(solution)/shard_map/ppermute | solution.py:237
  32.0 16.2 %all_to_all.5.row_ref = s32[8,4,128]{2,1,0:T(4,128)S(1)} all-to-all(s32[8,4,128]{2,1,0:T(4,128)S(1)} %get-tuple-element.46), channel_id=1, replica_groups=mesh['x'=4,'z'=8,'space'=8] {'z'}, dimensions={0} | all-to-all | bytes 32768 | tf_op jit(solution)/shard_map/all_to_all | solution.py:272
  48.3 2.5 %shard_map.39 = (s32[136]{0:T(256)S(1)}, s32[72]{0:T(128)S(1)}) custom-call(s32[2]{0:T(128)S(1)} %pad_add_fusion.place_ref, s32[8,4,128]{2,1,0:T(4,128)S(1)} %all_to_all.5.row_ref), custom_call_target="tpu_custom_call" | custom-call | bytes 4000000 | tf_op jit(solution)/shard_map/pallas_call | solution.py:147
  50.8 0.0 collective-permute-done.7.refs_3_
  50.8 1.1 shard_map.40
  51.9 0.5 collective-permute-start.8
  52.4 0.6 collective-permute-start.9
  53.0 0.0 collective-permute-done.18.refs_1_
  53.0 2.4 %collective-permute-start.10 = (f32[10,3,8,128]{3,2,1,0:T(8,128)S(1)}, f32[10,3,8,128]{3,2,1,0:T(8,128)S(1)}, u32[]{:S(2)}, u32[]{:S(2)}) collective-permute-start(f32[10,3,8,128]{3,2,1,0:T(8,128)S(1)} %get-tuple-element.56), channel_id=1, source_target_pairs={{0,24},{8,32},{16,40},{24,48},{32,56},{40,0},{48,8},{56,16},{1,25}... | collective-permute-start | bytes 368648 | tf_op jit(solution)/shard_map/ppermute | solution.py:237
  55.4 3.6 %collective-permute-start.11 = (f32[10,3,8,128]{3,2,1,0:T(8,128)S(1)}, f32[10,3,8,128]{3,2,1,0:T(8,128)S(1)}, u32[]{:S(2)}, u32[]{:S(2)}) collective-permute-start(f32[10,3,8,128]{3,2,1,0:T(8,128)S(1)} %get-tuple-element.57), channel_id=1, source_target_pairs={{0,32},{8,40},{16,48},{24,56},{32,0},{40,8},{48,16},{56,24},{1,33}... | collective-permute-start | bytes 368648 | tf_op jit(solution)/shard_map/ppermute | solution.py:237
  58.9 0.0 collective-permute-done.20.refs_3_
  58.9 2.3 %collective-permute-start.12 = (f32[10,3,8,128]{3,2,1,0:T(8,128)S(1)}, f32[10,3,8,128]{3,2,1,0:T(8,128)S(1)}, u32[]{:S(2)}, u32[]{:S(2)}) collective-permute-start(f32[10,3,8,128]{3,2,1,0:T(8,128)S(1)} %get-tuple-element.58), channel_id=1, source_target_pairs={{0,40},{8,48},{16,56},{24,0},{32,8},{40,16},{48,24},{56,32},{1,41}... | collective-permute-start | bytes 368648 | tf_op jit(solution)/shard_map/ppermute | solution.py:237
  61.2 0.0 collective-permute-done.8.refs_1_
  61.2 1.8 %collective-permute-start.13 = (f32[10,3,8,128]{3,2,1,0:T(8,128)S(1)}, f32[10,3,8,128]{3,2,1,0:T(8,128)S(1)}, u32[]{:S(2)}, u32[]{:S(2)}) collective-permute-start(f32[10,3,8,128]{3,2,1,0:T(8,128)S(1)} %get-tuple-element.59), channel_id=1, source_target_pairs={{0,48},{8,56},{16,0},{24,8},{32,16},{40,24},{48,32},{56,40},{1,49}... | collective-permute-start | bytes 368648 | tf_op jit(solution)/shard_map/ppermute | solution.py:237
  63.1 0.0 collective-permute-done.9.refs_2_
  63.1 1.7 %collective-permute-start.14 = (f32[10,3,8,128]{3,2,1,0:T(8,128)S(1)}, f32[10,3,8,128]{3,2,1,0:T(8,128)S(1)}, u32[]{:S(2)}, u32[]{:S(2)}) collective-permute-start(f32[10,3,8,128]{3,2,1,0:T(8,128)S(1)} %get-tuple-element.60), channel_id=1, source_target_pairs={{0,56},{8,0},{16,8},{24,16},{32,24},{40,32},{48,40},{56,48},{1,57}... | collective-permute-start | bytes 368648 | tf_op jit(solution)/shard_map/ppermute | solution.py:237
  64.7 1.1 shard_map.42
  65.8 5.9 %collective-permute-done.10.refs_3_ = f32[10,3,8,128]{3,2,1,0:T(8,128)S(1)} collective-permute-done((f32[10,3,8,128]{3,2,1,0:T(8,128)S(1)}, f32[10,3,8,128]{3,2,1,0:T(8,128)S(1)}, u32[]{:S(2)}, u32[]{:S(2)}) %collective-permute-start.10) | collective-permute-done | bytes 122912 | tf_op jit(solution)/shard_map/ppermute | solution.py:237
  71.7 0.6 collective-permute-done.11.refs_4_
  72.2 4.6 %collective-permute-start.22 = (f32[10,3,8,128]{3,2,1,0:T(8,128)S(1)}, f32[10,3,8,128]{3,2,1,0:T(8,128)S(1)}, u32[]{:S(2)}, u32[]{:S(2)}) collective-permute-start(f32[10,3,8,128]{3,2,1,0:T(8,128)S(1)} %get-tuple-element.71), channel_id=1, source_target_pairs={{0,16},{8,24},{16,32},{24,40},{32,48},{40,56},{48,0},{56,8},{1,17}... | collective-permute-start | bytes 368648 | tf_op jit(solution)/shard_map/ppermute | solution.py:237
  76.8 0.0 collective-permute-done.12.refs_5_
  76.8 0.0 collective-permute-start.23
  76.8 0.0 collective-permute-done.13.refs_6_
  76.8 3.9 %collective-permute-done.14.refs_7_ = f32[10,3,8,128]{3,2,1,0:T(8,128)S(1)} collective-permute-done((f32[10,3,8,128]{3,2,1,0:T(8,128)S(1)}, f32[10,3,8,128]{3,2,1,0:T(8,128)S(1)}, u32[]{:S(2)}, u32[]{:S(2)}) %collective-permute-start.14) | collective-permute-done | bytes 122912 | tf_op jit(solution)/shard_map/ppermute | solution.py:237
  80.7 1.2 %shard_map.41 = (f32[16,3,8,128]{3,2,1,0:T(8,128)S(1)}, f32[16,3,8,128]{3,2,1,0:T(8,128)S(1)}, f32[16,3,8,128]{3,2,1,0:T(8,128)S(1)}, f32[16,3,8,128]{3,2,1,0:T(8,128)S(1)}) custom-call(s32[2]{0:T(128)S(1)} %pad_add_fusion.place_ref, s32[72]{0:T(128)S(1)} %get-tuple-element.47.take_ref, f32[10,3,8,128]{3,2,1,0:T(8,128)S(1)} %get-tuple-element.53.refs_0_, ...), custom_call_target="tpu_custom_call" | custom-call | bytes 3000000 | tf_op jit(solution)/shard_map/pallas_call | solution.py:209
  81.9 2.2 %collective-permute-start.15 = (f32[16,3,8,128]{3,2,1,0:T(8,128)S(1)}, f32[16,3,8,128]{3,2,1,0:T(8,128)S(1)}, u32[]{:S(2)}, u32[]{:S(2)}) collective-permute-start(f32[16,3,8,128]{3,2,1,0:T(8,128)S(1)} %get-tuple-element.62), channel_id=1, source_target_pairs={{0,64},{64,128},{128,192},{192,0},{1,65},{65,129},{129,193},{193,1... | collective-permute-start | bytes 589832 | tf_op jit(solution)/shard_map/ppermute | solution.py:237
  84.1 6.5 %collective-permute-start.24 = (f32[10,3,8,128]{3,2,1,0:T(8,128)S(1)}, f32[10,3,8,128]{3,2,1,0:T(8,128)S(1)}, u32[]{:S(2)}, u32[]{:S(2)}) collective-permute-start(f32[10,3,8,128]{3,2,1,0:T(8,128)S(1)} %get-tuple-element.73), channel_id=1, source_target_pairs={{0,32},{8,40},{16,48},{24,56},{32,0},{40,8},{48,16},{56,24},{1,33}... | collective-permute-start | bytes 368648 | tf_op jit(solution)/shard_map/ppermute | solution.py:237
  90.6 0.0 collective-permute-done.21.refs_1_
  90.6 0.0 collective-permute-start.25
  90.6 2.7 %collective-permute-start.26 = (f32[10,3,8,128]{3,2,1,0:T(8,128)S(1)}, f32[10,3,8,128]{3,2,1,0:T(8,128)S(1)}, u32[]{:S(2)}, u32[]{:S(2)}) collective-permute-start(f32[10,3,8,128]{3,2,1,0:T(8,128)S(1)} %get-tuple-element.75), channel_id=1, source_target_pairs={{0,48},{8,56},{16,0},{24,8},{32,16},{40,24},{48,32},{56,40},{1,49}... | collective-permute-start | bytes 368648 | tf_op jit(solution)/shard_map/ppermute | solution.py:237
  93.3 1.5 %collective-permute-start.27 = (f32[10,3,8,128]{3,2,1,0:T(8,128)S(1)}, f32[10,3,8,128]{3,2,1,0:T(8,128)S(1)}, u32[]{:S(2)}, u32[]{:S(2)}) collective-permute-start(f32[10,3,8,128]{3,2,1,0:T(8,128)S(1)} %get-tuple-element.76), channel_id=1, source_target_pairs={{0,56},{8,0},{16,8},{24,16},{32,24},{40,32},{48,40},{56,48},{1,57}... | collective-permute-start | bytes 368648 | tf_op jit(solution)/shard_map/ppermute | solution.py:237
  94.8 2.8 %collective-permute-done.25.refs_5_ = f32[10,3,8,128]{3,2,1,0:T(8,128)S(1)} collective-permute-done((f32[10,3,8,128]{3,2,1,0:T(8,128)S(1)}, f32[10,3,8,128]{3,2,1,0:T(8,128)S(1)}, u32[]{:S(2)}, u32[]{:S(2)}) %collective-permute-start.25) | collective-permute-done | bytes 122912 | tf_op jit(solution)/shard_map/ppermute | solution.py:237
  97.7 0.0 collective-permute-start.17
  97.7 2.9 %collective-permute-done.26.refs_6_ = f32[10,3,8,128]{3,2,1,0:T(8,128)S(1)} collective-permute-done((f32[10,3,8,128]{3,2,1,0:T(8,128)S(1)}, f32[10,3,8,128]{3,2,1,0:T(8,128)S(1)}, u32[]{:S(2)}, u32[]{:S(2)}) %collective-permute-start.26) | collective-permute-done | bytes 122912 | tf_op jit(solution)/shard_map/ppermute | solution.py:237
  100.6 2.2 %collective-permute-done.27.refs_7_ = f32[10,3,8,128]{3,2,1,0:T(8,128)S(1)} collective-permute-done((f32[10,3,8,128]{3,2,1,0:T(8,128)S(1)}, f32[10,3,8,128]{3,2,1,0:T(8,128)S(1)}, u32[]{:S(2)}, u32[]{:S(2)}) %collective-permute-start.27) | collective-permute-done | bytes 122912 | tf_op jit(solution)/shard_map/ppermute | solution.py:237
  102.7 1.2 %shard_map.43 = (f32[16,3,8,128]{3,2,1,0:T(8,128)S(1)}, f32[16,3,8,128]{3,2,1,0:T(8,128)S(1)}, f32[16,3,8,128]{3,2,1,0:T(8,128)S(1)}, f32[16,3,8,128]{3,2,1,0:T(8,128)S(1)}) custom-call(s32[2]{0:T(128)S(1)} %pad_add_fusion.place_ref, s32[72]{0:T(128)S(1)} %get-tuple-element.47.take_ref, f32[10,3,8,128]{3,2,1,0:T(8,128)S(1)} %get-tuple-element.69.refs_0_, ...), custom_call_target="tpu_custom_call" | custom-call | bytes 3000000 | tf_op jit(solution)/shard_map/pallas_call | solution.py:209
  104.0 0.2 collective-permute-start.28
  104.2 0.0 collective-permute-start.29
  104.2 0.0 collective-permute-done.15.refs_1_
  104.2 3.1 %collective-permute-start.30 = (f32[16,3,8,128]{3,2,1,0:T(8,128)S(1)}, f32[16,3,8,128]{3,2,1,0:T(8,128)S(1)}, u32[]{:S(2)}, u32[]{:S(2)}) collective-permute-start(f32[16,3,8,128]{3,2,1,0:T(8,128)S(1)} %get-tuple-element.80), channel_id=1, source_target_pairs={{0,192},{64,0},{128,64},{192,128},{1,193},{65,1},{129,65},{193,129... | collective-permute-start | bytes 589832 | tf_op jit(solution)/shard_map/ppermute | solution.py:237
  107.3 0.0 collective-permute-done.17.refs_3_
  107.3 5.7 %collective-permute-done.28.refs_5_ = f32[16,3,8,128]{3,2,1,0:T(8,128)S(1)} collective-permute-done((f32[16,3,8,128]{3,2,1,0:T(8,128)S(1)}, f32[16,3,8,128]{3,2,1,0:T(8,128)S(1)}, u32[]{:S(2)}, u32[]{:S(2)}) %collective-permute-start.28) | collective-permute-done | bytes 196640 | tf_op jit(solution)/shard_map/ppermute | solution.py:237
  113.0 0.9 collective-permute-done.30.refs_7_
  113.9 1.9 %shard_map.44 = f32[16,3,16,512]{3,2,1,0:T(8,128)} custom-call(s32[2]{0:T(128)S(1)} %pad_add_fusion.place_ref, f32[16,3,8,128]{3,2,1,0:T(8,128)S(1)} %get-tuple-element.61.refs_0_, f32[16,3,8,128]{3,2,1,0:T(8,128)S(1)} %collective-permute-done.15.refs_1_, f32[16,3,8,128]{3,2,1,0:T(8,128)S(1)} %collective-permute-done.16.refs_2_, ...), custom_call_target="tpu_custom_call" | custom-call | tf_op jit(solution)/shard_map/pallas_call | solution.py:279
  (18 shorter events, 0.0 us)
Async XLA Ops:
  0.0 1.4 %copy-start = (f32[16,3,16,512]{3,2,1,0:T(8,128)S(1)}, f32[16,3,16,512]{3,2,1,0:T(8,128)}, u32[]{:S(2)}) copy-start(f32[16,3,16,512]{3,2,1,0:T(8,128)} %x_ref.3) | copy-start | bytes 4718596
  1.4 0.8 copy-start.2
  2.2 0.7 copy-start.4
  2.8 10.7 %copy-start.1 = (f32[16,3,16,512]{3,2,1,0:T(8,128)S(1)}, f32[16,3,16,512]{3,2,1,0:T(8,128)}, u32[]{:S(2)}) copy-start(f32[16,3,16,512]{3,2,1,0:T(8,128)} %x_ref.3) | copy-start | bytes 4718596
  2.8 10.7 %copy-start.3 = (f32[16,512]{1,0:T(8,128)S(1)}, f32[16,512]{1,0:T(8,128)}, u32[]{:S(2)}) copy-start(f32[16,512]{1,0:T(8,128)} %bed_ref.3) | copy-start | bytes 98308
  3.5 10.1 %collective-permute-start = (f32[49,2,512]{2,1,0:T(2,128)S(1)}, f32[49,2,512]{2,1,0:T(2,128)S(1)}, u32[]{:S(2)}, u32[]{:S(2)}) collective-permute-start(f32[49,2,512]{2,1,0:T(2,128)S(1)} %get-tuple-element.43), channel_id=1, source_target_pairs={{0,1},{1,2},{2,3},{3,4},{4,5},{5,6},{6,7},{7,0},{8,9},{9,10},{10,1... | collective-permute-start | bytes 602120 | tf_op jit(solution)/shard_map/ppermute | solution.py:253
  3.5 10.1 %collective-permute-start.1 = (f32[49,2,512]{2,1,0:T(2,128)S(1)}, f32[49,2,512]{2,1,0:T(2,128)S(1)}, u32[]{:S(2)}, u32[]{:S(2)}) collective-permute-start(f32[49,2,512]{2,1,0:T(2,128)S(1)} %get-tuple-element.44), channel_id=1, source_target_pairs={{1,0},{2,1},{3,2},{4,3},{5,4},{6,5},{7,6},{0,7},{9,8},{10,9},{11,1... | collective-permute-start | bytes 602120 | tf_op jit(solution)/shard_map/ppermute | solution.py:254
  5.2 4.5 %collective-permute-start.4 = (s32[1,128]{1,0:T(1,128)S(1)}, s32[1,128]{1,0:T(1,128)S(1)}, u32[]{:S(2)}, u32[]{:S(2)}) collective-permute-start(s32[1,128]{1,0:T(1,128)S(1)} %get-tuple-element.45.refs_0_), channel_id=1, source_target_pairs={{0,192},{64,0},{128,64},{192,128},{1,193},{65,1},{129,65},{193,129... | collective-permute-start | bytes 1544 | tf_op jit(solution)/shard_map/ppermute | solution.py:237
  8.0 5.0 %collective-permute-start.3 = (s32[1,128]{1,0:T(1,128)S(1)}, s32[1,128]{1,0:T(1,128)S(1)}, u32[]{:S(2)}, u32[]{:S(2)}) collective-permute-start(s32[1,128]{1,0:T(1,128)S(1)} %get-tuple-element.45.refs_0_), channel_id=1, source_target_pairs={{0,128},{64,192},{128,0},{192,64},{1,129},{65,193},{129,1},{193,65... | collective-permute-start | bytes 1544 | tf_op jit(solution)/shard_map/ppermute | solution.py:237
  8.8 4.8 %collective-permute-start.2 = (s32[1,128]{1,0:T(1,128)S(1)}, s32[1,128]{1,0:T(1,128)S(1)}, u32[]{:S(2)}, u32[]{:S(2)}) collective-permute-start(s32[1,128]{1,0:T(1,128)S(1)} %get-tuple-element.45.refs_0_), channel_id=1, source_target_pairs={{0,64},{64,128},{128,192},{192,0},{1,65},{65,129},{129,193},{193,1... | collective-permute-start | bytes 1544 | tf_op jit(solution)/shard_map/ppermute | solution.py:237
  19.0 13.0 %collective-permute-start.5 = (f32[16,3,8,128]{3,2,1,0:T(8,128)S(1)}, f32[16,3,8,128]{3,2,1,0:T(8,128)S(1)}, u32[]{:S(2)}, u32[]{:S(2)}) collective-permute-start(f32[16,3,8,128]{3,2,1,0:T(8,128)S(1)} %get-tuple-element.50), channel_id=1, source_target_pairs={{0,64},{64,128},{128,192},{192,0},{1,65},{65,129},{129,193},{193,1... | collective-permute-start | bytes 589832 | tf_op jit(solution)/shard_map/ppermute | solution.py:237
  19.1 31.7 %collective-permute-start.6 = (f32[16,3,8,128]{3,2,1,0:T(8,128)S(1)}, f32[16,3,8,128]{3,2,1,0:T(8,128)S(1)}, u32[]{:S(2)}, u32[]{:S(2)}) collective-permute-start(f32[16,3,8,128]{3,2,1,0:T(8,128)S(1)} %get-tuple-element.51), channel_id=1, source_target_pairs={{0,128},{64,192},{128,0},{192,64},{1,129},{65,193},{129,1},{193,65... | collective-permute-start | bytes 589832 | tf_op jit(solution)/shard_map/ppermute | solution.py:237
  20.9 29.9 %collective-permute-start.7 = (f32[16,3,8,128]{3,2,1,0:T(8,128)S(1)}, f32[16,3,8,128]{3,2,1,0:T(8,128)S(1)}, u32[]{:S(2)}, u32[]{:S(2)}) collective-permute-start(f32[16,3,8,128]{3,2,1,0:T(8,128)S(1)} %get-tuple-element.52), channel_id=1, source_target_pairs={{0,192},{64,0},{128,64},{192,128},{1,193},{65,1},{129,65},{193,129... | collective-permute-start | bytes 589832 | tf_op jit(solution)/shard_map/ppermute | solution.py:237
  23.2 29.8 %collective-permute-start.18 = (f32[16,3,8,128]{3,2,1,0:T(8,128)S(1)}, f32[16,3,8,128]{3,2,1,0:T(8,128)S(1)}, u32[]{:S(2)}, u32[]{:S(2)}) collective-permute-start(f32[16,3,8,128]{3,2,1,0:T(8,128)S(1)} %get-tuple-element.66), channel_id=1, source_target_pairs={{0,64},{64,128},{128,192},{192,0},{1,65},{65,129},{129,193},{193,1... | collective-permute-start | bytes 589832 | tf_op jit(solution)/shard_map/ppermute | solution.py:237
  23.2 32.2 %collective-permute-start.19 = (f32[16,3,8,128]{3,2,1,0:T(8,128)S(1)}, f32[16,3,8,128]{3,2,1,0:T(8,128)S(1)}, u32[]{:S(2)}, u32[]{:S(2)}) collective-permute-start(f32[16,3,8,128]{3,2,1,0:T(8,128)S(1)} %get-tuple-element.67), channel_id=1, source_target_pairs={{0,128},{64,192},{128,0},{192,64},{1,129},{65,193},{129,1},{193,65... | collective-permute-start | bytes 589832 | tf_op jit(solution)/shard_map/ppermute | solution.py:237
  32.0 26.9 %collective-permute-start.20 = (f32[16,3,8,128]{3,2,1,0:T(8,128)S(1)}, f32[16,3,8,128]{3,2,1,0:T(8,128)S(1)}, u32[]{:S(2)}, u32[]{:S(2)}) collective-permute-start(f32[16,3,8,128]{3,2,1,0:T(8,128)S(1)} %get-tuple-element.68), channel_id=1, source_target_pairs={{0,192},{64,0},{128,64},{192,128},{1,193},{65,1},{129,65},{193,129... | collective-permute-start | bytes 589832 | tf_op jit(solution)/shard_map/ppermute | solution.py:237
  51.9 9.4 %collective-permute-start.8 = (f32[10,3,8,128]{3,2,1,0:T(8,128)S(1)}, f32[10,3,8,128]{3,2,1,0:T(8,128)S(1)}, u32[]{:S(2)}, u32[]{:S(2)}) collective-permute-start(f32[10,3,8,128]{3,2,1,0:T(8,128)S(1)} %get-tuple-element.54), channel_id=1, source_target_pairs={{0,8},{8,16},{16,24},{24,32},{32,40},{40,48},{48,56},{56,0},{1,9},... | collective-permute-start | bytes 368648 | tf_op jit(solution)/shard_map/ppermute | solution.py:237
  52.4 10.7 %collective-permute-start.9 = (f32[10,3,8,128]{3,2,1,0:T(8,128)S(1)}, f32[10,3,8,128]{3,2,1,0:T(8,128)S(1)}, u32[]{:S(2)}, u32[]{:S(2)}) collective-permute-start(f32[10,3,8,128]{3,2,1,0:T(8,128)S(1)} %get-tuple-element.55), channel_id=1, source_target_pairs={{0,16},{8,24},{16,32},{24,40},{32,48},{40,56},{48,0},{56,8},{1,17}... | collective-permute-start | bytes 368648 | tf_op jit(solution)/shard_map/ppermute | solution.py:237
  53.0 18.7 %collective-permute-start.10 = (f32[10,3,8,128]{3,2,1,0:T(8,128)S(1)}, f32[10,3,8,128]{3,2,1,0:T(8,128)S(1)}, u32[]{:S(2)}, u32[]{:S(2)}) collective-permute-start(f32[10,3,8,128]{3,2,1,0:T(8,128)S(1)} %get-tuple-element.56), channel_id=1, source_target_pairs={{0,24},{8,32},{16,40},{24,48},{32,56},{40,0},{48,8},{56,16},{1,25}... | collective-permute-start | bytes 368648 | tf_op jit(solution)/shard_map/ppermute | solution.py:237
  55.4 16.9 %collective-permute-start.11 = (f32[10,3,8,128]{3,2,1,0:T(8,128)S(1)}, f32[10,3,8,128]{3,2,1,0:T(8,128)S(1)}, u32[]{:S(2)}, u32[]{:S(2)}) collective-permute-start(f32[10,3,8,128]{3,2,1,0:T(8,128)S(1)} %get-tuple-element.57), channel_id=1, source_target_pairs={{0,32},{8,40},{16,48},{24,56},{32,0},{40,8},{48,16},{56,24},{1,33}... | collective-permute-start | bytes 368648 | tf_op jit(solution)/shard_map/ppermute | solution.py:237
  58.9 17.9 %collective-permute-start.12 = (f32[10,3,8,128]{3,2,1,0:T(8,128)S(1)}, f32[10,3,8,128]{3,2,1,0:T(8,128)S(1)}, u32[]{:S(2)}, u32[]{:S(2)}) collective-permute-start(f32[10,3,8,128]{3,2,1,0:T(8,128)S(1)} %get-tuple-element.58), channel_id=1, source_target_pairs={{0,40},{8,48},{16,56},{24,0},{32,8},{40,16},{48,24},{56,32},{1,41}... | collective-permute-start | bytes 368648 | tf_op jit(solution)/shard_map/ppermute | solution.py:237
  61.2 15.6 %collective-permute-start.13 = (f32[10,3,8,128]{3,2,1,0:T(8,128)S(1)}, f32[10,3,8,128]{3,2,1,0:T(8,128)S(1)}, u32[]{:S(2)}, u32[]{:S(2)}) collective-permute-start(f32[10,3,8,128]{3,2,1,0:T(8,128)S(1)} %get-tuple-element.59), channel_id=1, source_target_pairs={{0,48},{8,56},{16,0},{24,8},{32,16},{40,24},{48,32},{56,40},{1,49}... | collective-permute-start | bytes 368648 | tf_op jit(solution)/shard_map/ppermute | solution.py:237
  63.1 17.6 %collective-permute-start.14 = (f32[10,3,8,128]{3,2,1,0:T(8,128)S(1)}, f32[10,3,8,128]{3,2,1,0:T(8,128)S(1)}, u32[]{:S(2)}, u32[]{:S(2)}) collective-permute-start(f32[10,3,8,128]{3,2,1,0:T(8,128)S(1)} %get-tuple-element.60), channel_id=1, source_target_pairs={{0,56},{8,0},{16,8},{24,16},{32,24},{40,32},{48,40},{56,48},{1,57}... | collective-permute-start | bytes 368648 | tf_op jit(solution)/shard_map/ppermute | solution.py:237
  71.7 18.9 %collective-permute-start.21 = (f32[10,3,8,128]{3,2,1,0:T(8,128)S(1)}, f32[10,3,8,128]{3,2,1,0:T(8,128)S(1)}, u32[]{:S(2)}, u32[]{:S(2)}) collective-permute-start(f32[10,3,8,128]{3,2,1,0:T(8,128)S(1)} %get-tuple-element.70), channel_id=1, source_target_pairs={{0,8},{8,16},{16,24},{24,32},{32,40},{40,48},{48,56},{56,0},{1,9},... | collective-permute-start | bytes 368648 | tf_op jit(solution)/shard_map/ppermute | solution.py:237
  72.2 18.4 %collective-permute-start.22 = (f32[10,3,8,128]{3,2,1,0:T(8,128)S(1)}, f32[10,3,8,128]{3,2,1,0:T(8,128)S(1)}, u32[]{:S(2)}, u32[]{:S(2)}) collective-permute-start(f32[10,3,8,128]{3,2,1,0:T(8,128)S(1)} %get-tuple-element.71), channel_id=1, source_target_pairs={{0,16},{8,24},{16,32},{24,40},{32,48},{40,56},{48,0},{56,8},{1,17}... | collective-permute-start | bytes 368648 | tf_op jit(solution)/shard_map/ppermute | solution.py:237
  76.8 16.5 %collective-permute-start.23 = (f32[10,3,8,128]{3,2,1,0:T(8,128)S(1)}, f32[10,3,8,128]{3,2,1,0:T(8,128)S(1)}, u32[]{:S(2)}, u32[]{:S(2)}) collective-permute-start(f32[10,3,8,128]{3,2,1,0:T(8,128)S(1)} %get-tuple-element.72), channel_id=1, source_target_pairs={{0,24},{8,32},{16,40},{24,48},{32,56},{40,0},{48,8},{56,16},{1,25}... | collective-permute-start | bytes 368648 | tf_op jit(solution)/shard_map/ppermute | solution.py:237
  81.9 22.3 %collective-permute-start.15 = (f32[16,3,8,128]{3,2,1,0:T(8,128)S(1)}, f32[16,3,8,128]{3,2,1,0:T(8,128)S(1)}, u32[]{:S(2)}, u32[]{:S(2)}) collective-permute-start(f32[16,3,8,128]{3,2,1,0:T(8,128)S(1)} %get-tuple-element.62), channel_id=1, source_target_pairs={{0,64},{64,128},{128,192},{192,0},{1,65},{65,129},{129,193},{193,1... | collective-permute-start | bytes 589832 | tf_op jit(solution)/shard_map/ppermute | solution.py:237
  84.1 10.7 %collective-permute-start.24 = (f32[10,3,8,128]{3,2,1,0:T(8,128)S(1)}, f32[10,3,8,128]{3,2,1,0:T(8,128)S(1)}, u32[]{:S(2)}, u32[]{:S(2)}) collective-permute-start(f32[10,3,8,128]{3,2,1,0:T(8,128)S(1)} %get-tuple-element.73), channel_id=1, source_target_pairs={{0,32},{8,40},{16,48},{24,56},{32,0},{40,8},{48,16},{56,24},{1,33}... | collective-permute-start | bytes 368648 | tf_op jit(solution)/shard_map/ppermute | solution.py:237
  90.6 7.1 %collective-permute-start.25 = (f32[10,3,8,128]{3,2,1,0:T(8,128)S(1)}, f32[10,3,8,128]{3,2,1,0:T(8,128)S(1)}, u32[]{:S(2)}, u32[]{:S(2)}) collective-permute-start(f32[10,3,8,128]{3,2,1,0:T(8,128)S(1)} %get-tuple-element.74), channel_id=1, source_target_pairs={{0,40},{8,48},{16,56},{24,0},{32,8},{40,16},{48,24},{56,32},{1,41}... | collective-permute-start | bytes 368648 | tf_op jit(solution)/shard_map/ppermute | solution.py:237
  90.6 9.9 %collective-permute-start.26 = (f32[10,3,8,128]{3,2,1,0:T(8,128)S(1)}, f32[10,3,8,128]{3,2,1,0:T(8,128)S(1)}, u32[]{:S(2)}, u32[]{:S(2)}) collective-permute-start(f32[10,3,8,128]{3,2,1,0:T(8,128)S(1)} %get-tuple-element.75), channel_id=1, source_target_pairs={{0,48},{8,56},{16,0},{24,8},{32,16},{40,24},{48,32},{56,40},{1,49}... | collective-permute-start | bytes 368648 | tf_op jit(solution)/shard_map/ppermute | solution.py:237
  93.3 9.4 %collective-permute-start.27 = (f32[10,3,8,128]{3,2,1,0:T(8,128)S(1)}, f32[10,3,8,128]{3,2,1,0:T(8,128)S(1)}, u32[]{:S(2)}, u32[]{:S(2)}) collective-permute-start(f32[10,3,8,128]{3,2,1,0:T(8,128)S(1)} %get-tuple-element.76), channel_id=1, source_target_pairs={{0,56},{8,0},{16,8},{24,16},{32,24},{40,32},{48,40},{56,48},{1,57}... | collective-permute-start | bytes 368648 | tf_op jit(solution)/shard_map/ppermute | solution.py:237
  94.8 12.5 %collective-permute-start.16 = (f32[16,3,8,128]{3,2,1,0:T(8,128)S(1)}, f32[16,3,8,128]{3,2,1,0:T(8,128)S(1)}, u32[]{:S(2)}, u32[]{:S(2)}) collective-permute-start(f32[16,3,8,128]{3,2,1,0:T(8,128)S(1)} %get-tuple-element.63), channel_id=1, source_target_pairs={{0,128},{64,192},{128,0},{192,64},{1,129},{65,193},{129,1},{193,65... | collective-permute-start | bytes 589832 | tf_op jit(solution)/shard_map/ppermute | solution.py:237
  97.7 9.6 %collective-permute-start.17 = (f32[16,3,8,128]{3,2,1,0:T(8,128)S(1)}, f32[16,3,8,128]{3,2,1,0:T(8,128)S(1)}, u32[]{:S(2)}, u32[]{:S(2)}) collective-permute-start(f32[16,3,8,128]{3,2,1,0:T(8,128)S(1)} %get-tuple-element.64), channel_id=1, source_target_pairs={{0,192},{64,0},{128,64},{192,128},{1,193},{65,1},{129,65},{193,129... | collective-permute-start | bytes 589832 | tf_op jit(solution)/shard_map/ppermute | solution.py:237
  104.0 9.1 %collective-permute-start.28 = (f32[16,3,8,128]{3,2,1,0:T(8,128)S(1)}, f32[16,3,8,128]{3,2,1,0:T(8,128)S(1)}, u32[]{:S(2)}, u32[]{:S(2)}) collective-permute-start(f32[16,3,8,128]{3,2,1,0:T(8,128)S(1)} %get-tuple-element.78), channel_id=1, source_target_pairs={{0,64},{64,128},{128,192},{192,0},{1,65},{65,129},{129,193},{193,1... | collective-permute-start | bytes 589832 | tf_op jit(solution)/shard_map/ppermute | solution.py:237
  104.2 8.9 %collective-permute-start.29 = (f32[16,3,8,128]{3,2,1,0:T(8,128)S(1)}, f32[16,3,8,128]{3,2,1,0:T(8,128)S(1)}, u32[]{:S(2)}, u32[]{:S(2)}) collective-permute-start(f32[16,3,8,128]{3,2,1,0:T(8,128)S(1)} %get-tuple-element.79), channel_id=1, source_target_pairs={{0,128},{64,192},{128,0},{192,64},{1,129},{65,193},{129,1},{193,65... | collective-permute-start | bytes 589832 | tf_op jit(solution)/shard_map/ppermute | solution.py:237
  104.2 9.8 %collective-permute-start.30 = (f32[16,3,8,128]{3,2,1,0:T(8,128)S(1)}, f32[16,3,8,128]{3,2,1,0:T(8,128)S(1)}, u32[]{:S(2)}, u32[]{:S(2)}) collective-permute-start(f32[16,3,8,128]{3,2,1,0:T(8,128)S(1)} %get-tuple-element.80), channel_id=1, source_target_pairs={{0,192},{64,0},{128,64},{192,128},{1,193},{65,1},{129,65},{193,129... | collective-permute-start | bytes 589832 | tf_op jit(solution)/shard_map/ppermute | solution.py:237

commit v5 on v4

--- a/solution.py
+++ b/solution.py
@@ -41,7 +41,7 @@
     )
 
 
-def edge_kernel(counts_ref, x_ref, bed_ref, low_ref, high_ref, row_ref):
+def edge_kernel(x_ref, bed_ref, low_ref, high_ref):
     count, fields, rows, _ = x_ref.shape
     for p in range(count):
         for f in range(fields):
@@ -49,19 +49,9 @@
             high_ref[p * fields + f] = x_ref[p, f, 0:2]
     low_ref[count * fields] = bed_ref[rows - 2 : rows]
     high_ref[count * fields] = bed_ref[0:2]
-    lane = lax.broadcasted_iota(jnp.int32, (1, LANES), 1)
-    total = jnp.int32(0)
-    tile = jnp.zeros((1, LANES), jnp.int32)
-    for j in range(count):
-        c = counts_ref[j]
-        total = total + c
-        tile = jnp.where(lane == j, c, tile)
-    tile = jnp.where(lane == count, total, tile)
-    row_ref[...] = tile
-
-
-def evolve_kernel(place_ref, x_ref, low_ref, high_ref, bed_ref, *refs):
-    rows_ref, refs = refs[0:XS], refs[XS:]
+
+
+def evolve_kernel(place_ref, counts_ref, x_ref, low_ref, high_ref, bed_ref, *refs):
     upper, lower = refs[0:XS], refs[XS : 2 * XS]
     row_ref, ext, sx, sy, res = refs[2 * XS :]
     count, fields, rows, cols = x_ref.shape
@@ -94,31 +84,35 @@
         return carry
 
     lax.fori_loop(0, count, body, 0)
-    for z in range(ZS):
-        for k in range(XS):
-            row_ref[z, k : k + 1] = rows_ref[k][...]
-
-
-def plan_kernel(place_ref, row_ref, put_ref, take_ref, base, ctr):
+    lane = lax.broadcasted_iota(jnp.int32, (1, LANES), 1)
+    total = jnp.int32(0)
+    tile = jnp.zeros((1, LANES), jnp.int32)
+    for j in range(count):
+        c = counts_ref[j]
+        total = total + c
+        tile = jnp.where(lane == j, c, tile)
+    tile = jnp.where(lane == count, total, tile)
+    for g in range(XS * ZS):
+        row_ref[g] = tile
+
+
+def send_plan_kernel(place_ref, row_ref, put_ref, base_ref, ctr):
     x, z = place_ref[0], place_ref[1]
-    back = [(x + XS - k) % XS for k in range(XS)]
     total = jnp.int32(0)
-    for at in range(XS):
-        k = (x + XS - at) % XS
-        for zs in range(ZS):
-            base[at * ZS + zs] = total
-            total = total + row_ref[zs, k, 16]
-    base[XS * ZS] = total
+    for g in range(XS * ZS):
+        base_ref[g] = total
+        total = total + row_ref[g, 0, 16]
+    base_ref[XS * ZS] = total
     for i in range(ZS):
         ctr[i] = 0
     for i in range(16 * ZS):
         put_ref[i] = 0
     dump = 16 * ZS
-
-    for k in range(XS):
-        e = base[back[k] * ZS + z]
+    for k in range(XS):
+        group = ((x + XS - k) % XS) * ZS + z
+        e = base_ref[group]
         for j in range(16):
-            c = row_ref[z, k, j]
+            c = row_ref[group, 0, j]
             for i in range(2):
                 to = (e + i - z) & (ZS - 1)
                 t = ctr[to]
@@ -127,13 +121,17 @@
                 put_ref[jnp.where(live, to * 16 + t, dump)] = k * 16 + j
             e = e + c
 
+
+def take_plan_kernel(place_ref, base_ref, take_ref, ctr):
+    x, z = place_ref[0], place_ref[1]
     for i in range(ZS):
         ctr[i] = 0
     dump = 16 * XS
     for k in range(XS):
         for zs in range(ZS):
-            lo = base[back[k] * ZS + zs]
-            hi = base[back[k] * ZS + zs + 1]
+            group = ((x + XS - k) % XS) * ZS + zs
+            lo = base_ref[group]
+            hi = base_ref[group + 1]
             first = lo + ((z - lo) & (ZS - 1))
             t0 = ctr[zs]
             box = ((z - zs) & (ZS - 1)) * 16 + t0
@@ -143,22 +141,31 @@
             ctr[zs] = t0 + jnp.maximum((hi - first + ZS - 1) >> 3, 0)
 
 
-def plan(place, row):
-    return pl.pallas_call(
-        plan_kernel,
+def send_plan(place, row):
+    return pl.pallas_call(
+        send_plan_kernel,
         in_specs=[SMEM, SMEM],
         out_specs=[SMEM, SMEM],
         out_shape=[
             jax.ShapeDtypeStruct((16 * ZS + 8,), jnp.int32),
-            jax.ShapeDtypeStruct((16 * XS + 8,), jnp.int32),
+            jax.ShapeDtypeStruct((XS * ZS + 8,), jnp.int32),
         ],
-        scratch_shapes=[
-            pltpu.SMEM((XS * ZS + 1,), jnp.int32),
-            pltpu.SMEM((ZS,), jnp.int32),
-        ],
+        scratch_shapes=[pltpu.SMEM((ZS,), jnp.int32)],
         compiler_params=PARAMS,
         cost_estimate=pl.CostEstimate(flops=0, bytes_accessed=4_000_000, transcendentals=0),
     )(place, row)
+
+
+def take_plan(place, base):
+    return pl.pallas_call(
+        take_plan_kernel,
+        in_specs=[SMEM, SMEM],
+        out_specs=SMEM,
+        out_shape=jax.ShapeDtypeStruct((16 * XS + 8,), jnp.int32),
+        scratch_shapes=[pltpu.SMEM((ZS,), jnp.int32)],
+        compiler_params=PARAMS,
+        cost_estimate=pl.CostEstimate(flops=0, bytes_accessed=4_000_000, transcendentals=0),
+    )(place, base)
 
 
 def pick(parts, code):
@@ -191,6 +198,57 @@
     )(put, *data)
 
 
+def pack_whole_kernel(place_ref, put_ref, *refs):
+    data, out = refs[0:XS], refs[XS]
+    z = place_ref[1]
+    for k in range(ZS):
+        to = (z + k) & (ZS - 1)
+
+        def body(t, carry):
+            out[to, t] = pick(data, put_ref[k * 16 + t])
+            return carry
+
+        lax.fori_loop(0, BOXES, body, 0, unroll=5)
+
+
+def pack_whole(place, put, data):
+    return pl.pallas_call(
+        pack_whole_kernel,
+        in_specs=[SMEM] * 2 + [VMEM] * XS,
+        out_specs=VMEM,
+        out_shape=jax.ShapeDtypeStruct((ZS, BOXES, 3, 8, LANES), F32),
+        compiler_params=PARAMS,
+        cost_estimate=pl.CostEstimate(flops=0, bytes_accessed=3_000_000, transcendentals=0),
+    )(place, put, *data)
+
+
+def spread_whole_kernel(place_ref, take_ref, boxes, *outs):
+    x, z = place_ref[0], place_ref[1]
+    for i in range(16 * XS):
+        outs[XS][i] = take_ref[i]
+    for k in range(XS):
+        to = (x + k) % XS
+
+        def body(i, carry):
+            code = take_ref[i * XS + to]
+            outs[k][i] = boxes[(z - (code >> 4)) & (ZS - 1), code & 15]
+            return carry
+
+        lax.fori_loop(0, 16, body, 0, unroll=4)
+
+
+def spread_whole(place, take, boxes):
+    return pl.pallas_call(
+        spread_whole_kernel,
+        in_specs=[SMEM, SMEM, VMEM],
+        out_specs=[VMEM] * XS + [SMEM],
+        out_shape=[jax.ShapeDtypeStruct((16, 3, 8, LANES), F32)] * XS
+        + [jax.ShapeDtypeStruct((16 * XS,), jnp.int32)],
+        compiler_params=PARAMS,
+        cost_estimate=pl.CostEstimate(flops=0, bytes_accessed=3_000_000, transcendentals=0),
+    )(place, take, boxes)
+
+
 def spread_kernel(place_ref, take_ref, *refs):
     boxes, outs = refs[0:ZS], refs[ZS:]
     x = place_ref[0]
@@ -242,23 +300,22 @@
     count, fields, rows, cols = particles.shape
     place = jnp.stack([lax.axis_index("x"), lax.axis_index("z")]).astype(jnp.int32)
     edges = jax.ShapeDtypeStruct((count * fields + 1, 2, cols), F32)
-    low, high, row = pl.pallas_call(
+    low, high = pl.pallas_call(
         edge_kernel,
-        in_specs=[SMEM, VMEM, VMEM],
-        out_specs=[VMEM] * 3,
-        out_shape=[edges, edges, jax.ShapeDtypeStruct((1, LANES), jnp.int32)],
-        compiler_params=PARAMS,
-    )(counts, particles, bed)
+        in_specs=[VMEM, VMEM],
+        out_specs=[VMEM] * 2,
+        out_shape=[edges, edges],
+        compiler_params=PARAMS,
+    )(particles, bed)
     strips = lax.axis_size("space")
     low = lax.ppermute(low, "space", [(i, (i + 1) % strips) for i in range(strips)])
     high = lax.ppermute(high, "space", [((i + 1) % strips, i) for i in range(strips)])
-    known = along("x", [row] * XS)
     half = jax.ShapeDtypeStruct((count, fields, 8, LANES), F32)
     *parts, row = pl.pallas_call(
         evolve_kernel,
-        in_specs=[SMEM] + [VMEM] * (4 + XS),
+        in_specs=[SMEM] * 2 + [VMEM] * 4,
         out_specs=[VMEM] * (2 * XS + 1),
-        out_shape=[half] * (2 * XS) + [jax.ShapeDtypeStruct((ZS, XS, LANES), jnp.int32)],
+        out_shape=[half] * (2 * XS) + [jax.ShapeDtypeStruct((XS * ZS, 1, LANES), jnp.int32)],
         scratch_shapes=[
             pltpu.VMEM((fields, rows + 8, cols), F32),
             pltpu.VMEM((rows + 8, cols), F32),
@@ -267,14 +324,16 @@
         ],
         compiler_params=PARAMS,
         cost_estimate=pl.CostEstimate(flops=0, bytes_accessed=20_000_000, transcendentals=0),
-    )(place, particles, low, high, bed, *known)
+    )(place, counts, particles, low, high, bed)
     upper = along("x", parts[:XS])
-    row = lax.all_to_all(row, "z", 0, 0, tiled=True)
+    row = lax.all_to_all(row, ("x", "z"), 0, 0, tiled=True)
     lower = along("x", parts[XS:])
-    put, take = plan(place, row)
-    boxes_a = along("z", pack(put, upper))
+    put, base = send_plan(place, row)
+    boxes_a = lax.all_to_all(pack_whole(place, put, upper), "z", 0, 0, tiled=True)
     boxes_b = along("z", pack(put, lower))
-    out_a = along("x", spread(place, take, boxes_a))
+    take = take_plan(place, base)
+    *out_a, take = spread_whole(place, take, boxes_a)
+    out_a = along("x", out_a)
     out_b = along("x", spread(place, take, boxes_b))
     return pl.pallas_call(
         join_kernel,

time: 116 us -> 113 us (0.974)
  starting transfers between devices: 46.1 us -> 37.6 us
  blocking collectives: 16.2 us -> 18.5 us
  Pallas kernels: 15.1 us -> 16.8 us
  waiting for transfers between devices: 35.4 us -> 36.9 us
    ppermute x29 -> x19, starting transfers between devices: 44.3 us -> 32.3 us  [along(): lax.ppermute(parts[k], axis, [(i, (i + k) % n) for i in range(n)])]
    ppermute x29 -> x19, waiting for transfers between devices: 35.4 us -> 28 us  [along(): lax.ppermute(parts[k], axis, [(i, (i + k) % n) for i in range(n)])]
    all_to_all x0 -> x1, waiting for transfers between devices: none -> 5.59 us  [per_device(): lax.all_to_all(pack_whole(place, put, upper), 'z', 0, 0, tiled=True)]
    pallas_call x3 -> x6, Pallas kernels: 8.6 us -> 12.5 us  [the longest x1 5.46 us: per_device(): pl.pallas_call(evolve_kernel, in_specs=[SMEM] * 2 + [VMEM] * 4, out_specs...]
    all_to_all x0 -> x1, starting transfers between devices: none -> 3.56 us  [per_device(): lax.all_to_all(pack_whole(place, put, upper), 'z', 0, 0, tiled=True)]
    ppermute x1, waiting for transfers between devices: 0.01 us -> 3.32 us  [per_device(): lax.ppermute(low, 'space', [(i, (i + 1) % strips) for i in range(strips)])]
    all_to_all x1, blocking collectives: 16.2 us -> 18.5 us  [per_device(): row = lax.all_to_all(row, ('x', 'z'), 0, 0, tiled=True)]
    pallas_call x2 -> x1, Pallas kernels: 2.48 us -> 1.24 us  [spread(): pl.pallas_call(spread_kernel, in_specs=[SMEM, SMEM] + [VMEM] * ZS, out_sp...]
  transfers between devices with their start and end apart: 31 -> 22, of which waited for: 11 -> 12; matrix products, arithmetic and copies ran while one was open for 0% -> 0% of each run, Pallas kernels for 6% -> 7%
where the time goes in v5:
time: 113 us; the launch traced here: 112 us
  starting transfers between devices  37.6 us (33%)
  waiting for transfers between devices  36.9 us (33%)
  blocking collectives  18.5 us (16%)
  Pallas kernels  16.8 us (15%)
  local copies, waits for them, and re-layouts  2.18 us (2%)
    ppermute x19, starting transfers between devices, along(): lax.ppermute(parts[k], axis, [(i, (i + k) % n) for i in range(n)])  32.3 us
    ppermute x19, waiting for transfers between devices, along(): lax.ppermute(parts[k], axis, [(i, (i + k) % n) for i in range(n)])  28 us
    all_to_all x1, blocking collectives, per_device(): row = lax.all_to_all(row, ('x', 'z'), 0, 0, tiled=True)  18.5 us
    all_to_all x1, waiting for transfers between devices, per_device(): lax.all_to_all(pack_whole(place, put, upper), 'z', 0, 0, tiled=True)  5.59 us
    pallas_call x1, Pallas kernels, per_device(): pl.pallas_call(evolve_kernel, in_specs=[SMEM] * 2 + [VMEM] * 4, out_specs...  5.46 us
    all_to_all x1, starting transfers between devices, per_device(): lax.all_to_all(pack_whole(place, put, upper), 'z', 0, 0, tiled=True)  3.56 us
    ppermute x1, waiting for transfers between devices, per_device(): lax.ppermute(low, 'space', [(i, (i + 1) % strips) for i in range(strips)])  3.32 us
  transfers between devices with their start and end apart: 22, of which 12 were waited for; matrix products, arithmetic and copies ran while one was open for 0% of the time, Pallas kernels for 7%

profile of v5, /device:TPU:16, one launch (start us, length us, event | category | flops | bytes accessed | tf_op | source)
XLA Modules:
  0.0 112.1 jit_solution(2220041708982867684)
XLA Ops:
  0.0 0.0 copy-start
  0.0 1.4 %copy-done = f32[16,3,16,512]{3,2,1,0:T(8,128)S(1)} copy-done((f32[16,3,16,512]{3,2,1,0:T(8,128)S(1)}, f32[16,3,16,512]{3,2,1,0:T(8,128)}, u32[]{:S(2)}) %copy-start) | copy-done | bytes 1572888
  1.4 0.0 copy-start.2
  1.4 0.8 copy-done.2
  2.2 0.0 copy-start.1
  2.2 0.0 copy-start.3
  2.2 0.1 shard_map.37
  2.3 0.0 collective-permute-start
  2.3 1.7 %collective-permute-start.1 = (f32[49,2,512]{2,1,0:T(2,128)S(1)}, f32[49,2,512]{2,1,0:T(2,128)S(1)}, u32[]{:S(2)}, u32[]{:S(2)}) collective-permute-start(f32[49,2,512]{2,1,0:T(2,128)S(1)} %get-tuple-element.36), channel_id=1, source_target_pairs={{1,0},{2,1},{3,2},{4,3},{5,4},{6,5},{7,6},{0,7},{9,8},{10,9},{11,1... | collective-permute-start | bytes 602120 | tf_op jit(solution)/shard_map/ppermute | solution.py:312
  4.0 0.1 pad_add_fusion.place_ref
  4.1 3.3 %collective-permute-done.low_ref = f32[49,2,512]{2,1,0:T(2,128)S(1)} collective-permute-done((f32[49,2,512]{2,1,0:T(2,128)S(1)}, f32[49,2,512]{2,1,0:T(2,128)S(1)}, u32[]{:S(2)}, u32[]{:S(2)}) %collective-permute-start) | collective-permute-done | bytes 200736 | tf_op jit(solution)/shard_map/ppermute | solution.py:311
  7.4 0.0 collective-permute-done.1.high_ref
  7.4 0.0 copy-done.1
  7.4 0.0 copy-done.3
  7.4 0.0 copy-done.4
  7.4 5.5 %shard_map.38 = (f32[16,3,8,128]{3,2,1,0:T(8,128)S(1)}, f32[16,3,8,128]{3,2,1,0:T(8,128)S(1)}, f32[16,3,8,128]{3,2,1,0:T(8,128)S(1)}, f32[16,3,8,128]{3,2,1,0:T(...) custom-call(s32[2]{0:T(128)S(1)} %pad_add_fusion.place_ref, ...), custom_call_target="tpu_custom_call" | custom-call | bytes 20000000 | tf_op jit(solution)/shard_map/pallas_call | solution.py:314
  12.9 1.5 %collective-permute-start.2 = (f32[16,3,8,128]{3,2,1,0:T(8,128)S(1)}, f32[16,3,8,128]{3,2,1,0:T(8,128)S(1)}, u32[]{:S(2)}, u32[]{:S(2)}) collective-permute-start(f32[16,3,8,128]{3,2,1,0:T(8,128)S(1)} %get-tuple-element.41), channel_id=1, source_target_pairs={{0,64},{64,128},{128,192},{192,0},{1,65},{65,129},{129,193},{193,1... | collective-permute-start | bytes 589832 | tf_op jit(solution)/shard_map/ppermute | solution.py:295
  14.4 2.8 %collective-permute-start.3 = (f32[16,3,8,128]{3,2,1,0:T(8,128)S(1)}, f32[16,3,8,128]{3,2,1,0:T(8,128)S(1)}, u32[]{:S(2)}, u32[]{:S(2)}) collective-permute-start(f32[16,3,8,128]{3,2,1,0:T(8,128)S(1)} %get-tuple-element.42), channel_id=1, source_target_pairs={{0,128},{64,192},{128,0},{192,64},{1,129},{65,193},{129,1},{193,65... | collective-permute-start | bytes 589832 | tf_op jit(solution)/shard_map/ppermute | solution.py:295
  17.2 1.4 %collective-permute-start.4 = (f32[16,3,8,128]{3,2,1,0:T(8,128)S(1)}, f32[16,3,8,128]{3,2,1,0:T(8,128)S(1)}, u32[]{:S(2)}, u32[]{:S(2)}) collective-permute-start(f32[16,3,8,128]{3,2,1,0:T(8,128)S(1)} %get-tuple-element.43), channel_id=1, source_target_pairs={{0,192},{64,0},{128,64},{192,128},{1,193},{65,1},{129,65},{193,129... | collective-permute-start | bytes 589832 | tf_op jit(solution)/shard_map/ppermute | solution.py:295
  18.6 18.5 %all_to_all.10.row_ref = s32[32,1,128]{2,1,0:T(1,128)S(1)} all-to-all(s32[32,1,128]{2,1,0:T(1,128)S(1)} %get-tuple-element.37), channel_id=1, replica_groups=mesh['x'=4,'z'=8,'space'=8] {'x','z'}, dimensions={0} | all-to-all | bytes 32768 | tf_op jit(solution)/shard_map/all_to_all | solution.py:329
  37.1 2.1 %shard_map.39 = (s32[136]{0:T(256)S(1)}, s32[40]{0:T(128)S(1)}) custom-call(s32[2]{0:T(128)S(1)} %pad_add_fusion.place_ref, s32[32,1,128]{2,1,0:T(1,128)S(1)} %all_to_all.10.row_ref), custom_call_target="tpu_custom_call" | custom-call | bytes 4000000 | tf_op jit(solution)/shard_map/pallas_call | solution.py:145
  39.2 0.0 collective-permute-done.2.refs_1_
  39.2 0.0 collective-permute-done.3.refs_2_
  39.2 0.0 collective-permute-done.4.refs_3_
  39.2 2.0 %shard_map.41 = f32[8,10,3,8,128]{4,3,2,1,0:T(8,128)} custom-call(s32[2]{0:T(128)S(1)} %pad_add_fusion.place_ref, s32[136]{0:T(256)S(1)} %get-tuple-element.39.put_ref, f32[16,3,8,128]{3,2,1,0:T(8,128)S(1)} %get-tuple-element.40.refs_0_, f32[16,3,8,128]{3,2,1,0:T(8,128)S(1)} %collective-permute-done.2.refs_1_, ...), custom_call_target="tpu_custom_call" | custom-call | bytes 3000000 | tf_op jit(solution)/shard_map/pallas_call | solution.py:215
  41.2 3.6 %all-to-all-start.1 = ((f32[8,10,3,8,128]{4,3,2,1,0:T(8,128)}), f32[8,10,3,8,128]{4,3,2,1,0:T(8,128)S(1)}, u32[]{:S(2)}, u32[]{:S(2)}) async-start(f32[8,10,3,8,128]{4,3,2,1,0:T(8,128)} %shard_map.41), calls=%async_computation.1 | async-start | bytes 1966080 | tf_op jit(solution)/shard_map/all_to_all | solution.py:332
  44.8 0.7 collective-permute-start.8
  45.5 2.0 %collective-permute-start.9 = (f32[16,3,8,128]{3,2,1,0:T(8,128)S(1)}, f32[16,3,8,128]{3,2,1,0:T(8,128)S(1)}, u32[]{:S(2)}, u32[]{:S(2)}) collective-permute-start(f32[16,3,8,128]{3,2,1,0:T(8,128)S(1)} %get-tuple-element.51), channel_id=1, source_target_pairs={{0,128},{64,192},{128,0},{192,64},{1,129},{65,193},{129,1},{193,65... | collective-permute-start | bytes 589832 | tf_op jit(solution)/shard_map/ppermute | solution.py:295
  47.5 1.2 %collective-permute-start.10 = (f32[16,3,8,128]{3,2,1,0:T(8,128)S(1)}, f32[16,3,8,128]{3,2,1,0:T(8,128)S(1)}, u32[]{:S(2)}, u32[]{:S(2)}) collective-permute-start(f32[16,3,8,128]{3,2,1,0:T(8,128)S(1)} %get-tuple-element.52), channel_id=1, source_target_pairs={{0,192},{64,0},{128,64},{192,128},{1,193},{65,1},{129,65},{193,129... | collective-permute-start | bytes 589832 | tf_op jit(solution)/shard_map/ppermute | solution.py:295
  48.7 7.5 %collective-permute-done.8.refs_1_ = f32[16,3,8,128]{3,2,1,0:T(8,128)S(1)} collective-permute-done((f32[16,3,8,128]{3,2,1,0:T(8,128)S(1)}, f32[16,3,8,128]{3,2,1,0:T(8,128)S(1)}, u32[]{:S(2)}, u32[]{:S(2)}) %collective-permute-start.8) | collective-permute-done | bytes 196640 | tf_op jit(solution)/shard_map/ppermute | solution.py:295
  56.2 0.0 collective-permute-done.9.refs_2_
  56.2 0.6 collective-permute-done.10.refs_3_
  56.8 1.1 shard_map.43
  57.9 1.6 %collective-permute-start.11 = (f32[10,3,8,128]{3,2,1,0:T(8,128)S(1)}, f32[10,3,8,128]{3,2,1,0:T(8,128)S(1)}, u32[]{:S(2)}, u32[]{:S(2)}) collective-permute-start(f32[10,3,8,128]{3,2,1,0:T(8,128)S(1)} %get-tuple-element.54), channel_id=1, source_target_pairs={{0,8},{8,16},{16,24},{24,32},{32,40},{40,48},{48,56},{56,0},{1,9},... | collective-permute-start | bytes 368648 | tf_op jit(solution)/shard_map/ppermute | solution.py:295
  59.5 2.4 %collective-permute-start.12 = (f32[10,3,8,128]{3,2,1,0:T(8,128)S(1)}, f32[10,3,8,128]{3,2,1,0:T(8,128)S(1)}, u32[]{:S(2)}, u32[]{:S(2)}) collective-permute-start(f32[10,3,8,128]{3,2,1,0:T(8,128)S(1)} %get-tuple-element.55), channel_id=1, source_target_pairs={{0,16},{8,24},{16,32},{24,40},{32,48},{40,56},{48,0},{56,8},{1,17}... | collective-permute-start | bytes 368648 | tf_op jit(solution)/shard_map/ppermute | solution.py:295
  61.9 2.7 %collective-permute-start.13 = (f32[10,3,8,128]{3,2,1,0:T(8,128)S(1)}, f32[10,3,8,128]{3,2,1,0:T(8,128)S(1)}, u32[]{:S(2)}, u32[]{:S(2)}) collective-permute-start(f32[10,3,8,128]{3,2,1,0:T(8,128)S(1)} %get-tuple-element.56), channel_id=1, source_target_pairs={{0,24},{8,32},{16,40},{24,48},{32,56},{40,0},{48,8},{56,16},{1,25}... | collective-permute-start | bytes 368648 | tf_op jit(solution)/shard_map/ppermute | solution.py:295
  64.6 1.5 %shard_map.40.take_ref = s32[72]{0:T(128)S(1)} custom-call(s32[2]{0:T(128)S(1)} %pad_add_fusion.place_ref, s32[40]{0:T(128)S(1)} %get-tuple-element.38.base_ref), custom_call_target="tpu_custom_call" | custom-call | bytes 4000000 | tf_op jit(solution)/shard_map/pallas_call | solution.py:160
  66.1 5.6 %all-to-all-done.1.boxes = f32[8,10,3,8,128]{4,3,2,1,0:T(8,128)S(1)} async-done(((f32[8,10,3,8,128]{4,3,2,1,0:T(8,128)}), f32[8,10,3,8,128]{4,3,2,1,0:T(8,128)S(1)}, u32[]{:S(2)}, u32[]{:S(2)}) %all-to-all-start.1) | async-done | bytes 983072 | tf_op jit(solution)/shard_map/all_to_all | solution.py:332
  71.7 1.4 %shard_map.42 = (f32[16,3,8,128]{3,2,1,0:T(8,128)S(1)}, f32[16,3,8,128]{3,2,1,0:T(8,128)S(1)}, f32[16,3,8,128]{3,2,1,0:T(8,128)S(1)}, f32[16,3,8,128]{3,2,1,0:T(8,128)S(1)}, s32[64]{0:T(128)S(1)}) custom-call(s32[2]{0:T(128)S(1)} %pad_add_fusion.place_ref, s32[72]{0:T(128)S(1)} %shard_map.40.take_ref, f32[8,10,3,8,128]{4,3,2,1,0:T(8,128)S(1)} %all-to-all-done.1.boxes), custom_call_target="tpu_custom_call" | custom-call | bytes 3000000 | tf_op jit(solution)/shard_map/pallas_call | solution.py:241
  73.1 0.7 collective-permute-start.5
  73.8 1.8 %collective-permute-start.14 = (f32[10,3,8,128]{3,2,1,0:T(8,128)S(1)}, f32[10,3,8,128]{3,2,1,0:T(8,128)S(1)}, u32[]{:S(2)}, u32[]{:S(2)}) collective-permute-start(f32[10,3,8,128]{3,2,1,0:T(8,128)S(1)} %get-tuple-element.57), channel_id=1, source_target_pairs={{0,32},{8,40},{16,48},{24,56},{32,0},{40,8},{48,16},{56,24},{1,33}... | collective-permute-start | bytes 368648 | tf_op jit(solution)/shard_map/ppermute | solution.py:295
  75.6 0.0 collective-permute-done.11.refs_1_
  75.6 3.2 %collective-permute-start.15 = (f32[10,3,8,128]{3,2,1,0:T(8,128)S(1)}, f32[10,3,8,128]{3,2,1,0:T(8,128)S(1)}, u32[]{:S(2)}, u32[]{:S(2)}) collective-permute-start(f32[10,3,8,128]{3,2,1,0:T(8,128)S(1)} %get-tuple-element.58), channel_id=1, source_target_pairs={{0,40},{8,48},{16,56},{24,0},{32,8},{40,16},{48,24},{56,32},{1,41}... | collective-permute-start | bytes 368648 | tf_op jit(solution)/shard_map/ppermute | solution.py:295
  78.8 0.4 collective-permute-done.12.refs_2_
  79.1 2.0 %collective-permute-start.16 = (f32[10,3,8,128]{3,2,1,0:T(8,128)S(1)}, f32[10,3,8,128]{3,2,1,0:T(8,128)S(1)}, u32[]{:S(2)}, u32[]{:S(2)}) collective-permute-start(f32[10,3,8,128]{3,2,1,0:T(8,128)S(1)} %get-tuple-element.59), channel_id=1, source_target_pairs={{0,48},{8,56},{16,0},{24,8},{32,16},{40,24},{48,32},{56,40},{1,49}... | collective-permute-start | bytes 368648 | tf_op jit(solution)/shard_map/ppermute | solution.py:295
  81.2 5.5 %collective-permute-done.13.refs_3_ = f32[10,3,8,128]{3,2,1,0:T(8,128)S(1)} collective-permute-done((f32[10,3,8,128]{3,2,1,0:T(8,128)S(1)}, f32[10,3,8,128]{3,2,1,0:T(8,128)S(1)}, u32[]{:S(2)}, u32[]{:S(2)}) %collective-permute-start.13) | collective-permute-done | bytes 122912 | tf_op jit(solution)/shard_map/ppermute | solution.py:295
  86.6 0.0 collective-permute-start.17
  86.6 3.8 %collective-permute-done.14.refs_4_ = f32[10,3,8,128]{3,2,1,0:T(8,128)S(1)} collective-permute-done((f32[10,3,8,128]{3,2,1,0:T(8,128)S(1)}, f32[10,3,8,128]{3,2,1,0:T(8,128)S(1)}, u32[]{:S(2)}, u32[]{:S(2)}) %collective-permute-start.14) | collective-permute-done | bytes 122912 | tf_op jit(solution)/shard_map/ppermute | solution.py:295
  90.4 1.3 %collective-permute-start.6 = (f32[16,3,8,128]{3,2,1,0:T(8,128)S(1)}, f32[16,3,8,128]{3,2,1,0:T(8,128)S(1)}, u32[]{:S(2)}, u32[]{:S(2)}) collective-permute-start(f32[16,3,8,128]{3,2,1,0:T(8,128)S(1)} %get-tuple-element.46), channel_id=1, source_target_pairs={{0,128},{64,192},{128,0},{192,64},{1,129},{65,193},{129,1},{193,65... | collective-permute-start | bytes 589832 | tf_op jit(solution)/shard_map/ppermute | solution.py:295
  91.8 0.0 collective-permute-done.15.refs_5_
  91.8 2.0 %collective-permute-start.7 = (f32[16,3,8,128]{3,2,1,0:T(8,128)S(1)}, f32[16,3,8,128]{3,2,1,0:T(8,128)S(1)}, u32[]{:S(2)}, u32[]{:S(2)}) collective-permute-start(f32[16,3,8,128]{3,2,1,0:T(8,128)S(1)} %get-tuple-element.47), channel_id=1, source_target_pairs={{0,192},{64,0},{128,64},{192,128},{1,193},{65,1},{129,65},{193,129... | collective-permute-start | bytes 589832 | tf_op jit(solution)/shard_map/ppermute | solution.py:295
  93.7 0.0 collective-permute-done.16.refs_6_
  93.7 0.4 collective-permute-done.17.refs_7_
  94.1 1.2 %shard_map.44 = (f32[16,3,8,128]{3,2,1,0:T(8,128)S(1)}, f32[16,3,8,128]{3,2,1,0:T(8,128)S(1)}, f32[16,3,8,128]{3,2,1,0:T(8,128)S(1)}, f32[16,3,8,128]{3,2,1,0:T(8,128)S(1)}) custom-call(s32[2]{0:T(128)S(1)} %pad_add_fusion.place_ref, s32[64]{0:T(128)S(1)} %get-tuple-element.48.take_ref, f32[10,3,8,128]{3,2,1,0:T(8,128)S(1)} %get-tuple-element.53.refs_0_, ...), custom_call_target="tpu_custom_call" | custom-call | bytes 3000000 | tf_op jit(solution)/shard_map/pallas_call | solution.py:267
  95.4 0.7 collective-permute-start.18
  96.0 3.5 %collective-permute-start.19 = (f32[16,3,8,128]{3,2,1,0:T(8,128)S(1)}, f32[16,3,8,128]{3,2,1,0:T(8,128)S(1)}, u32[]{:S(2)}, u32[]{:S(2)}) collective-permute-start(f32[16,3,8,128]{3,2,1,0:T(8,128)S(1)} %get-tuple-element.63), channel_id=1, source_target_pairs={{0,128},{64,192},{128,0},{192,64},{1,129},{65,193},{129,1},{193,65... | collective-permute-start | bytes 589832 | tf_op jit(solution)/shard_map/ppermute | solution.py:295
  99.6 0.0 collective-permute-done.5.refs_1_
  99.6 0.8 collective-permute-start.20
  100.4 0.0 collective-permute-done.6.refs_2_
  100.4 2.3 %collective-permute-done.7.refs_3_ = f32[16,3,8,128]{3,2,1,0:T(8,128)S(1)} collective-permute-done((f32[16,3,8,128]{3,2,1,0:T(8,128)S(1)}, f32[16,3,8,128]{3,2,1,0:T(8,128)S(1)}, u32[]{:S(2)}, u32[]{:S(2)}) %collective-permute-start.7) | collective-permute-done | bytes 196640 | tf_op jit(solution)/shard_map/ppermute | solution.py:295
  102.7 2.9 %collective-permute-done.18.refs_5_ = f32[16,3,8,128]{3,2,1,0:T(8,128)S(1)} collective-permute-done((f32[16,3,8,128]{3,2,1,0:T(8,128)S(1)}, f32[16,3,8,128]{3,2,1,0:T(8,128)S(1)}, u32[]{:S(2)}, u32[]{:S(2)}) %collective-permute-start.18) | collective-permute-done | bytes 196640 | tf_op jit(solution)/shard_map/ppermute | solution.py:295
  105.6 1.6 %collective-permute-done.19.refs_6_ = f32[16,3,8,128]{3,2,1,0:T(8,128)S(1)} collective-permute-done((f32[16,3,8,128]{3,2,1,0:T(8,128)S(1)}, f32[16,3,8,128]{3,2,1,0:T(8,128)S(1)}, u32[]{:S(2)}, u32[]{:S(2)}) %collective-permute-start.19) | collective-permute-done | bytes 196640 | tf_op jit(solution)/shard_map/ppermute | solution.py:295
  107.2 2.9 %collective-permute-done.20.refs_7_ = f32[16,3,8,128]{3,2,1,0:T(8,128)S(1)} collective-permute-done((f32[16,3,8,128]{3,2,1,0:T(8,128)S(1)}, f32[16,3,8,128]{3,2,1,0:T(8,128)S(1)}, u32[]{:S(2)}, u32[]{:S(2)}) %collective-permute-start.20) | collective-permute-done | bytes 196640 | tf_op jit(solution)/shard_map/ppermute | solution.py:295
  110.2 1.9 %shard_map.45 = f32[16,3,16,512]{3,2,1,0:T(8,128)} custom-call(s32[2]{0:T(128)S(1)} %pad_add_fusion.place_ref, f32[16,3,8,128]{3,2,1,0:T(8,128)S(1)} %get-tuple-element.44.refs_0_, f32[16,3,8,128]{3,2,1,0:T(8,128)S(1)} %collective-permute-done.5.refs_1_, f32[16,3,8,128]{3,2,1,0:T(8,128)S(1)} %collective-permute-done.6.refs_2_, ...), custom_call_target="tpu_custom_call" | custom-call | tf_op jit(solution)/shard_map/pallas_call | solution.py:338
  (1 shorter events, 0.0 us)
Async XLA Ops:
  0.0 1.4 %copy-start = (f32[16,3,16,512]{3,2,1,0:T(8,128)S(1)}, f32[16,3,16,512]{3,2,1,0:T(8,128)}, u32[]{:S(2)}) copy-start(f32[16,3,16,512]{3,2,1,0:T(8,128)} %x_ref.3) | copy-start | bytes 4718596
  1.4 0.8 copy-start.2
  2.2 5.2 %copy-start.1 = (f32[16,3,16,512]{3,2,1,0:T(8,128)S(1)}, f32[16,3,16,512]{3,2,1,0:T(8,128)}, u32[]{:S(2)}) copy-start(f32[16,3,16,512]{3,2,1,0:T(8,128)} %x_ref.3) | copy-start | bytes 4718596
  2.2 5.2 %copy-start.3 = (f32[16,512]{1,0:T(8,128)S(1)}, f32[16,512]{1,0:T(8,128)}, u32[]{:S(2)}) copy-start(f32[16,512]{1,0:T(8,128)} %bed_ref.3) | copy-start | bytes 98308
  2.2 5.2 %copy-start.4 = (s32[16]{0:T(128)S(1)}, s32[16]{0:T(128)}, u32[]{:S(2)}) copy-start(s32[16]{0:T(128)} %counts_ref.1) | copy-start | bytes 196
  2.3 5.2 %collective-permute-start = (f32[49,2,512]{2,1,0:T(2,128)S(1)}, f32[49,2,512]{2,1,0:T(2,128)S(1)}, u32[]{:S(2)}, u32[]{:S(2)}) collective-permute-start(f32[49,2,512]{2,1,0:T(2,128)S(1)} %get-tuple-element.35), channel_id=1, source_target_pairs={{0,1},{1,2},{2,3},{3,4},{4,5},{5,6},{6,7},{7,0},{8,9},{9,10},{10,1... | collective-permute-start | bytes 602120 | tf_op jit(solution)/shard_map/ppermute | solution.py:311
  2.3 5.1 %collective-permute-start.1 = (f32[49,2,512]{2,1,0:T(2,128)S(1)}, f32[49,2,512]{2,1,0:T(2,128)S(1)}, u32[]{:S(2)}, u32[]{:S(2)}) collective-permute-start(f32[49,2,512]{2,1,0:T(2,128)S(1)} %get-tuple-element.36), channel_id=1, source_target_pairs={{1,0},{2,1},{3,2},{4,3},{5,4},{6,5},{7,6},{0,7},{9,8},{10,9},{11,1... | collective-permute-start | bytes 602120 | tf_op jit(solution)/shard_map/ppermute | solution.py:312
  12.9 26.3 %collective-permute-start.2 = (f32[16,3,8,128]{3,2,1,0:T(8,128)S(1)}, f32[16,3,8,128]{3,2,1,0:T(8,128)S(1)}, u32[]{:S(2)}, u32[]{:S(2)}) collective-permute-start(f32[16,3,8,128]{3,2,1,0:T(8,128)S(1)} %get-tuple-element.41), channel_id=1, source_target_pairs={{0,64},{64,128},{128,192},{192,0},{1,65},{65,129},{129,193},{193,1... | collective-permute-start | bytes 589832 | tf_op jit(solution)/shard_map/ppermute | solution.py:295
  14.4 24.8 %collective-permute-start.3 = (f32[16,3,8,128]{3,2,1,0:T(8,128)S(1)}, f32[16,3,8,128]{3,2,1,0:T(8,128)S(1)}, u32[]{:S(2)}, u32[]{:S(2)}) collective-permute-start(f32[16,3,8,128]{3,2,1,0:T(8,128)S(1)} %get-tuple-element.42), channel_id=1, source_target_pairs={{0,128},{64,192},{128,0},{192,64},{1,129},{65,193},{129,1},{193,65... | collective-permute-start | bytes 589832 | tf_op jit(solution)/shard_map/ppermute | solution.py:295
  17.2 22.0 %collective-permute-start.4 = (f32[16,3,8,128]{3,2,1,0:T(8,128)S(1)}, f32[16,3,8,128]{3,2,1,0:T(8,128)S(1)}, u32[]{:S(2)}, u32[]{:S(2)}) collective-permute-start(f32[16,3,8,128]{3,2,1,0:T(8,128)S(1)} %get-tuple-element.43), channel_id=1, source_target_pairs={{0,192},{64,0},{128,64},{192,128},{1,193},{65,1},{129,65},{193,129... | collective-permute-start | bytes 589832 | tf_op jit(solution)/shard_map/ppermute | solution.py:295
  41.2 30.5 %all-to-all-start.1 = ((f32[8,10,3,8,128]{4,3,2,1,0:T(8,128)}), f32[8,10,3,8,128]{4,3,2,1,0:T(8,128)S(1)}, u32[]{:S(2)}, u32[]{:S(2)}) async-start(f32[8,10,3,8,128]{4,3,2,1,0:T(8,128)} %shard_map.41), calls=%async_computation.1 | async-start | bytes 1966080 | tf_op jit(solution)/shard_map/all_to_all | solution.py:332
  44.8 11.4 %collective-permute-start.8 = (f32[16,3,8,128]{3,2,1,0:T(8,128)S(1)}, f32[16,3,8,128]{3,2,1,0:T(8,128)S(1)}, u32[]{:S(2)}, u32[]{:S(2)}) collective-permute-start(f32[16,3,8,128]{3,2,1,0:T(8,128)S(1)} %get-tuple-element.50), channel_id=1, source_target_pairs={{0,64},{64,128},{128,192},{192,0},{1,65},{65,129},{129,193},{193,1... | collective-permute-start | bytes 589832 | tf_op jit(solution)/shard_map/ppermute | solution.py:295
  45.5 10.7 %collective-permute-start.9 = (f32[16,3,8,128]{3,2,1,0:T(8,128)S(1)}, f32[16,3,8,128]{3,2,1,0:T(8,128)S(1)}, u32[]{:S(2)}, u32[]{:S(2)}) collective-permute-start(f32[16,3,8,128]{3,2,1,0:T(8,128)S(1)} %get-tuple-element.51), channel_id=1, source_target_pairs={{0,128},{64,192},{128,0},{192,64},{1,129},{65,193},{129,1},{193,65... | collective-permute-start | bytes 589832 | tf_op jit(solution)/shard_map/ppermute | solution.py:295
  47.5 9.3 %collective-permute-start.10 = (f32[16,3,8,128]{3,2,1,0:T(8,128)S(1)}, f32[16,3,8,128]{3,2,1,0:T(8,128)S(1)}, u32[]{:S(2)}, u32[]{:S(2)}) collective-permute-start(f32[16,3,8,128]{3,2,1,0:T(8,128)S(1)} %get-tuple-element.52), channel_id=1, source_target_pairs={{0,192},{64,0},{128,64},{192,128},{1,193},{65,1},{129,65},{193,129... | collective-permute-start | bytes 589832 | tf_op jit(solution)/shard_map/ppermute | solution.py:295
  57.9 17.7 %collective-permute-start.11 = (f32[10,3,8,128]{3,2,1,0:T(8,128)S(1)}, f32[10,3,8,128]{3,2,1,0:T(8,128)S(1)}, u32[]{:S(2)}, u32[]{:S(2)}) collective-permute-start(f32[10,3,8,128]{3,2,1,0:T(8,128)S(1)} %get-tuple-element.54), channel_id=1, source_target_pairs={{0,8},{8,16},{16,24},{24,32},{32,40},{40,48},{48,56},{56,0},{1,9},... | collective-permute-start | bytes 368648 | tf_op jit(solution)/shard_map/ppermute | solution.py:295
  59.5 19.6 %collective-permute-start.12 = (f32[10,3,8,128]{3,2,1,0:T(8,128)S(1)}, f32[10,3,8,128]{3,2,1,0:T(8,128)S(1)}, u32[]{:S(2)}, u32[]{:S(2)}) collective-permute-start(f32[10,3,8,128]{3,2,1,0:T(8,128)S(1)} %get-tuple-element.55), channel_id=1, source_target_pairs={{0,16},{8,24},{16,32},{24,40},{32,48},{40,56},{48,0},{56,8},{1,17}... | collective-permute-start | bytes 368648 | tf_op jit(solution)/shard_map/ppermute | solution.py:295
  61.9 24.7 %collective-permute-start.13 = (f32[10,3,8,128]{3,2,1,0:T(8,128)S(1)}, f32[10,3,8,128]{3,2,1,0:T(8,128)S(1)}, u32[]{:S(2)}, u32[]{:S(2)}) collective-permute-start(f32[10,3,8,128]{3,2,1,0:T(8,128)S(1)} %get-tuple-element.56), channel_id=1, source_target_pairs={{0,24},{8,32},{16,40},{24,48},{32,56},{40,0},{48,8},{56,16},{1,25}... | collective-permute-start | bytes 368648 | tf_op jit(solution)/shard_map/ppermute | solution.py:295
  73.1 26.4 %collective-permute-start.5 = (f32[16,3,8,128]{3,2,1,0:T(8,128)S(1)}, f32[16,3,8,128]{3,2,1,0:T(8,128)S(1)}, u32[]{:S(2)}, u32[]{:S(2)}) collective-permute-start(f32[16,3,8,128]{3,2,1,0:T(8,128)S(1)} %get-tuple-element.45), channel_id=1, source_target_pairs={{0,64},{64,128},{128,192},{192,0},{1,65},{65,129},{129,193},{193,1... | collective-permute-start | bytes 589832 | tf_op jit(solution)/shard_map/ppermute | solution.py:295
  73.8 16.6 %collective-permute-start.14 = (f32[10,3,8,128]{3,2,1,0:T(8,128)S(1)}, f32[10,3,8,128]{3,2,1,0:T(8,128)S(1)}, u32[]{:S(2)}, u32[]{:S(2)}) collective-permute-start(f32[10,3,8,128]{3,2,1,0:T(8,128)S(1)} %get-tuple-element.57), channel_id=1, source_target_pairs={{0,32},{8,40},{16,48},{24,56},{32,0},{40,8},{48,16},{56,24},{1,33}... | collective-permute-start | bytes 368648 | tf_op jit(solution)/shard_map/ppermute | solution.py:295
  75.6 16.2 %collective-permute-start.15 = (f32[10,3,8,128]{3,2,1,0:T(8,128)S(1)}, f32[10,3,8,128]{3,2,1,0:T(8,128)S(1)}, u32[]{:S(2)}, u32[]{:S(2)}) collective-permute-start(f32[10,3,8,128]{3,2,1,0:T(8,128)S(1)} %get-tuple-element.58), channel_id=1, source_target_pairs={{0,40},{8,48},{16,56},{24,0},{32,8},{40,16},{48,24},{56,32},{1,41}... | collective-permute-start | bytes 368648 | tf_op jit(solution)/shard_map/ppermute | solution.py:295
  79.1 14.6 %collective-permute-start.16 = (f32[10,3,8,128]{3,2,1,0:T(8,128)S(1)}, f32[10,3,8,128]{3,2,1,0:T(8,128)S(1)}, u32[]{:S(2)}, u32[]{:S(2)}) collective-permute-start(f32[10,3,8,128]{3,2,1,0:T(8,128)S(1)} %get-tuple-element.59), channel_id=1, source_target_pairs={{0,48},{8,56},{16,0},{24,8},{32,16},{40,24},{48,32},{56,40},{1,49}... | collective-permute-start | bytes 368648 | tf_op jit(solution)/shard_map/ppermute | solution.py:295
  86.6 7.5 %collective-permute-start.17 = (f32[10,3,8,128]{3,2,1,0:T(8,128)S(1)}, f32[10,3,8,128]{3,2,1,0:T(8,128)S(1)}, u32[]{:S(2)}, u32[]{:S(2)}) collective-permute-start(f32[10,3,8,128]{3,2,1,0:T(8,128)S(1)} %get-tuple-element.60), channel_id=1, source_target_pairs={{0,56},{8,0},{16,8},{24,16},{32,24},{40,32},{48,40},{56,48},{1,57}... | collective-permute-start | bytes 368648 | tf_op jit(solution)/shard_map/ppermute | solution.py:295
  90.4 10.0 %collective-permute-start.6 = (f32[16,3,8,128]{3,2,1,0:T(8,128)S(1)}, f32[16,3,8,128]{3,2,1,0:T(8,128)S(1)}, u32[]{:S(2)}, u32[]{:S(2)}) collective-permute-start(f32[16,3,8,128]{3,2,1,0:T(8,128)S(1)} %get-tuple-element.46), channel_id=1, source_target_pairs={{0,128},{64,192},{128,0},{192,64},{1,129},{65,193},{129,1},{193,65... | collective-permute-start | bytes 589832 | tf_op jit(solution)/shard_map/ppermute | solution.py:295
  91.8 10.9 %collective-permute-start.7 = (f32[16,3,8,128]{3,2,1,0:T(8,128)S(1)}, f32[16,3,8,128]{3,2,1,0:T(8,128)S(1)}, u32[]{:S(2)}, u32[]{:S(2)}) collective-permute-start(f32[16,3,8,128]{3,2,1,0:T(8,128)S(1)} %get-tuple-element.47), channel_id=1, source_target_pairs={{0,192},{64,0},{128,64},{192,128},{1,193},{65,1},{129,65},{193,129... | collective-permute-start | bytes 589832 | tf_op jit(solution)/shard_map/ppermute | solution.py:295
  95.4 10.2 %collective-permute-start.18 = (f32[16,3,8,128]{3,2,1,0:T(8,128)S(1)}, f32[16,3,8,128]{3,2,1,0:T(8,128)S(1)}, u32[]{:S(2)}, u32[]{:S(2)}) collective-permute-start(f32[16,3,8,128]{3,2,1,0:T(8,128)S(1)} %get-tuple-element.62), channel_id=1, source_target_pairs={{0,64},{64,128},{128,192},{192,0},{1,65},{65,129},{129,193},{193,1... | collective-permute-start | bytes 589832 | tf_op jit(solution)/shard_map/ppermute | solution.py:295
  96.0 11.2 %collective-permute-start.19 = (f32[16,3,8,128]{3,2,1,0:T(8,128)S(1)}, f32[16,3,8,128]{3,2,1,0:T(8,128)S(1)}, u32[]{:S(2)}, u32[]{:S(2)}) collective-permute-start(f32[16,3,8,128]{3,2,1,0:T(8,128)S(1)} %get-tuple-element.63), channel_id=1, source_target_pairs={{0,128},{64,192},{128,0},{192,64},{1,129},{65,193},{129,1},{193,65... | collective-permute-start | bytes 589832 | tf_op jit(solution)/shard_map/ppermute | solution.py:295
  99.6 10.6 %collective-permute-start.20 = (f32[16,3,8,128]{3,2,1,0:T(8,128)S(1)}, f32[16,3,8,128]{3,2,1,0:T(8,128)S(1)}, u32[]{:S(2)}, u32[]{:S(2)}) collective-permute-start(f32[16,3,8,128]{3,2,1,0:T(8,128)S(1)} %get-tuple-element.64), channel_id=1, source_target_pairs={{0,192},{64,0},{128,64},{192,128},{1,193},{65,1},{129,65},{193,129... | collective-permute-start | bytes 589832 | tf_op jit(solution)/shard_map/ppermute | solution.py:295

commit v6 on v1

v6 whole, which is shorter than its diff:
```python
import jax
import jax.numpy as jnp
from jax import lax
from jax.experimental import pallas as pl
from jax.experimental.pallas import tpu as pltpu
from jax.sharding import PartitionSpec as P

F32 = jnp.float32
LANES = 128
VMEM = pl.BlockSpec(memory_space=pltpu.VMEM)
SMEM = pl.BlockSpec(memory_space=pltpu.SMEM)
PARAMS = pltpu.CompilerParams(vmem_limit_bytes=12 * 1024 * 1024)


def one_step(h, m, n, slope_x, slope_y):
    rows, cols = h.shape
    inv = 1.0 / h
    u = m * inv
    press = 0.0625 * (h * h)
    fx = 0.125 * (m * u) + press
    cross = 0.125 * (u * n)
    gy = 0.125 * (n * (n * inv)) + press

    def combine(q, f, g):
        q = 0.25 * q
        return (
            pltpu.roll(q - f, cols - 1, 1)
            + pltpu.roll(q + f, 1, 1)
            + pltpu.roll(q - g, rows - 1, 0)
            + pltpu.roll(q + g, 1, 0)
        )

    return (
        combine(h, 0.125 * m, 0.125 * n),
        combine(m, fx, cross) + h * slope_x,
        combine(n, cross, gy) + h * slope_y,
    )


def edge_kernel(x_ref, bed_ref, low_ref, high_ref):
    count, fields, rows, _ = x_ref.shape
    for p in range(count):
        for f in range(fields):
            low_ref[p * fields + f] = x_ref[p, f, rows - 2 : rows]
            high_ref[p * fields + f] = x_ref[p, f, 0:2]
    low_ref[count * fields] = bed_ref[rows - 2 : rows]
    high_ref[count * fields] = bed_ref[0:2]


def row_kernel(counts_ref, row_ref):
    total = counts_ref[0]
    for j in range(1, counts_ref.shape[0]):
        total = total + counts_ref[j]
    row_ref[...] = jnp.full(row_ref.shape, total, jnp.int32)


def evolve_kernel(x_ref, low_ref, high_ref, bed_ref, out_ref, token_ref, ext, sx, sy):
    count, fields, rows, cols = x_ref.shape
    ext[...] = jnp.ones_like(ext)
    ext[0, 0:rows] = bed_ref[...]
    ext[0, rows : rows + 2] = high_ref[count * fields]
    ext[0, rows + 6 : rows + 8] = low_ref[count * fields]
    b = ext[0]
    sx[...] = -0.125 * (pltpu.roll(b, cols - 1, 1) - pltpu.roll(b, 1, 1))
    sy[...] = -0.125 * (pltpu.roll(b, rows + 7, 0) - pltpu.roll(b, 1, 0))

    def body(p, carry):
        for f in range(fields):
            ext[f, 0:rows] = x_ref[p, f]
            ext[f, rows : rows + 2] = high_ref[p * fields + f]
            ext[f, rows + 6 : rows + 8] = low_ref[p * fields + f]
        slope_x = sx[...]
        slope_y = sy[...]
        state = (ext[0], ext[1], ext[2])
        for _ in range(2):
            state = one_step(*state, slope_x, slope_y)
        for f in range(fields):
            out_ref[p, f] = state[f][0:rows]
        return carry

    lax.fori_loop(0, count, body, 0)
    token_ref[0] = 0


def pack_kernel(place_ref, token_ref, counts_ref, row_ref, done_ref, out_ref, entry_ref, source):
    groups = row_ref.shape[0]
    count = counts_ref.shape[0]
    me = place_ref[0]
    for r in range(groups + 1):
        source[r] = 0
    for k in range(count):
        entry_ref[k] = 0
    total = jnp.int32(0)
    mine = jnp.int32(0)
    for g in range(groups):
        mine = jnp.where(me == g, total, mine)
        later = total + row_ref[g, 0, 0]
        k = (total - me + groups - 1) // groups
        entry_ref[jnp.where(k * groups + me < later, k, count)] = g
        total = later
    e = mine
    for p in range(count):
        c = counts_ref[p]
        source[jnp.where(c > 0, e & (groups - 1), groups)] = p
        source[jnp.where(c > 1, (e + 1) & (groups - 1), groups)] = p
        e = e + c

    def body(r, carry):
        out_ref[r] = done_ref[source[r]]
        return carry

    lax.fori_loop(0, groups, body, 0, unroll=2)


def unpack_kernel(entry_ref, parcel_ref, out_ref, sem):
    count = out_ref.shape[0]
    copies = [
        pltpu.make_async_copy(parcel_ref.at[entry_ref[k]], out_ref.at[k], sem.at[k])
        for k in range(count)
    ]
    for copy in copies:
        copy.start()
    for copy in copies:
        copy.wait()


def per_device(particles, counts, bed):
    count, fields, rows, cols = particles.shape
    groups = lax.axis_size("dom")
    place = lax.axis_index("dom").astype(jnp.int32)[None]
    edges = jax.ShapeDtypeStruct((count * fields + 1, 2, cols), F32)
    row = pl.pallas_call(
        row_kernel,
        in_specs=[SMEM],
        out_specs=VMEM,
        out_shape=jax.ShapeDtypeStruct((groups, 1, LANES), jnp.int32),
        compiler_params=PARAMS,
    )(counts)
    row = lax.all_to_all(row, "dom", 0, 0, tiled=True)
    low, high = pl.pallas_call(
        edge_kernel,
        in_specs=[VMEM, VMEM],
        out_specs=[VMEM] * 2,
        out_shape=[edges, edges],
        compiler_params=PARAMS,
    )(particles, bed)
    strips = lax.axis_size("space")
    low = lax.ppermute(low, "space", [(i, (i + 1) % strips) for i in range(strips)])
    high = lax.ppermute(high, "space", [((i + 1) % strips, i) for i in range(strips)])
    done, token = pl.pallas_call(
        evolve_kernel,
        in_specs=[VMEM] * 4,
        out_specs=[VMEM, SMEM],
        out_shape=[
            jax.ShapeDtypeStruct(particles.shape, F32),
            jax.ShapeDtypeStruct((1,), jnp.int32),
        ],
        scratch_shapes=[
            pltpu.VMEM((fields, rows + 8, cols), F32),
            pltpu.VMEM((rows + 8, cols), F32),
            pltpu.VMEM((rows + 8, cols), F32),
        ],
        compiler_params=PARAMS,
        cost_estimate=pl.CostEstimate(flops=0, bytes_accessed=20_000_000, transcendentals=0),
    )(particles, low, high, bed)
    any_spec = pl.BlockSpec(memory_space=pl.ANY)
    parcel, entry = pl.pallas_call(
        pack_kernel,
        in_specs=[SMEM] * 4 + [VMEM],
        out_specs=[VMEM, SMEM],
        out_shape=[
            jax.ShapeDtypeStruct((groups,) + particles.shape[1:], F32),
            jax.ShapeDtypeStruct((count + 8,), jnp.int32),
        ],
        scratch_shapes=[pltpu.SMEM((groups + 8,), jnp.int32)],
        compiler_params=PARAMS,
        cost_estimate=pl.CostEstimate(flops=0, bytes_accessed=5_000_000, transcendentals=0),
    )(place, token, counts, row, done)
    parcel = lax.all_to_all(parcel, "dom", 0, 0, tiled=True)
    return pl.pallas_call(
        unpack_kernel,
        in_specs=[SMEM, any_spec],
        out_specs=any_spec,
        out_shape=jax.ShapeDtypeStruct(particles.shape, F32),
        scratch_shapes=[pltpu.SemaphoreType.DMA((count,))],
        compiler_params=PARAMS,
    )(entry, parcel)


def solution(mesh):
    in_specs = (P("dom", None, "space", None), P("dom"), P("space", None))
    out_specs = P("dom", None, "space", None)
    return jax.shard_map(
        per_device, mesh=mesh, in_specs=in_specs, out_specs=out_specs, check_vma=False
    )
```

time: 126 us -> 110 us (0.87)
  blocking collectives: 0 us -> 78.7 us
  waiting for transfers between devices: 82.4 us -> 3.89 us
  local copies, waits for them, and re-layouts: 10.6 us -> 2.93 us
  starting transfers between devices: 17.1 us -> 13.2 us
  other arithmetic: 3.41 us -> 0 us
    all_to_all x0 -> x1, blocking collectives: none -> 78.7 us  [per_device(): parcel = lax.all_to_all(parcel, 'dom', 0, 0, tiled=True)]
    all_to_all x2 -> x1, waiting for transfers between devices: 82.4 us -> 3.89 us  [per_device(): row = lax.all_to_all(row, 'dom', 0, 0, tiled=True)]
    gather x2 -> x0, local copies, waits for them, and re-layouts: 5.61 us -> none  [the longest x1 3.82 us: per_device(): jnp.take(done, jnp.minimum(source, per_group - 1), axis=0, mode='clip')]
    all_to_all x2 -> x1, starting transfers between devices: 15.4 us -> 11.4 us  [per_device(): row = lax.all_to_all(row, 'dom', 0, 0, tiled=True)]
    broadcast_in_dim x2 -> x0, local copies, waits for them, and re-layouts: 2.05 us -> none  [the longest x1 1.3 us: per_device(): jnp.broadcast_to(total[None], (groups,))]
    reduce_sum x5 -> x0, other arithmetic: 1.74 us -> none  [the longest x1 0.71 us: per_device(): total = jnp.sum(counts)]
    unnamed x6 -> x10, local copies, waits for them, and re-layouts: 1.33 us -> 2.93 us
    slice x1 -> x0, local copies, waits for them, and re-layouts: 1.56 us -> none  [edge(): return jnp.concatenate([flat[:, lo:lo + 2], bed[None, lo:lo + 2]], axis=0)]
  transfers between devices with their start and end apart: 4 -> 3, of which waited for: 2 -> 1; matrix products, arithmetic and copies ran while one was open for 4% -> 0% of each run, Pallas kernels for 0% -> 5%
where the time goes in v6:
time: 110 us; the launch traced here: 109 us
  blocking collectives  78.7 us (72%)
  starting transfers between devices  13.2 us (12%)
  Pallas kernels  10.6 us (10%)
  waiting for transfers between devices  3.89 us (4%)
  local copies, waits for them, and re-layouts  2.93 us (3%)
    all_to_all x1, blocking collectives, per_device(): parcel = lax.all_to_all(parcel, 'dom', 0, 0, tiled=True)  78.7 us
    all_to_all x1, starting transfers between devices, per_device(): row = lax.all_to_all(row, 'dom', 0, 0, tiled=True)  11.4 us
    pallas_call x1, Pallas kernels, per_device(): pl.pallas_call(evolve_kernel, in_specs=[VMEM] * 4, out_specs=[VMEM, SMEM]...  4.84 us
    all_to_all x1, waiting for transfers between devices, per_device(): row = lax.all_to_all(row, 'dom', 0, 0, tiled=True)  3.89 us
    unnamed x10, local copies, waits for them, and re-layouts  2.93 us
    pallas_call x1, Pallas kernels, per_device(): pl.pallas_call(pack_kernel, in_specs=[SMEM] * 4 + [VMEM], out_specs=[VMEM...  2.69 us
  transfers between devices with their start and end apart: 3, of which 1 were waited for; matrix products, arithmetic and copies ran while one was open for 0% of the time, Pallas kernels for 5%

profile of v6, /device:TPU:16, one launch (start us, length us, event | category | flops | bytes accessed | tf_op | source)
XLA Modules:
  0.0 109.4 jit_solution(14000180646349007609)
XLA Ops:
  0.0 0.0 copy-start
  0.0 1.4 %copy-done = f32[16,3,16,512]{3,2,1,0:T(8,128)S(1)} copy-done((f32[16,3,16,512]{3,2,1,0:T(8,128)S(1)}, f32[16,3,16,512]{3,2,1,0:T(8,128)}, u32[]{:S(2)}) %copy-start) | copy-done | bytes 1572888
  1.4 0.0 copy-start.2
  1.4 0.8 copy-done.2
  2.2 0.0 copy-start.4
  2.2 0.0 copy-start.1
  2.2 0.1 shard_map.37
  2.3 0.0 collective-permute-start
  2.3 1.7 %collective-permute-start.1 = (f32[49,2,512]{2,1,0:T(2,128)S(1)}, f32[49,2,512]{2,1,0:T(2,128)S(1)}, u32[]{:S(2)}, u32[]{:S(2)}) collective-permute-start(f32[49,2,512]{2,1,0:T(2,128)S(1)} %get-tuple-element.12), channel_id=1, source_target_pairs={{1,0},{2,1},{3,2},{4,3},{5,4},{6,5},{7,6},{0,7},{9,8},{10,9},{11,1... | collective-permute-start | bytes 602120 | tf_op jit(solution)/shard_map/ppermute | solution.py:149
  4.0 0.0 copy-done.4
  4.0 1.2 %shard_map.39 = s32[32,1,128]{2,1,0:T(1,128)} custom-call(s32[16]{0:T(128)S(1)} %copy-done.4), custom_call_target="tpu_custom_call" | custom-call | tf_op jit(solution)/shard_map/pallas_call | solution.py:132
  5.2 11.4 %all-to-all-start = ((s32[32,1,128]{2,1,0:T(1,128)}), s32[32,1,128]{2,1,0:T(1,128)}, u32[]{:S(2)}, u32[]{:S(2)}) async-start(s32[32,1,128]{2,1,0:T(1,128)} %shard_map.39), calls=%async_computation | async-start | bytes 32768 | tf_op jit(solution)/shard_map/all_to_all | solution.py:139
  16.6 0.0 collective-permute-done.low_ref
  16.6 0.0 collective-permute-done.1.high_ref
  16.7 0.0 copy-done.1
  16.7 0.0 copy-start.3
  16.7 0.7 copy-done.3
  17.4 4.8 %shard_map.38 = (f32[16,3,16,512]{3,2,1,0:T(8,128)S(1)}, s32[1]{0:T(128)}) custom-call(f32[16,3,16,512]{3,2,1,0:T(8,128)S(1)} %copy-done.1, f32[49,2,512]{2,1,0:T(2,128)S(1)} %collective-permute-done.low_ref, f32[49,2,512]{2,1,0:T(2,128)S(1)} %collective-permute-done.1.high_ref, f32[16,512]{1,0:T(8,128)S(1)} %copy-done.3), custom_call_target="tpu_custom_call" | custom-call | bytes 20000000 | tf_op jit(solution)/shard_map/pallas_call | solution.py:150
  22.3 3.9 %all-to-all-done.row_ref = s32[32,1,128]{2,1,0:T(1,128)} async-done(((s32[32,1,128]{2,1,0:T(1,128)}), s32[32,1,128]{2,1,0:T(1,128)}, u32[]{:S(2)}, u32[]{:S(2)}) %all-to-all-start) | async-done | bytes 16416 | tf_op jit(solution)/shard_map/all_to_all | solution.py:139
  26.2 2.7 %shard_map.40 = (f32[32,3,16,512]{3,2,1,0:T(8,128)S(1)}, s32[24]{0:T(128)S(1)}) custom-call(s32[1]{0:T(128)} %bitcast.place_ref, s32[1]{0:T(128)} %get-tuple-element.13.token_ref, s32[16]{0:T(128)S(1)} %copy-done.4, s32[32,1,128]{2,1,0:T(1,128)} %all-to-all-done.row_ref, f32[16,3,16,512]{3,2,1,0:T(8,128)S(1)} %get-tuple-element.14.done_ref), custom_call_target="tpu_custom_call" | custom-call | bytes 5000000 | tf_op jit(solution)/shard_map/pallas_call | solution.py:167
  28.9 78.7 %all_to_all.10.parcel_ref = f32[32,3,16,512]{3,2,1,0:T(8,128)S(1)} all-to-all(f32[32,3,16,512]{3,2,1,0:T(8,128)S(1)} %get-tuple-element.16), channel_id=1, replica_groups=mesh['dom'=32,'space'=8] {'dom'}, dimensions={0} | all-to-all | bytes 6291456 | tf_op jit(solution)/shard_map/all_to_all | solution.py:179
  107.6 1.8 %shard_map.41 = f32[16,3,16,512]{3,2,1,0:T(8,128)} custom-call(s32[24]{0:T(128)S(1)} %get-tuple-element.15.entry_ref, f32[32,3,16,512]{3,2,1,0:T(8,128)S(1)} %all_to_all.10.parcel_ref), custom_call_target="tpu_custom_call" | custom-call | tf_op jit(solution)/shard_map/pallas_call | solution.py:180
Async XLA Ops:
  0.0 1.4 %copy-start = (f32[16,3,16,512]{3,2,1,0:T(8,128)S(1)}, f32[16,3,16,512]{3,2,1,0:T(8,128)}, u32[]{:S(2)}) copy-start(f32[16,3,16,512]{3,2,1,0:T(8,128)} %x_ref.3) | copy-start | bytes 4718596
  1.4 0.8 copy-start.2
  2.2 1.8 %copy-start.4 = (s32[16]{0:T(128)S(1)}, s32[16]{0:T(128)}, u32[]{:S(2)}) copy-start(s32[16]{0:T(128)} %counts_ref.3) | copy-start | bytes 196
  2.2 14.5 %copy-start.1 = (f32[16,3,16,512]{3,2,1,0:T(8,128)S(1)}, f32[16,3,16,512]{3,2,1,0:T(8,128)}, u32[]{:S(2)}) copy-start(f32[16,3,16,512]{3,2,1,0:T(8,128)} %x_ref.3) | copy-start | bytes 4718596
  2.3 14.4 %collective-permute-start = (f32[49,2,512]{2,1,0:T(2,128)S(1)}, f32[49,2,512]{2,1,0:T(2,128)S(1)}, u32[]{:S(2)}, u32[]{:S(2)}) collective-permute-start(f32[49,2,512]{2,1,0:T(2,128)S(1)} %get-tuple-element.11), channel_id=1, source_target_pairs={{0,1},{1,2},{2,3},{3,4},{4,5},{5,6},{6,7},{7,0},{8,9},{9,10},{10,1... | collective-permute-start | bytes 602120 | tf_op jit(solution)/shard_map/ppermute | solution.py:148
  2.3 14.4 %collective-permute-start.1 = (f32[49,2,512]{2,1,0:T(2,128)S(1)}, f32[49,2,512]{2,1,0:T(2,128)S(1)}, u32[]{:S(2)}, u32[]{:S(2)}) collective-permute-start(f32[49,2,512]{2,1,0:T(2,128)S(1)} %get-tuple-element.12), channel_id=1, source_target_pairs={{1,0},{2,1},{3,2},{4,3},{5,4},{6,5},{7,6},{0,7},{9,8},{10,9},{11,1... | collective-permute-start | bytes 602120 | tf_op jit(solution)/shard_map/ppermute | solution.py:149
  5.2 21.0 %all-to-all-start = ((s32[32,1,128]{2,1,0:T(1,128)}), s32[32,1,128]{2,1,0:T(1,128)}, u32[]{:S(2)}, u32[]{:S(2)}) async-start(s32[32,1,128]{2,1,0:T(1,128)} %shard_map.39), calls=%async_computation | async-start | bytes 32768 | tf_op jit(solution)/shard_map/all_to_all | solution.py:139
  16.7 0.8 copy-start.3

commit v7 on v6

--- a/solution.py
+++ b/solution.py
@@ -7,6 +7,7 @@
 
 F32 = jnp.float32
 LANES = 128
+PAIR = 4
 VMEM = pl.BlockSpec(memory_space=pltpu.VMEM)
 SMEM = pl.BlockSpec(memory_space=pltpu.SMEM)
 PARAMS = pltpu.CompilerParams(vmem_limit_bytes=12 * 1024 * 1024)
@@ -64,21 +65,25 @@
     sx[...] = -0.125 * (pltpu.roll(b, cols - 1, 1) - pltpu.roll(b, 1, 1))
     sy[...] = -0.125 * (pltpu.roll(b, rows + 7, 0) - pltpu.roll(b, 1, 0))
 
-    def body(p, carry):
+    def one(p, at):
         for f in range(fields):
-            ext[f, 0:rows] = x_ref[p, f]
-            ext[f, rows : rows + 2] = high_ref[p * fields + f]
-            ext[f, rows + 6 : rows + 8] = low_ref[p * fields + f]
+            ext[at + f, 0:rows] = x_ref[p, f]
+            ext[at + f, rows : rows + 2] = high_ref[p * fields + f]
+            ext[at + f, rows + 6 : rows + 8] = low_ref[p * fields + f]
         slope_x = sx[...]
         slope_y = sy[...]
-        state = (ext[0], ext[1], ext[2])
+        state = (ext[at], ext[at + 1], ext[at + 2])
         for _ in range(2):
             state = one_step(*state, slope_x, slope_y)
         for f in range(fields):
             out_ref[p, f] = state[f][0:rows]
+
+    def body(i, carry):
+        for j in range(PAIR):
+            one(i * PAIR + j, j * fields)
         return carry
 
-    lax.fori_loop(0, count, body, 0)
+    lax.fori_loop(0, count // PAIR, body, 0)
     token_ref[0] = 0
 
 
@@ -86,16 +91,15 @@
     groups = row_ref.shape[0]
     count = counts_ref.shape[0]
     me = place_ref[0]
+    shift = groups.bit_length() - 1
     for r in range(groups + 1):
         source[r] = 0
-    for k in range(count):
-        entry_ref[k] = 0
     total = jnp.int32(0)
     mine = jnp.int32(0)
     for g in range(groups):
         mine = jnp.where(me == g, total, mine)
         later = total + row_ref[g, 0, 0]
-        k = (total - me + groups - 1) // groups
+        k = (total - me + groups - 1) >> shift
         entry_ref[jnp.where(k * groups + me < later, k, count)] = g
         total = later
     e = mine
@@ -156,7 +160,7 @@
             jax.ShapeDtypeStruct((1,), jnp.int32),
         ],
         scratch_shapes=[
-            pltpu.VMEM((fields, rows + 8, cols), F32),
+            pltpu.VMEM((PAIR * fields, rows + 8, cols), F32),
             pltpu.VMEM((rows + 8, cols), F32),
             pltpu.VMEM((rows + 8, cols), F32),
         ],

time: 110 us -> 109 us (level)
  no operation moved by 1% of the time
where the time goes in v7:
time: 109 us; the launch traced here: 108 us
  blocking collectives  77.8 us (71%)
  starting transfers between devices  13.2 us (12%)
  Pallas kernels  9.6 us (9%)
  waiting for transfers between devices  4.76 us (4%)
  local copies, waits for them, and re-layouts  2.93 us (3%)
    all_to_all x1, blocking collectives, per_device(): parcel = lax.all_to_all(parcel, 'dom', 0, 0, tiled=True)  77.8 us
    all_to_all x1, starting transfers between devices, per_device(): row = lax.all_to_all(row, 'dom', 0, 0, tiled=True)  11.4 us
    all_to_all x1, waiting for transfers between devices, per_device(): row = lax.all_to_all(row, 'dom', 0, 0, tiled=True)  4.75 us
    pallas_call x1, Pallas kernels, per_device(): pl.pallas_call(evolve_kernel, in_specs=[VMEM] * 4, out_specs=[VMEM, SMEM]...  3.98 us
    unnamed x10, local copies, waits for them, and re-layouts  2.93 us
    pallas_call x1, Pallas kernels, per_device(): pl.pallas_call(pack_kernel, in_specs=[SMEM] * 4 + [VMEM], out_specs=[VMEM...  2.56 us
  transfers between devices with their start and end apart: 3, of which 1 were waited for; matrix products, arithmetic and copies ran while one was open for 0% of the time, Pallas kernels for 5%

profile of v7, /device:TPU:16, one launch (start us, length us, event | category | flops | bytes accessed | tf_op | source)
XLA Modules:
  0.0 108.4 jit_solution(7492031868665196569)
XLA Ops:
  0.0 0.0 copy-start
  0.0 1.4 %copy-done = f32[16,3,16,512]{3,2,1,0:T(8,128)S(1)} copy-done((f32[16,3,16,512]{3,2,1,0:T(8,128)S(1)}, f32[16,3,16,512]{3,2,1,0:T(8,128)}, u32[]{:S(2)}) %copy-start) | copy-done | bytes 1572888
  1.4 0.0 copy-start.2
  1.4 0.8 copy-done.2
  2.2 0.0 copy-start.4
  2.2 0.0 copy-start.1
  2.2 0.1 shard_map.37
  2.3 0.0 collective-permute-start
  2.3 1.7 %collective-permute-start.1 = (f32[49,2,512]{2,1,0:T(2,128)S(1)}, f32[49,2,512]{2,1,0:T(2,128)S(1)}, u32[]{:S(2)}, u32[]{:S(2)}) collective-permute-start(f32[49,2,512]{2,1,0:T(2,128)S(1)} %get-tuple-element.12), channel_id=1, source_target_pairs={{1,0},{2,1},{3,2},{4,3},{5,4},{6,5},{7,6},{0,7},{9,8},{10,9},{11,1... | collective-permute-start | bytes 602120 | tf_op jit(solution)/shard_map/ppermute | solution.py:153
  4.0 0.0 copy-done.4
  4.0 1.2 %shard_map.39 = s32[32,1,128]{2,1,0:T(1,128)} custom-call(s32[16]{0:T(128)S(1)} %copy-done.4), custom_call_target="tpu_custom_call" | custom-call | tf_op jit(solution)/shard_map/pallas_call | solution.py:136
  5.2 11.4 %all-to-all-start = ((s32[32,1,128]{2,1,0:T(1,128)}), s32[32,1,128]{2,1,0:T(1,128)}, u32[]{:S(2)}, u32[]{:S(2)}) async-start(s32[32,1,128]{2,1,0:T(1,128)} %shard_map.39), calls=%async_computation | async-start | bytes 32768 | tf_op jit(solution)/shard_map/all_to_all | solution.py:143
  16.6 0.0 collective-permute-done.low_ref
  16.6 0.0 collective-permute-done.1.high_ref
  16.7 0.0 copy-done.1
  16.7 0.0 copy-start.3
  16.7 0.7 copy-done.3
  17.4 4.0 %shard_map.38 = (f32[16,3,16,512]{3,2,1,0:T(8,128)S(1)}, s32[1]{0:T(128)}) custom-call(f32[16,3,16,512]{3,2,1,0:T(8,128)S(1)} %copy-done.1, f32[49,2,512]{2,1,0:T(2,128)S(1)} %collective-permute-done.low_ref, f32[49,2,512]{2,1,0:T(2,128)S(1)} %collective-permute-done.1.high_ref, f32[16,512]{1,0:T(8,128)S(1)} %copy-done.3), custom_call_target="tpu_custom_call" | custom-call | bytes 20000000 | tf_op jit(solution)/shard_map/pallas_call | solution.py:154
  21.4 4.8 %all-to-all-done.row_ref = s32[32,1,128]{2,1,0:T(1,128)} async-done(((s32[32,1,128]{2,1,0:T(1,128)}), s32[32,1,128]{2,1,0:T(1,128)}, u32[]{:S(2)}, u32[]{:S(2)}) %all-to-all-start) | async-done | bytes 16416 | tf_op jit(solution)/shard_map/all_to_all | solution.py:143
  26.2 2.6 %shard_map.40 = (f32[32,3,16,512]{3,2,1,0:T(8,128)S(1)}, s32[24]{0:T(128)S(1)}) custom-call(s32[1]{0:T(128)} %bitcast.place_ref, s32[1]{0:T(128)} %get-tuple-element.13.token_ref, s32[16]{0:T(128)S(1)} %copy-done.4, s32[32,1,128]{2,1,0:T(1,128)} %all-to-all-done.row_ref, f32[16,3,16,512]{3,2,1,0:T(8,128)S(1)} %get-tuple-element.14.done_ref), custom_call_target="tpu_custom_call" | custom-call | bytes 5000000 | tf_op jit(solution)/shard_map/pallas_call | solution.py:171
  28.7 77.8 %all_to_all.10.parcel_ref = f32[32,3,16,512]{3,2,1,0:T(8,128)S(1)} all-to-all(f32[32,3,16,512]{3,2,1,0:T(8,128)S(1)} %get-tuple-element.16), channel_id=1, replica_groups=mesh['dom'=32,'space'=8] {'dom'}, dimensions={0} | all-to-all | bytes 6291456 | tf_op jit(solution)/shard_map/all_to_all | solution.py:183
  106.6 1.8 %shard_map.41 = f32[16,3,16,512]{3,2,1,0:T(8,128)} custom-call(s32[24]{0:T(128)S(1)} %get-tuple-element.15.entry_ref, f32[32,3,16,512]{3,2,1,0:T(8,128)S(1)} %all_to_all.10.parcel_ref), custom_call_target="tpu_custom_call" | custom-call | tf_op jit(solution)/shard_map/pallas_call | solution.py:184
Async XLA Ops:
  0.0 1.4 %copy-start = (f32[16,3,16,512]{3,2,1,0:T(8,128)S(1)}, f32[16,3,16,512]{3,2,1,0:T(8,128)}, u32[]{:S(2)}) copy-start(f32[16,3,16,512]{3,2,1,0:T(8,128)} %x_ref.3) | copy-start | bytes 4718596
  1.4 0.8 copy-start.2
  2.2 1.8 %copy-start.4 = (s32[16]{0:T(128)S(1)}, s32[16]{0:T(128)}, u32[]{:S(2)}) copy-start(s32[16]{0:T(128)} %counts_ref.3) | copy-start | bytes 196
  2.2 14.5 %copy-start.1 = (f32[16,3,16,512]{3,2,1,0:T(8,128)S(1)}, f32[16,3,16,512]{3,2,1,0:T(8,128)}, u32[]{:S(2)}) copy-start(f32[16,3,16,512]{3,2,1,0:T(8,128)} %x_ref.3) | copy-start | bytes 4718596
  2.3 14.4 %collective-permute-start = (f32[49,2,512]{2,1,0:T(2,128)S(1)}, f32[49,2,512]{2,1,0:T(2,128)S(1)}, u32[]{:S(2)}, u32[]{:S(2)}) collective-permute-start(f32[49,2,512]{2,1,0:T(2,128)S(1)} %get-tuple-element.11), channel_id=1, source_target_pairs={{0,1},{1,2},{2,3},{3,4},{4,5},{5,6},{6,7},{7,0},{8,9},{9,10},{10,1... | collective-permute-start | bytes 602120 | tf_op jit(solution)/shard_map/ppermute | solution.py:152
  2.3 14.4 %collective-permute-start.1 = (f32[49,2,512]{2,1,0:T(2,128)S(1)}, f32[49,2,512]{2,1,0:T(2,128)S(1)}, u32[]{:S(2)}, u32[]{:S(2)}) collective-permute-start(f32[49,2,512]{2,1,0:T(2,128)S(1)} %get-tuple-element.12), channel_id=1, source_target_pairs={{1,0},{2,1},{3,2},{4,3},{5,4},{6,5},{7,6},{0,7},{9,8},{10,9},{11,1... | collective-permute-start | bytes 602120 | tf_op jit(solution)/shard_map/ppermute | solution.py:153
  5.2 21.0 %all-to-all-start = ((s32[32,1,128]{2,1,0:T(1,128)}), s32[32,1,128]{2,1,0:T(1,128)}, u32[]{:S(2)}, u32[]{:S(2)}) async-start(s32[32,1,128]{2,1,0:T(1,128)} %shard_map.39), calls=%async_computation | async-start | bytes 32768 | tf_op jit(solution)/shard_map/all_to_all | solution.py:143
  16.7 0.8 copy-start.3

commit v8 on v7

--- a/solution.py
+++ b/solution.py
@@ -38,7 +38,7 @@
     )
 
 
-def edge_kernel(x_ref, bed_ref, low_ref, high_ref):
+def edge_kernel(counts_ref, x_ref, bed_ref, low_ref, high_ref, row_ref):
     count, fields, rows, _ = x_ref.shape
     for p in range(count):
         for f in range(fields):
@@ -46,11 +46,8 @@
             high_ref[p * fields + f] = x_ref[p, f, 0:2]
     low_ref[count * fields] = bed_ref[rows - 2 : rows]
     high_ref[count * fields] = bed_ref[0:2]
-
-
-def row_kernel(counts_ref, row_ref):
     total = counts_ref[0]
-    for j in range(1, counts_ref.shape[0]):
+    for j in range(1, count):
         total = total + counts_ref[j]
     row_ref[...] = jnp.full(row_ref.shape, total, jnp.int32)
 
@@ -133,21 +130,14 @@
     groups = lax.axis_size("dom")
     place = lax.axis_index("dom").astype(jnp.int32)[None]
     edges = jax.ShapeDtypeStruct((count * fields + 1, 2, cols), F32)
-    row = pl.pallas_call(
-        row_kernel,
-        in_specs=[SMEM],
-        out_specs=VMEM,
-        out_shape=jax.ShapeDtypeStruct((groups, 1, LANES), jnp.int32),
-        compiler_params=PARAMS,
-    )(counts)
+    low, high, row = pl.pallas_call(
+        edge_kernel,
+        in_specs=[SMEM, VMEM, VMEM],
+        out_specs=[VMEM] * 3,
+        out_shape=[edges, edges, jax.ShapeDtypeStruct((groups, 1, LANES), jnp.int32)],
+        compiler_params=pltpu.CompilerParams(vmem_limit_bytes=60 * 1024 * 1024),
+    )(counts, particles, bed)
     row = lax.all_to_all(row, "dom", 0, 0, tiled=True)
-    low, high = pl.pallas_call(
-        edge_kernel,
-        in_specs=[VMEM, VMEM],
-        out_specs=[VMEM] * 2,
-        out_shape=[edges, edges],
-        compiler_params=PARAMS,
-    )(particles, bed)
     strips = lax.axis_size("space")
     low = lax.ppermute(low, "space", [(i, (i + 1) % strips) for i in range(strips)])
     high = lax.ppermute(high, "space", [((i + 1) % strips, i) for i in range(strips)])

time: 109 us -> 108 us (level)
  local copies, waits for them, and re-layouts: 2.93 us -> 0.76 us
  Pallas kernels: 9.6 us -> 10.8 us
    unnamed x10 -> x6, local copies, waits for them, and re-layouts: 2.93 us -> 0.76 us
    pallas_call x2 -> x1, Pallas kernels: 1.24 us -> 2.32 us  [per_device(): pl.pallas_call(edge_kernel, in_specs=[SMEM, VMEM, VMEM], out_specs=[VMEM]...]
  transfers between devices with their start and end apart: 3 -> 3, of which waited for: 1 -> 1; matrix products, arithmetic and copies ran while one was open for 0% -> 0% of each run, Pallas kernels for 5% -> 4%
where the time goes in v8:
time: 108 us; the launch traced here: 107 us
  blocking collectives  77.8 us (72%)
  starting transfers between devices  13.2 us (12%)
  Pallas kernels  10.8 us (10%)
  waiting for transfers between devices  4.81 us (4%)
    all_to_all x1, blocking collectives, per_device(): parcel = lax.all_to_all(parcel, 'dom', 0, 0, tiled=True)  77.8 us
    all_to_all x1, starting transfers between devices, per_device(): row = lax.all_to_all(row, 'dom', 0, 0, tiled=True)  11.4 us
    all_to_all x1, waiting for transfers between devices, per_device(): row = lax.all_to_all(row, 'dom', 0, 0, tiled=True)  4.8 us
    pallas_call x1, Pallas kernels, per_device(): pl.pallas_call(evolve_kernel, in_specs=[VMEM] * 4, out_specs=[VMEM, SMEM]...  4 us
    pallas_call x1, Pallas kernels, per_device(): pl.pallas_call(pack_kernel, in_specs=[SMEM] * 4 + [VMEM], out_specs=[VMEM...  2.65 us
    pallas_call x1, Pallas kernels, per_device(): pl.pallas_call(edge_kernel, in_specs=[SMEM, VMEM, VMEM], out_specs=[VMEM]...  2.32 us
  transfers between devices with their start and end apart: 3, of which 1 were waited for; matrix products, arithmetic and copies ran while one was open for 0% of the time, Pallas kernels for 4%

profile of v8, /device:TPU:16, one launch (start us, length us, event | category | flops | bytes accessed | tf_op | source)
XLA Modules:
  0.0 107.4 jit_solution(497094301972002087)
XLA Ops:
  0.0 0.0 copy-start.2
  0.0 0.0 copy-start
  0.0 2.3 %shard_map.37 = (f32[49,2,512]{2,1,0:T(2,128)}, f32[49,2,512]{2,1,0:T(2,128)}, s32[32,1,128]{2,1,0:T(1,128)}) custom-call(s32[16]{0:T(128)} %counts_ref.3, f32[16,3,16,512]{3,2,1,0:T(8,128)} %x_ref.3, f32[16,512]{1,0:T(8,128)} %bed_ref.3), custom_call_target="tpu_custom_call" | custom-call | tf_op jit(solution)/shard_map/pallas_call | solution.py:133
  2.3 0.0 collective-permute-start
  2.3 1.7 %collective-permute-start.1 = (f32[49,2,512]{2,1,0:T(2,128)}, f32[49,2,512]{2,1,0:T(2,128)S(1)}, u32[]{:S(2)}, u32[]{:S(2)}) collective-permute-start(f32[49,2,512]{2,1,0:T(2,128)} %get-tuple-element.13), channel_id=1, source_target_pairs={{1,0},{2,1},{3,2},{4,3},{5,4},{6,5},{7,6},{0,7},{9,8},{10,9},{11,1... | collective-permute-start | bytes 602120 | tf_op jit(solution)/shard_map/ppermute | solution.py:143
  4.1 11.4 %all-to-all-start = ((s32[32,1,128]{2,1,0:T(1,128)}), s32[32,1,128]{2,1,0:T(1,128)}, u32[]{:S(2)}, u32[]{:S(2)}) async-start(s32[32,1,128]{2,1,0:T(1,128)} %get-tuple-element.15), calls=%async_computation | async-start | bytes 32768 | tf_op jit(solution)/shard_map/all_to_all | solution.py:140
  15.5 0.0 collective-permute-done.low_ref
  15.5 0.0 collective-permute-done.1.high_ref
  15.6 0.0 copy-done
  15.6 0.0 copy-start.1
  15.6 0.7 copy-done.1
  16.3 4.0 %shard_map.38 = (f32[16,3,16,512]{3,2,1,0:T(8,128)S(1)}, s32[1]{0:T(128)}) custom-call(f32[16,3,16,512]{3,2,1,0:T(8,128)S(1)} %copy-done, f32[49,2,512]{2,1,0:T(2,128)S(1)} %collective-permute-done.low_ref, f32[49,2,512]{2,1,0:T(2,128)S(1)} %collective-permute-done.1.high_ref, f32[16,512]{1,0:T(8,128)S(1)} %copy-done.1), custom_call_target="tpu_custom_call" | custom-call | bytes 20000000 | tf_op jit(solution)/shard_map/pallas_call | solution.py:144
  20.3 4.8 %all-to-all-done.row_ref = s32[32,1,128]{2,1,0:T(1,128)} async-done(((s32[32,1,128]{2,1,0:T(1,128)}), s32[32,1,128]{2,1,0:T(1,128)}, u32[]{:S(2)}, u32[]{:S(2)}) %all-to-all-start) | async-done | bytes 16416 | tf_op jit(solution)/shard_map/all_to_all | solution.py:140
  25.1 0.0 copy-done.2
  25.1 2.6 %shard_map.39 = (f32[32,3,16,512]{3,2,1,0:T(8,128)S(1)}, s32[24]{0:T(128)S(1)}) custom-call(s32[1]{0:T(128)} %bitcast.place_ref, s32[1]{0:T(128)} %get-tuple-element.14.token_ref, s32[16]{0:T(128)S(1)} %copy-done.2, s32[32,1,128]{2,1,0:T(1,128)} %all-to-all-done.row_ref, f32[16,3,16,512]{3,2,1,0:T(8,128)S(1)} %get-tuple-element.16.done_ref), custom_call_target="tpu_custom_call" | custom-call | bytes 5000000 | tf_op jit(solution)/shard_map/pallas_call | solution.py:161
  27.8 77.8 %all_to_all.10.parcel_ref = f32[32,3,16,512]{3,2,1,0:T(8,128)S(1)} all-to-all(f32[32,3,16,512]{3,2,1,0:T(8,128)S(1)} %get-tuple-element.18), channel_id=1, replica_groups=mesh['dom'=32,'space'=8] {'dom'}, dimensions={0} | all-to-all | bytes 6291456 | tf_op jit(solution)/shard_map/all_to_all | solution.py:173
  105.6 1.8 %shard_map.40 = f32[16,3,16,512]{3,2,1,0:T(8,128)} custom-call(s32[24]{0:T(128)S(1)} %get-tuple-element.17.entry_ref, f32[32,3,16,512]{3,2,1,0:T(8,128)S(1)} %all_to_all.10.parcel_ref), custom_call_target="tpu_custom_call" | custom-call | tf_op jit(solution)/shard_map/pallas_call | solution.py:174
Async XLA Ops:
  0.0 25.1 %copy-start.2 = (s32[16]{0:T(128)S(1)}, s32[16]{0:T(128)}, u32[]{:S(2)}) copy-start(s32[16]{0:T(128)} %counts_ref.3) | copy-start | bytes 196
  0.0 15.6 %copy-start = (f32[16,3,16,512]{3,2,1,0:T(8,128)S(1)}, f32[16,3,16,512]{3,2,1,0:T(8,128)}, u32[]{:S(2)}) copy-start(f32[16,3,16,512]{3,2,1,0:T(8,128)} %x_ref.3) | copy-start | bytes 4718596
  2.3 13.2 %collective-permute-start = (f32[49,2,512]{2,1,0:T(2,128)}, f32[49,2,512]{2,1,0:T(2,128)S(1)}, u32[]{:S(2)}, u32[]{:S(2)}) collective-permute-start(f32[49,2,512]{2,1,0:T(2,128)} %get-tuple-element.12), channel_id=1, source_target_pairs={{0,1},{1,2},{2,3},{3,4},{4,5},{5,6},{6,7},{7,0},{8,9},{9,10},{10,1... | collective-permute-start | bytes 602120 | tf_op jit(solution)/shard_map/ppermute | solution.py:142
  2.3 13.2 %collective-permute-start.1 = (f32[49,2,512]{2,1,0:T(2,128)}, f32[49,2,512]{2,1,0:T(2,128)S(1)}, u32[]{:S(2)}, u32[]{:S(2)}) collective-permute-start(f32[49,2,512]{2,1,0:T(2,128)} %get-tuple-element.13), channel_id=1, source_target_pairs={{1,0},{2,1},{3,2},{4,3},{5,4},{6,5},{7,6},{0,7},{9,8},{10,9},{11,1... | collective-permute-start | bytes 602120 | tf_op jit(solution)/shard_map/ppermute | solution.py:143
  4.1 21.1 %all-to-all-start = ((s32[32,1,128]{2,1,0:T(1,128)}), s32[32,1,128]{2,1,0:T(1,128)}, u32[]{:S(2)}, u32[]{:S(2)}) async-start(s32[32,1,128]{2,1,0:T(1,128)} %get-tuple-element.15), calls=%async_computation | async-start | bytes 32768 | tf_op jit(solution)/shard_map/all_to_all | solution.py:140
  15.6 0.8 copy-start.1

commit v9 on v8

--- a/solution.py
+++ b/solution.py
@@ -7,7 +7,7 @@
 
 F32 = jnp.float32
 LANES = 128
-PAIR = 4
+PAIR = 8
 VMEM = pl.BlockSpec(memory_space=pltpu.VMEM)
 SMEM = pl.BlockSpec(memory_space=pltpu.SMEM)
 PARAMS = pltpu.CompilerParams(vmem_limit_bytes=12 * 1024 * 1024)

time: 108 us -> 108 us (level)
  no operation moved by 1% of the time
where the time goes in v9:
time: 108 us; the launch traced here: 107 us
  blocking collectives  77.8 us (72%)
  starting transfers between devices  13.2 us (12%)
  Pallas kernels  10.8 us (10%)
  waiting for transfers between devices  4.82 us (4%)
    all_to_all x1, blocking collectives, per_device(): parcel = lax.all_to_all(parcel, 'dom', 0, 0, tiled=True)  77.8 us
    all_to_all x1, starting transfers between devices, per_device(): row = lax.all_to_all(row, 'dom', 0, 0, tiled=True)  11.4 us
    all_to_all x1, waiting for transfers between devices, per_device(): row = lax.all_to_all(row, 'dom', 0, 0, tiled=True)  4.81 us
    pallas_call x1, Pallas kernels, per_device(): pl.pallas_call(evolve_kernel, in_specs=[VMEM] * 4, out_specs=[VMEM, SMEM]...  3.99 us
    pallas_call x1, Pallas kernels, per_device(): pl.pallas_call(pack_kernel, in_specs=[SMEM] * 4 + [VMEM], out_specs=[VMEM...  2.65 us
    pallas_call x1, Pallas kernels, per_device(): pl.pallas_call(edge_kernel, in_specs=[SMEM, VMEM, VMEM], out_specs=[VMEM]...  2.32 us
  transfers between devices with their start and end apart: 3, of which 1 were waited for; matrix products, arithmetic and copies ran while one was open for 0% of the time, Pallas kernels for 4%

profile of v9, /device:TPU:16, one launch (start us, length us, event | category | flops | bytes accessed | tf_op | source)
XLA Modules:
  0.0 107.4 jit_solution(5447494420972905906)
XLA Ops:
  0.0 0.0 copy-start.2
  0.0 0.0 copy-start
  0.0 2.3 %shard_map.37 = (f32[49,2,512]{2,1,0:T(2,128)}, f32[49,2,512]{2,1,0:T(2,128)}, s32[32,1,128]{2,1,0:T(1,128)}) custom-call(s32[16]{0:T(128)} %counts_ref.3, f32[16,3,16,512]{3,2,1,0:T(8,128)} %x_ref.3, f32[16,512]{1,0:T(8,128)} %bed_ref.3), custom_call_target="tpu_custom_call" | custom-call | tf_op jit(solution)/shard_map/pallas_call | solution.py:133
  2.3 0.0 collective-permute-start
  2.3 1.7 %collective-permute-start.1 = (f32[49,2,512]{2,1,0:T(2,128)}, f32[49,2,512]{2,1,0:T(2,128)S(1)}, u32[]{:S(2)}, u32[]{:S(2)}) collective-permute-start(f32[49,2,512]{2,1,0:T(2,128)} %get-tuple-element.13), channel_id=1, source_target_pairs={{1,0},{2,1},{3,2},{4,3},{5,4},{6,5},{7,6},{0,7},{9,8},{10,9},{11,1... | collective-permute-start | bytes 602120 | tf_op jit(solution)/shard_map/ppermute | solution.py:143
  4.1 11.4 %all-to-all-start = ((s32[32,1,128]{2,1,0:T(1,128)}), s32[32,1,128]{2,1,0:T(1,128)}, u32[]{:S(2)}, u32[]{:S(2)}) async-start(s32[32,1,128]{2,1,0:T(1,128)} %get-tuple-element.15), calls=%async_computation | async-start | bytes 32768 | tf_op jit(solution)/shard_map/all_to_all | solution.py:140
  15.5 0.0 collective-permute-done.low_ref
  15.5 0.0 collective-permute-done.1.high_ref
  15.6 0.0 copy-done
  15.6 0.0 copy-start.1
  15.6 0.7 copy-done.1
  16.3 4.0 %shard_map.38 = (f32[16,3,16,512]{3,2,1,0:T(8,128)S(1)}, s32[1]{0:T(128)}) custom-call(f32[16,3,16,512]{3,2,1,0:T(8,128)S(1)} %copy-done, f32[49,2,512]{2,1,0:T(2,128)S(1)} %collective-permute-done.low_ref, f32[49,2,512]{2,1,0:T(2,128)S(1)} %collective-permute-done.1.high_ref, f32[16,512]{1,0:T(8,128)S(1)} %copy-done.1), custom_call_target="tpu_custom_call" | custom-call | bytes 20000000 | tf_op jit(solution)/shard_map/pallas_call | solution.py:144
  20.3 4.8 %all-to-all-done.row_ref = s32[32,1,128]{2,1,0:T(1,128)} async-done(((s32[32,1,128]{2,1,0:T(1,128)}), s32[32,1,128]{2,1,0:T(1,128)}, u32[]{:S(2)}, u32[]{:S(2)}) %all-to-all-start) | async-done | bytes 16416 | tf_op jit(solution)/shard_map/all_to_all | solution.py:140
  25.1 0.0 copy-done.2
  25.1 2.6 %shard_map.39 = (f32[32,3,16,512]{3,2,1,0:T(8,128)S(1)}, s32[24]{0:T(128)S(1)}) custom-call(s32[1]{0:T(128)} %bitcast.place_ref, s32[1]{0:T(128)} %get-tuple-element.14.token_ref, s32[16]{0:T(128)S(1)} %copy-done.2, s32[32,1,128]{2,1,0:T(1,128)} %all-to-all-done.row_ref, f32[16,3,16,512]{3,2,1,0:T(8,128)S(1)} %get-tuple-element.16.done_ref), custom_call_target="tpu_custom_call" | custom-call | bytes 5000000 | tf_op jit(solution)/shard_map/pallas_call | solution.py:161
  27.8 77.8 %all_to_all.10.parcel_ref = f32[32,3,16,512]{3,2,1,0:T(8,128)S(1)} all-to-all(f32[32,3,16,512]{3,2,1,0:T(8,128)S(1)} %get-tuple-element.18), channel_id=1, replica_groups=mesh['dom'=32,'space'=8] {'dom'}, dimensions={0} | all-to-all | bytes 6291456 | tf_op jit(solution)/shard_map/all_to_all | solution.py:173
  105.6 1.8 %shard_map.40 = f32[16,3,16,512]{3,2,1,0:T(8,128)} custom-call(s32[24]{0:T(128)S(1)} %get-tuple-element.17.entry_ref, f32[32,3,16,512]{3,2,1,0:T(8,128)S(1)} %all_to_all.10.parcel_ref), custom_call_target="tpu_custom_call" | custom-call | tf_op jit(solution)/shard_map/pallas_call | solution.py:174
Async XLA Ops:
  0.0 25.1 %copy-start.2 = (s32[16]{0:T(128)S(1)}, s32[16]{0:T(128)}, u32[]{:S(2)}) copy-start(s32[16]{0:T(128)} %counts_ref.3) | copy-start | bytes 196
  0.0 15.6 %copy-start = (f32[16,3,16,512]{3,2,1,0:T(8,128)S(1)}, f32[16,3,16,512]{3,2,1,0:T(8,128)}, u32[]{:S(2)}) copy-start(f32[16,3,16,512]{3,2,1,0:T(8,128)} %x_ref.3) | copy-start | bytes 4718596
  2.3 13.2 %collective-permute-start = (f32[49,2,512]{2,1,0:T(2,128)}, f32[49,2,512]{2,1,0:T(2,128)S(1)}, u32[]{:S(2)}, u32[]{:S(2)}) collective-permute-start(f32[49,2,512]{2,1,0:T(2,128)} %get-tuple-element.12), channel_id=1, source_target_pairs={{0,1},{1,2},{2,3},{3,4},{4,5},{5,6},{6,7},{7,0},{8,9},{9,10},{10,1... | collective-permute-start | bytes 602120 | tf_op jit(solution)/shard_map/ppermute | solution.py:142
  2.3 13.2 %collective-permute-start.1 = (f32[49,2,512]{2,1,0:T(2,128)}, f32[49,2,512]{2,1,0:T(2,128)S(1)}, u32[]{:S(2)}, u32[]{:S(2)}) collective-permute-start(f32[49,2,512]{2,1,0:T(2,128)} %get-tuple-element.13), channel_id=1, source_target_pairs={{1,0},{2,1},{3,2},{4,3},{5,4},{6,5},{7,6},{0,7},{9,8},{10,9},{11,1... | collective-permute-start | bytes 602120 | tf_op jit(solution)/shard_map/ppermute | solution.py:143
  4.1 21.1 %all-to-all-start = ((s32[32,1,128]{2,1,0:T(1,128)}), s32[32,1,128]{2,1,0:T(1,128)}, u32[]{:S(2)}, u32[]{:S(2)}) async-start(s32[32,1,128]{2,1,0:T(1,128)} %get-tuple-element.15), calls=%async_computation | async-start | bytes 32768 | tf_op jit(solution)/shard_map/all_to_all | solution.py:140
  15.6 0.8 copy-start.1
